TPU v7x, 32 devices: a whole 2x2x4 slice. The times are simulated.
32 devices in a mesh: sec: 8 (over z, core), patch: 4 (over y, x).
Axes of the slice: x: 2, y: 2, z: 4, core: 2. Of those that a mesh axis runs over, the one named last changes fastest.
Arguments:
- rhs: bfloat16 [24, 196608], P(None, ('sec', 'patch')), may hold values from -6 to 6
- curl_blocks: bfloat16 [2048, 4, 9216], P(('sec', 'patch')), may hold values from -0.3125 to 0.3125
- block_cols: int32 [2048, 4], P(('sec', 'patch')), may hold values from 0 to 63
- hole_mask: int32 [2048], P(('sec', 'patch')), may hold values 0 or 1
- edge_flip: int32 [196608], P(('sec', 'patch')), may hold values from 0 to 1
- send_list: int32 [8, 4, 4, 8], P('sec', 'patch'), may hold values from 0 to 63
- send_count: int32 [8, 4, 4], P('sec', 'patch'), may hold values from 5 to 8
- recv_list: int32 [8, 4, 4, 8], P('sec', 'patch'), may hold values from 0 to 63
- dtn_blocks: bfloat16 [8, 4, 4, 8, 9216], P('sec', 'patch'), may hold values from -0.4375 to 0.4375
Outputs:
- state: float32 [24, 196608], P(None, ('sec', 'patch'))
Inputs may be any that keep to these rules, and one draw needn't show every extreme that they name: Slots f >= send_count carry no block.
All inputs are finite; a program needn't handle non-finite values. No bound on the sum of `hole_mask` on one device may be relied on, other than what follows from the above.
Results may differ from a plain program's by a relative error of at most 0.029.
Values may be sent and summed in bfloat16 or wider, within the bound.
No kernel may reach another device: no remote copies, remote signals or barrier semaphores. Data moves between devices by JAX's collectives and lax.ppermute only.
A program may use at most 64 MiB of HBM per device.

v0:
```python
import jax
import jax.numpy as jnp
from jax import lax
from jax.sharding import PartitionSpec as P

BS = 96
COLS = 24
NB = 64
K = 4
F = 8
NI = 8
ITERS = 8
TICKS = 2


def shifted(x, axis, by):
    size = lax.axis_size(axis)
    pairs = [(i, i + by) for i in range(size) if 0 <= i + by < size]
    return lax.ppermute(x, axis, pairs)


def shards(
    rhs, curl_blocks, block_cols, hole_mask, edge_flip, send_list, send_count, recv_list, dtn_blocks
):
    coupling = 0.85
    peers = send_list.shape[2]
    matrices = curl_blocks.reshape(NB, K, BS, BS)
    keepers = hole_mask.astype(jnp.float32)[None, :, None]
    source = rhs.astype(jnp.float32).reshape(COLS, NB, BS)
    edge_sign = (1 - 2 * edge_flip).astype(jnp.bfloat16).reshape(NB, BS)
    send_slots = send_list[0, 0]
    counts = send_count[0, 0]
    targets = recv_list[0, 0]
    dtn_mats = dtn_blocks[0, 0].reshape(peers, F, BS, BS)
    filled = (jnp.arange(F)[None, :] < counts[:, None]).astype(jnp.bfloat16)
    flip_rows = edge_sign[send_slots] * filled[:, :, None]
    onehot = (targets[..., None] == jnp.arange(NB)[None, None, :]).astype(jnp.bfloat16)
    state = keepers * source
    from_left = jnp.zeros((COLS, NI, BS), jnp.float32)
    from_right = jnp.zeros((COLS, NI, BS), jnp.float32)
    for segment in range(TICKS):
        state_bf = state.astype(jnp.bfloat16)
        sent = state_bf.transpose(1, 0, 2)[send_slots] * flip_rows[:, :, None, :]
        received = lax.all_to_all(sent, "patch", split_axis=0, concat_axis=0, tiled=True)
        products = jnp.einsum(
            "qfed,qfcd->qfce", dtn_mats, received, preferred_element_type=jnp.float32
        )
        products = products.astype(jnp.bfloat16)
        face_terms = jnp.einsum(
            "qfn,qfce->cne", onehot, products, preferred_element_type=jnp.float32
        )
        forcing = source + face_terms
        forcing = forcing.at[:, :NI].add(from_left)
        forcing = forcing.at[:, NB - NI :].add(from_right)
        for sweep_idx in range(ITERS):
            state_bf = state.astype(jnp.bfloat16)
            nearby = state_bf[:, block_cols]
            image = jnp.einsum(
                "nked,cnkd->cne", matrices, nearby, preferred_element_type=jnp.float32
            )
            state = keepers * (forcing - coupling * image)
        if segment < TICKS - 1:
            to_right = state[:, NB - NI :].astype(jnp.bfloat16).reshape(COLS, NI * BS)
            to_left = state[:, :NI].astype(jnp.bfloat16).reshape(COLS, NI * BS)
            arrived_left = shifted(to_right, "sec", 1)
            arrived_right = shifted(to_left, "sec", -1)
            from_left = arrived_left.astype(jnp.float32).reshape(COLS, NI, BS)
            from_right = arrived_right.astype(jnp.float32).reshape(COLS, NI, BS)
    return state.reshape(COLS, NB * BS)


def solution(mesh):
    in_specs = (
        P(None, ("sec", "patch")),
        P(("sec", "patch"), None, None),
        P(("sec", "patch"), None),
        P(("sec", "patch")),
        P(("sec", "patch")),
        P("sec", "patch", None, None),
        P("sec", "patch", None),
        P("sec", "patch", None, None),
        P("sec", "patch", None, None, None),
    )
    out_specs = P(None, ("sec", "patch"))
    return jax.shard_map(shards, mesh=mesh, in_specs=in_specs, out_specs=out_specs, check_vma=False)
```

profile of v0, /device:TPU:1, one launch (start us, length us, event | category | flops | bytes accessed | tf_op | source)
XLA Modules:
  0.0 152.4 jit_solution(18386603379897111735)
XLA Ops:
  6.7 4.3 %all-to-all-start = ((bf16[4,8,24,96]{3,2,1,0:T(8,128)(2,1)}), bf16[4,8,24,96]{3,2,1,0:T(8,128)(2,1)}, u32[]{:S(2)}, u32[]{:S(2)}) async-start(bf16[4,8,24,96]{3,2,1,0:T(8,128)(2,1)} %broadcast_multiply_fusion.1), calls=%async_computation | async-start | bytes 393216 | tf_op jit(solution)/shard_map/all_to_all | solution.py:44
  11.7 10.7 %reshape.202 = bf16[64,4,96,96]{3,2,1,0:T(8,128)(2,1)} reshape(bf16[64,4,9216]{2,1,0:T(4,128)(2,1)} %param.18) | data formatting | bytes 9437184 | tf_op jit(solution)/shard_map/reshape | solution.py:27
  23.3 5.5 %convolution_bitcast_fusion.16 = f32[64,24,96]{2,1,0:T(8,128)} fusion(bf16[24,64,4,96]{3,0,2,1:T(8,128)(2,1)S(1)} %bitcast.260, bf16[64,4,96,96]{3,2,1,0:T(8,128)(2,1)} %reshape.202), kind=kOutput, calls=%fused_computation.35 | convolution fusion | flops 113246208 | bytes 6488064 | tf_op jit(solution)/shard_map/nked,cnkd->cne/dot_general | solution.py:58
  32.1 2.0 %gather_fusion.3 = bf16[256,24,96]{2,1,0:T(8,128)(2,1)} fusion(bf16[24,64,96]{2,0,1:T(8,128)(2,1)S(1)} %copy.46, s32[1024]{0:T(1024)S(1)} %pad_clamp_fusion), kind=kCustom, calls=%fused_computation.3 | custom fusion | bytes 2360320 | tf_op jit(solution)/shard_map/gather | solution.py:57
  34.2 5.0 %convolution_bitcast_fusion.15 = f32[64,24,96]{2,1,0:T(8,128)S(1)} fusion(bf16[24,64,4,96]{3,0,2,1:T(8,128)(2,1)} %bitcast.261, bf16[64,4,96,96]{3,2,1,0:T(8,128)(2,1)} %reshape.202), kind=kOutput, calls=%fused_computation.34 | convolution fusion | flops 113246208 | bytes 6488064 | tf_op jit(solution)/shard_map/nked,cnkd->cne/dot_general | solution.py:58
  39.7 2.0 %gather_fusion.4 = bf16[256,24,96]{2,1,0:T(8,128)(2,1)} fusion(bf16[24,64,96]{2,0,1:T(8,128)(2,1)S(1)} %copy.48, s32[1024]{0:T(1024)S(1)} %pad_clamp_fusion), kind=kCustom, calls=%fused_computation.4 | custom fusion | bytes 2360320 | tf_op jit(solution)/shard_map/gather | solution.py:57
  41.7 5.0 %convolution_bitcast_fusion.14 = f32[64,24,96]{2,1,0:T(8,128)S(1)} fusion(bf16[24,64,4,96]{3,0,2,1:T(8,128)(2,1)} %bitcast.262, bf16[64,4,96,96]{3,2,1,0:T(8,128)(2,1)} %reshape.202), kind=kOutput, calls=%fused_computation.33 | convolution fusion | flops 113246208 | bytes 6488064 | tf_op jit(solution)/shard_map/nked,cnkd->cne/dot_general | solution.py:58
  49.3 5.0 %convolution_bitcast_fusion.13 = f32[64,24,96]{2,1,0:T(8,128)S(1)} fusion(bf16[24,64,4,96]{3,0,2,1:T(8,128)(2,1)} %bitcast.263, bf16[64,4,96,96]{3,2,1,0:T(8,128)(2,1)} %reshape.202), kind=kOutput, calls=%fused_computation.32 | convolution fusion | flops 113246208 | bytes 6488064 | tf_op jit(solution)/shard_map/nked,cnkd->cne/dot_general | solution.py:58
  56.9 5.0 %convolution_bitcast_fusion.12 = f32[64,24,96]{2,1,0:T(8,128)S(1)} fusion(bf16[24,64,4,96]{3,0,2,1:T(8,128)(2,1)} %bitcast.264, bf16[64,4,96,96]{3,2,1,0:T(8,128)(2,1)} %reshape.202), kind=kOutput, calls=%fused_computation.31 | convolution fusion | flops 113246208 | bytes 6488064 | tf_op jit(solution)/shard_map/nked,cnkd->cne/dot_general | solution.py:58
  64.5 5.0 %convolution_bitcast_fusion.11 = f32[64,24,96]{2,1,0:T(8,128)S(1)} fusion(bf16[24,64,4,96]{3,0,2,1:T(8,128)(2,1)} %bitcast.265, bf16[64,4,96,96]{3,2,1,0:T(8,128)(2,1)} %reshape.202), kind=kOutput, calls=%fused_computation.30 | convolution fusion | flops 113246208 | bytes 6488064 | tf_op jit(solution)/shard_map/nked,cnkd->cne/dot_general | solution.py:58
  70.2 2.0 %gather_fusion.8 = bf16[256,24,96]{2,1,0:T(8,128)(2,1)} fusion(bf16[24,64,96]{2,0,1:T(8,128)(2,1)S(1)} %copy.56, s32[1024]{0:T(1024)S(1)} %pad_clamp_fusion), kind=kCustom, calls=%fused_computation.8 | custom fusion | bytes 2360320 | tf_op jit(solution)/shard_map/gather | solution.py:57
  72.2 5.0 %convolution_bitcast_fusion.10 = f32[64,24,96]{2,1,0:T(8,128)S(1)} fusion(bf16[24,64,4,96]{3,0,2,1:T(8,128)(2,1)} %bitcast.266, bf16[64,4,96,96]{3,2,1,0:T(8,128)(2,1)} %reshape.202), kind=kOutput, calls=%fused_computation.29 | convolution fusion | flops 113246208 | bytes 6488064 | tf_op jit(solution)/shard_map/nked,cnkd->cne/dot_general | solution.py:58
  77.8 2.0 %gather_fusion.9 = bf16[256,24,96]{2,1,0:T(8,128)(2,1)} fusion(bf16[24,64,96]{2,0,1:T(8,128)(2,1)S(1)} %copy.58, s32[1024]{0:T(1024)S(1)} %pad_clamp_fusion), kind=kCustom, calls=%fused_computation.9 | custom fusion | bytes 2360320 | tf_op jit(solution)/shard_map/gather | solution.py:57
  79.8 5.0 %convolution_bitcast_fusion.9 = f32[64,24,96]{2,1,0:T(8,128)S(1)} fusion(bf16[24,64,4,96]{3,0,2,1:T(8,128)(2,1)} %bitcast.267, bf16[64,4,96,96]{3,2,1,0:T(8,128)(2,1)} %reshape.202), kind=kOutput, calls=%fused_computation.28 | convolution fusion | flops 113246208 | bytes 6488064 | tf_op jit(solution)/shard_map/nked,cnkd->cne/dot_general | solution.py:58
  86.8 4.4 %collective-permute-start = (bf16[24,768]{1,0:T(8,128)(2,1)}, bf16[24,768]{1,0:T(8,128)(2,1)}, u32[]{:S(2)}, u32[]{:S(2)}) collective-permute-start(bf16[24,768]{1,0:T(8,128)(2,1)} %reshape.203), channel_id=1, source_target_pairs={{0,4},{4,8},{8,12},{12,16},{16,20},{20,24},{24,28},{1,5},{5,9},{9,... | collective-permute-start | bytes 110600 | tf_op jit(solution)/shard_map/ppermute | solution.py:19
  94.7 3.8 %all-to-all-start.1 = ((bf16[4,8,24,96]{3,2,1,0:T(8,128)(2,1)}), bf16[4,8,24,96]{3,2,1,0:T(8,128)(2,1)S(1)}, u32[]{:S(2)}, u32[]{:S(2)}) async-start(bf16[4,8,24,96]{3,2,1,0:T(8,128)(2,1)} %broadcast_multiply_fusion), calls=%async_computation.1 | async-start | bytes 393216 | tf_op jit(solution)/shard_map/all_to_all | solution.py:44
  100.6 5.0 %convolution_bitcast_fusion.7 = f32[64,24,96]{2,1,0:T(8,128)S(1)} fusion(bf16[24,64,4,96]{3,0,2,1:T(8,128)(2,1)} %bitcast.268, bf16[64,4,96,96]{3,2,1,0:T(8,128)(2,1)} %reshape.202), kind=kOutput, calls=%fused_computation.26 | convolution fusion | flops 113246208 | bytes 6488064 | tf_op jit(solution)/shard_map/nked,cnkd->cne/dot_general | solution.py:58
  109.9 4.5 %convolution_bitcast_fusion.6 = f32[64,24,96]{2,1,0:T(8,128)S(1)} fusion(bf16[24,64,4,96]{3,0,2,1:T(8,128)(2,1)S(1)} %bitcast.269, bf16[64,4,96,96]{3,2,1,0:T(8,128)(2,1)} %reshape.202), kind=kOutput, calls=%fused_computation.25 | convolution fusion | flops 113246208 | bytes 6488064 | tf_op jit(solution)/shard_map/nked,cnkd->cne/dot_general | solution.py:58
  115.9 4.5 %convolution_bitcast_fusion.5 = f32[64,24,96]{2,1,0:T(8,128)S(1)} fusion(bf16[24,64,4,96]{3,0,2,1:T(8,128)(2,1)S(1)} %bitcast.270, bf16[64,4,96,96]{3,2,1,0:T(8,128)(2,1)} %reshape.202), kind=kOutput, calls=%fused_computation.24 | convolution fusion | flops 113246208 | bytes 6488064 | tf_op jit(solution)/shard_map/nked,cnkd->cne/dot_general | solution.py:58
  122.0 4.5 %convolution_bitcast_fusion.4 = f32[64,24,96]{2,1,0:T(8,128)S(1)} fusion(bf16[24,64,4,96]{3,0,2,1:T(8,128)(2,1)S(1)} %bitcast.271, bf16[64,4,96,96]{3,2,1,0:T(8,128)(2,1)} %reshape.202), kind=kOutput, calls=%fused_computation.23 | convolution fusion | flops 113246208 | bytes 6488064 | tf_op jit(solution)/shard_map/nked,cnkd->cne/dot_general | solution.py:58
  128.0 4.5 %convolution_bitcast_fusion.3 = f32[64,24,96]{2,1,0:T(8,128)S(1)} fusion(bf16[24,64,4,96]{3,0,2,1:T(8,128)(2,1)S(1)} %bitcast.272, bf16[64,4,96,96]{3,2,1,0:T(8,128)(2,1)} %reshape.202), kind=kOutput, calls=%fused_computation.22 | convolution fusion | flops 113246208 | bytes 6488064 | tf_op jit(solution)/shard_map/nked,cnkd->cne/dot_general | solution.py:58
  134.1 4.5 %convolution_bitcast_fusion.2 = f32[64,24,96]{2,1,0:T(8,128)S(1)} fusion(bf16[24,64,4,96]{3,0,2,1:T(8,128)(2,1)S(1)} %bitcast.273, bf16[64,4,96,96]{3,2,1,0:T(8,128)(2,1)} %reshape.202), kind=kOutput, calls=%fused_computation.21 | convolution fusion | flops 113246208 | bytes 6488064 | tf_op jit(solution)/shard_map/nked,cnkd->cne/dot_general | solution.py:58
  140.4 4.5 %convolution_bitcast_fusion.1 = f32[64,24,96]{2,1,0:T(8,128)S(1)} fusion(bf16[24,64,4,96]{3,0,2,1:T(8,128)(2,1)S(1)} %bitcast.274, bf16[64,4,96,96]{3,2,1,0:T(8,128)(2,1)} %reshape.202), kind=kOutput, calls=%fused_computation.20 | convolution fusion | flops 113246208 | bytes 6488064 | tf_op jit(solution)/shard_map/nked,cnkd->cne/dot_general | solution.py:58
  146.4 4.5 %convolution_bitcast_fusion = f32[64,24,96]{2,1,0:T(8,128)S(1)} fusion(bf16[24,64,4,96]{3,0,2,1:T(8,128)(2,1)S(1)} %bitcast.259, bf16[64,4,96,96]{3,2,1,0:T(8,128)(2,1)} %reshape.202), kind=kOutput, calls=%fused_computation.19 | convolution fusion | flops 113246208 | bytes 6488064 | tf_op jit(solution)/shard_map/nked,cnkd->cne/dot_general | solution.py:58
  (100 shorter events, 43.8 us)
Async XLA Ops:
  2.2 3.2 %copy-start.2 = (s32[1024]{0:T(1024)}, s32[1024]{0:T(1024)S(1)}, u32[]{:S(2)}) copy-start(s32[1024]{0:T(1024)S(1)} %pad_clamp_fusion.1) | copy-start | bytes 12292
  4.5 6.7 %copy-start.6 = (s32[64,4]{0,1:T(4,128)S(1)}, s32[64,4]{0,1:T(4,128)}, u32[]{:S(2)}) copy-start(s32[64,4]{0,1:T(4,128)} %param.19) | copy-start | bytes 3076
  6.7 22.9 %all-to-all-start = ((bf16[4,8,24,96]{3,2,1,0:T(8,128)(2,1)}), bf16[4,8,24,96]{3,2,1,0:T(8,128)(2,1)}, u32[]{:S(2)}, u32[]{:S(2)}) async-start(bf16[4,8,24,96]{3,2,1,0:T(8,128)(2,1)} %broadcast_multiply_fusion.1), calls=%async_computation | async-start | bytes 393216 | tf_op jit(solution)/shard_map/all_to_all | solution.py:44
  23.3 5.5 %copy-start.1 = (bf16[1,1,4,8,9216]{4,3,2,1,0:T(8,128)(2,1)S(1)}, bf16[1,1,4,8,9216]{4,3,2,1,0:T(8,128)(2,1)}, u32[]{:S(2)}) copy-start(bf16[1,1,4,8,9216]{4,3,2,1,0:T(8,128)(2,1)} %param.25) | copy-start | bytes 1769476
  28.8 2.3 %copy-start.4 = (s32[1,1,4,8]{3,2,1,0:T(4,128)S(1)}, s32[1,1,4,8]{3,2,1,0:T(4,128)}, u32[]{:S(2)}) copy-start(s32[1,1,4,8]{3,2,1,0:T(4,128)} %param.24) | copy-start | bytes 388
  29.6 2.0 %copy-start = (f32[64,24,96]{2,1,0:T(8,128)S(1)}, f32[64,24,96]{2,1,0:T(8,128)}, u32[]{:S(2)}) copy-start(f32[64,24,96]{2,1,0:T(8,128)} %convolution_bitcast_fusion.16) | copy-start | bytes 1769476
  84.8 8.6 %copy-start.3 = (s32[1024]{0:T(1024)S(1)}, s32[1024]{0:T(1024)}, u32[]{:S(2)}) copy-start(s32[1024]{0:T(1024)} %copy-done.2) | copy-start | bytes 12292
  86.8 19.6 %collective-permute-start = (bf16[24,768]{1,0:T(8,128)(2,1)}, bf16[24,768]{1,0:T(8,128)(2,1)}, u32[]{:S(2)}, u32[]{:S(2)}) collective-permute-start(bf16[24,768]{1,0:T(8,128)(2,1)} %reshape.203), channel_id=1, source_target_pairs={{0,4},{4,8},{8,12},{12,16},{16,20},{20,24},{24,28},{1,5},{5,9},{9,... | collective-permute-start | bytes 110600 | tf_op jit(solution)/shard_map/ppermute | solution.py:19
  91.2 14.4 %collective-permute-start.1 = (bf16[24,768]{1,0:T(8,128)(2,1)}, bf16[24,768]{1,0:T(8,128)(2,1)}, u32[]{:S(2)}, u32[]{:S(2)}) collective-permute-start(bf16[24,768]{1,0:T(8,128)(2,1)} %reshape.205), channel_id=1, source_target_pairs={{4,0},{8,4},{12,8},{16,12},{20,16},{24,20},{28,24},{5,1},{9,5},{13... | collective-permute-start | bytes 110600 | tf_op jit(solution)/shard_map/ppermute | solution.py:19
  94.7 12.7 %all-to-all-start.1 = ((bf16[4,8,24,96]{3,2,1,0:T(8,128)(2,1)}), bf16[4,8,24,96]{3,2,1,0:T(8,128)(2,1)S(1)}, u32[]{:S(2)}, u32[]{:S(2)}) async-start(bf16[4,8,24,96]{3,2,1,0:T(8,128)(2,1)} %broadcast_multiply_fusion), calls=%async_computation.1 | async-start | bytes 393216 | tf_op jit(solution)/shard_map/all_to_all | solution.py:44
  100.6 7.3 %copy-start.5 = (s32[1,1,4,8]{3,2,1,0:T(4,128)S(1)}, s32[1,1,4,8]{3,2,1,0:T(4,128)}, u32[]{:S(2)}) copy-start(s32[1,1,4,8]{3,2,1,0:T(4,128)} %param.24) | copy-start | bytes 388
where the time goes:
time: 154 us; the launch traced here: 152 us
  matrix products  79.7 us (52%)
  local copies, waits for them, and re-layouts  48.6 us (32%)
  starting transfers between devices  14.4 us (9%)
  other arithmetic  9.18 us (6%)
    dot_general x16, matrix products, shards(): jnp.einsum('nked,cnkd->cne', matrices, nearby, preferred_element_type=jnp...  76.9 us
    gather x16, local copies, waits for them, and re-layouts, shards(): nearby = state_bf[:, block_cols]  24.3 us
    reshape x1, local copies, waits for them, and re-layouts, shards(): matrices = curl_blocks.reshape(NB, K, BS, BS)  10.7 us
    all_to_all x2, starting transfers between devices, shards(): lax.all_to_all(sent, 'patch', split_axis=0, concat_axis=0, tiled=True)  8.11 us
    ppermute x2, starting transfers between devices, shifted(): return lax.ppermute(x, axis, pairs)  6.27 us
    convert_element_type x16, local copies, waits for them, and re-layouts, shards(): state_bf = state.astype(jnp.bfloat16)  4.37 us
    convert_element_type x16, other arithmetic, shards(): state_bf = state.astype(jnp.bfloat16)  4.36 us
  transfers between devices with their start and end apart: 4, of which 0 were waited for; matrix products, arithmetic and copies ran while one was open for 19% of the time, Pallas kernels for 0%

commit v1 on v0

v1 whole, which is shorter than its diff:
```python
import functools

import jax
import jax.numpy as jnp
from jax import lax
from jax.experimental import pallas as pl
from jax.experimental.pallas import tpu as pltpu
from jax.sharding import PartitionSpec as P

BS = 96
COLS = 24
NB = 64
K = 4
F = 8
NI = 8
ITERS = 8
TICKS = 2
COUPLING = 0.85

LANES = 128
PAD = 128
QUAD = 4
TILES = 3
VMEM_LIMIT = 30 * 2**20
UNROLL = 32

VMEM = pl.BlockSpec(memory_space=pltpu.VMEM)
SMEM = pl.BlockSpec(memory_space=pltpu.SMEM)


def params():
    return pltpu.CompilerParams(vmem_limit_bytes=VMEM_LIMIT)


def cost(flops, size):
    return pl.CostEstimate(flops=flops, bytes_accessed=size, transcendentals=0)


def iota(shape, axis):
    return lax.broadcasted_iota(jnp.int32, shape, axis)


def split_quad(tiles):
    first, second, third = tiles
    lane = iota(first.shape, 1)
    parts = (
        first,
        jnp.where(lane < 64, second, first),
        jnp.where(lane < 64, third, second),
        third,
    )
    keep = lane < BS
    return [
        jnp.where(keep, pltpu.roll(part, 32 * j, 1) if j else part, 0.0)
        for j, part in enumerate(parts)
    ]


def join_quad(blocks):
    lane = iota(blocks[0].shape, 1)
    parts = [
        pltpu.roll(block, LANES - 32 * j, 1) if j else block for j, block in enumerate(blocks)
    ]
    return [
        jnp.where(lane < 96, parts[0], parts[1]),
        jnp.where(lane < 64, parts[1], parts[2]),
        jnp.where(lane < 32, parts[2], parts[3]),
    ]


def write_sent(peers, send_ref, count_ref, sign_ref, state_ref, sent_ref):
    for q in range(peers):
        for f in range(F):
            block = send_ref[q, f]
            scale = jnp.where(f < count_ref[q], 1.0, 0.0).astype(jnp.float32)
            sign = sign_ref[block % QUAD, pl.ds(block // QUAD, 1), :] * scale
            picked = state_ref[block].astype(jnp.float32) * sign
            sent_ref[q * F + f] = picked.astype(jnp.bfloat16)


def prep_kernel(
    peers, send_ref, count_ref, hole_ref, flip_ref, rhs_ref, source_ref, state_ref, sign_ref, sent_ref
):
    quads = NB // QUAD
    flips = [
        1.0 - 2.0 * flip_ref[pl.ds(u, quads, stride=TILES), :].astype(jnp.float32)
        for u in range(TILES)
    ]
    for j, sign in enumerate(split_quad(flips)):
        sign_ref[j] = sign
    for q in range(quads):
        at = q * TILES * LANES
        tiles = [
            rhs_ref[:, at + u * LANES : at + (u + 1) * LANES].astype(jnp.float32)
            for u in range(TILES)
        ]
        for j, block in enumerate(split_quad(tiles)):
            n = q * QUAD + j
            source_ref[n] = block
            keep = hole_ref[n].astype(jnp.float32)
            state_ref[n] = (keep * block).astype(jnp.bfloat16)
    write_sent(peers, send_ref, count_ref, sign_ref, state_ref, sent_ref)


def picker(group):
    depth = 8 * TILES * group
    row = iota((32 * group, 2 * depth), 0)
    at = iota((32 * group, 2 * depth), 1)
    member, e = row // 32, row % 32
    r, j = e // QUAD, e % QUAD
    low = jnp.where(j == 0, 0, jnp.where(j == 1, 1, 2))
    high = jnp.where(j < 2, 0, j - 1)
    want_low = (r * TILES + low) * group + member
    want_high = (r * TILES + high) * group + member + depth
    return ((at == want_low) | (at == want_high)).astype(jnp.float32).astype(jnp.bfloat16)


def spread(select, rows, group):
    depth = 8 * TILES * group
    parts = [rows[g * depth : (g + 1) * depth] for g in range(3)]
    wide = jnp.concatenate(parts, axis=1)
    high = iota(wide.shape, 1) % LANES >= 64
    zero = jnp.zeros_like(wide)
    stacked = jnp.concatenate([jnp.where(high, zero, wide), jnp.where(high, wide, zero)], axis=0)
    picked = jnp.dot(select, stacked, preferred_element_type=jnp.float32).astype(jnp.bfloat16)
    pad = jnp.zeros((PAD - BS, LANES), jnp.bfloat16)
    phase = iota((32, LANES), 1) % QUAD
    results = []
    for member in range(group):
        mine = picked[32 * member : 32 * (member + 1)]
        square = jnp.concatenate(
            [mine[:, g * LANES : (g + 1) * LANES] for g in range(3)] + [pad], axis=0
        )
        turned = square.T
        bands = [turned[32 * a : 32 * (a + 1)] for a in range(4)]
        fixed = []
        for a in range(4):
            band = bands[a]
            for j in range(1, QUAD):
                band = jnp.where(phase == j, bands[(a - j) % 4], band)
            fixed.append(band)
        results.append(jnp.concatenate(fixed, axis=0))
    return results


def spread_kernel(peers, curl_ref, dtn_ref, matrix_ref, face_ref):
    select = picker(K)

    def curl_step(n, carry):
        for k, block in enumerate(spread(select, curl_ref[n], K)):
            matrix_ref[n, k * PAD : (k + 1) * PAD] = block
        return carry

    lax.fori_loop(0, NB, curl_step, 0, unroll=2)
    select_faces = picker(F)

    def face_step(q, carry):
        for f, block in enumerate(spread(select_faces, dtn_ref[q], F)):
            face_ref[q * F + f] = block
        return carry

    lax.fori_loop(0, peers, face_step, 0)


def add_faces(peers, target_ref, hole_ref, received_ref, face_ref, forcing_ref):
    products = []
    for i in range(peers * F):
        product = jnp.dot(received_ref[i], face_ref[i], preferred_element_type=jnp.float32)
        products.append(product.astype(jnp.bfloat16).astype(jnp.float32))
    for i, product in enumerate(products):
        n = target_ref[i // F, i % F]
        forcing_ref[n] = forcing_ref[n] + product
    for n in range(NB):
        forcing_ref[n] = forcing_ref[n] * hole_ref[n].astype(jnp.float32)


def sweep(cols_ref, hole_ref, matrix_ref, forcing_ref, old_ref, new_ref):
    def body(i, carry):
        images = []
        for step in range(UNROLL):
            n = i * UNROLL + step
            nearby = jnp.concatenate([old_ref[cols_ref[k, n]] for k in range(K)], axis=1)
            images.append(jnp.dot(nearby, matrix_ref[n], preferred_element_type=jnp.float32))
        for step in range(UNROLL):
            n = i * UNROLL + step
            scale = COUPLING * hole_ref[n].astype(jnp.float32)
            new_ref[n] = (forcing_ref[n] - scale * images[step]).astype(new_ref.dtype)
        return carry

    lax.fori_loop(0, NB // UNROLL, body, 0)


def first_tick_kernel(
    peers, cols_ref, hole_ref, target_ref, send_ref, count_ref, sign_ref, matrix_ref, face_ref,
    received_ref, source_ref, start_ref, state_ref, sent_ref, left_ref, right_ref, forcing_ref,
    other_ref,
):
    forcing_ref[...] = source_ref[...]
    add_faces(peers, target_ref, hole_ref, received_ref, face_ref, forcing_ref)
    state_ref[...] = start_ref[...]

    def two(i, carry):
        sweep(cols_ref, hole_ref, matrix_ref, forcing_ref, state_ref, other_ref)
        sweep(cols_ref, hole_ref, matrix_ref, forcing_ref, other_ref, state_ref)
        return carry

    lax.fori_loop(0, ITERS // 2, two, 0)
    left_ref[...] = state_ref[:NI]
    right_ref[...] = state_ref[NB - NI :]
    write_sent(peers, send_ref, count_ref, sign_ref, state_ref, sent_ref)


def last_tick_kernel(
    peers, cols_ref, hole_ref, target_ref, matrix_ref, face_ref, received_ref, source_ref, start_ref,
    from_left_ref, from_right_ref, out_ref, forcing_ref, state_ref, other_ref, final_ref,
):
    forcing_ref[...] = source_ref[...]
    forcing_ref[:NI] = forcing_ref[:NI] + from_left_ref[...].astype(jnp.float32)
    forcing_ref[NB - NI :] = forcing_ref[NB - NI :] + from_right_ref[...].astype(jnp.float32)
    add_faces(peers, target_ref, hole_ref, received_ref, face_ref, forcing_ref)
    state_ref[...] = start_ref[...]

    def two(i, carry):
        sweep(cols_ref, hole_ref, matrix_ref, forcing_ref, state_ref, other_ref)
        sweep(cols_ref, hole_ref, matrix_ref, forcing_ref, other_ref, state_ref)
        return carry

    lax.fori_loop(0, ITERS // 2 - 1, two, 0)
    sweep(cols_ref, hole_ref, matrix_ref, forcing_ref, state_ref, other_ref)
    sweep(cols_ref, hole_ref, matrix_ref, forcing_ref, other_ref, final_ref)
    for q in range(NB // QUAD):
        tiles = join_quad([final_ref[q * QUAD + j] for j in range(QUAD)])
        for u, tile in enumerate(tiles):
            at = (q * TILES + u) * LANES
            out_ref[:, at : at + LANES] = tile


def shifted(x, axis, by):
    size = lax.axis_size(axis)
    pairs = [(i, i + by) for i in range(size) if 0 <= i + by < size]
    return lax.ppermute(x, axis, pairs)


def shape(dims, dtype):
    return jax.ShapeDtypeStruct(dims, dtype)


def shards(
    rhs, curl_blocks, block_cols, hole_mask, edge_flip, send_list, send_count, recv_list, dtn_blocks
):
    peers = send_list.shape[2]
    f32, bf16 = jnp.float32, jnp.bfloat16
    tiles = BS * BS // LANES
    cols = block_cols.T
    sends, counts, targets = send_list[0, 0], send_count[0, 0], recv_list[0, 0]
    flips = edge_flip.reshape(NB * BS // LANES, LANES)
    curl_rows = curl_blocks.reshape(NB, K, tiles, LANES).transpose(0, 2, 1, 3)
    curl_rows = curl_rows.reshape(NB, tiles * K, LANES)
    dtn_rows = dtn_blocks[0, 0].reshape(peers, F, tiles, LANES).transpose(0, 2, 1, 3)
    dtn_rows = dtn_rows.reshape(peers, tiles * F, LANES)

    block_shape = (NB, COLS, PAD)
    face_shape = (peers * F, COLS, PAD)
    source, start, sign, sent = pl.pallas_call(
        functools.partial(prep_kernel, peers),
        out_shape=(
            shape(block_shape, f32),
            shape(block_shape, bf16),
            shape((QUAD, NB // QUAD, LANES), f32),
            shape(face_shape, bf16),
        ),
        in_specs=[SMEM] * 3 + [VMEM] * 2,
        out_specs=[VMEM] * 4,
        compiler_params=params(),
        cost_estimate=cost(10**6, 10**6),
    )(sends, counts, hole_mask, flips, rhs)

    matrices, faces = pl.pallas_call(
        functools.partial(spread_kernel, peers),
        out_shape=(shape((NB, K * PAD, PAD), bf16), shape((peers * F, PAD, PAD), bf16)),
        in_specs=[VMEM] * 2,
        out_specs=[VMEM] * 2,
        compiler_params=params(),
        cost_estimate=cost(4 * 10**9, 16 * 10**6),
    )(curl_rows, dtn_rows)

    def exchange(sent):
        sent = sent.reshape((peers, F, COLS, PAD))
        received = lax.all_to_all(sent, "patch", split_axis=0, concat_axis=0, tiled=True)
        return received.reshape(face_shape)

    received = exchange(sent)
    state, sent, to_left, to_right = pl.pallas_call(
        functools.partial(first_tick_kernel, peers),
        out_shape=(
            shape(block_shape, bf16),
            shape(face_shape, bf16),
            shape((NI, COLS, PAD), bf16),
            shape((NI, COLS, PAD), bf16),
        ),
        in_specs=[SMEM] * 5 + [VMEM] * 6,
        out_specs=[VMEM] * 4,
        scratch_shapes=[pltpu.VMEM(block_shape, f32), pltpu.VMEM(block_shape, bf16)],
        compiler_params=params(),
        cost_estimate=cost(10**10, 16 * 10**6),
    )(cols, hole_mask, targets, sends, counts, sign, matrices, faces, received, source, start)

    received = exchange(sent)
    from_left = shifted(to_right, "sec", 1)
    from_right = shifted(to_left, "sec", -1)
    return pl.pallas_call(
        functools.partial(last_tick_kernel, peers),
        out_shape=shape((COLS, NB * BS), f32),
        in_specs=[SMEM] * 3 + [VMEM] * 7,
        out_specs=VMEM,
        scratch_shapes=[
            pltpu.VMEM(block_shape, f32),
            pltpu.VMEM(block_shape, bf16),
            pltpu.VMEM(block_shape, bf16),
            pltpu.VMEM(block_shape, f32),
        ],
        compiler_params=params(),
        cost_estimate=cost(10**10, 16 * 10**6),
    )(cols, hole_mask, targets, matrices, faces, received, source, state, from_left, from_right)


def solution(mesh):
    in_specs = (
        P(None, ("sec", "patch")),
        P(("sec", "patch"), None, None),
        P(("sec", "patch"), None),
        P(("sec", "patch")),
        P(("sec", "patch")),
        P("sec", "patch", None, None),
        P("sec", "patch", None),
        P("sec", "patch", None, None),
        P("sec", "patch", None, None, None),
    )
    out_specs = P(None, ("sec", "patch"))
    return jax.shard_map(shards, mesh=mesh, in_specs=in_specs, out_specs=out_specs, check_vma=False)
```

time: 154 us -> 77 us (0.50)
  matrix products: 79.7 us -> 0 us
  Pallas kernels: 0 us -> 41.2 us
  local copies, waits for them, and re-layouts: 48.6 us -> 17.1 us
  other arithmetic: 9.18 us -> 0 us
  waiting for transfers between devices: 0.01 us -> 3.48 us
    dot_general x20 -> x0, matrix products: 79.7 us -> none  [the longest x16 76.9 us: shards(): jnp.einsum('nked,cnkd->cne', matrices, nearby, preferred_element_type=jnp...]
    pallas_call x0 -> x4, Pallas kernels: none -> 41.2 us  [the longest x1 14.1 us: shards(): pl.pallas_call(functools.partial(last_tick_kernel, peers), out_shape=shap...]
    gather x19 -> x0, local copies, waits for them, and re-layouts: 26.1 us -> none  [the longest x16 24.3 us: shards(): nearby = state_bf[:, block_cols]]
    unnamed x14 -> x30, local copies, waits for them, and re-layouts: 0.03 us -> 17.1 us
    reshape x6 -> x0, local copies, waits for them, and re-layouts: 14.7 us -> none  [the longest x1 10.7 us: shards(): matrices = curl_blocks.reshape(NB, K, BS, BS)]
    convert_element_type x19 -> x0, other arithmetic: 6.49 us -> none  [the longest x16 4.36 us: shards(): state_bf = state.astype(jnp.bfloat16)]
    convert_element_type x16 -> x0, local copies, waits for them, and re-layouts: 4.37 us -> none  [shards(): state_bf = state.astype(jnp.bfloat16)]
    ppermute x2, waiting for transfers between devices: 0.01 us -> 3.47 us  [shifted(): return lax.ppermute(x, axis, pairs)]
  transfers between devices with their start and end apart: 4 -> 4, of which waited for: 0 -> 1; matrix products, arithmetic and copies ran while one was open for 19% -> 0% of each run, Pallas kernels for 0% -> 15%
where the time goes in v1:
time: 77 us; the launch traced here: 76.4 us
  Pallas kernels  41.2 us (54%)
  local copies, waits for them, and re-layouts  17.1 us (22%)
  starting transfers between devices  14.5 us (19%)
  waiting for transfers between devices  3.48 us (5%)
    unnamed x30, local copies, waits for them, and re-layouts  17.1 us
    pallas_call x1, Pallas kernels, shards(): pl.pallas_call(functools.partial(last_tick_kernel, peers), out_shape=shap...  14.1 us
    pallas_call x1, Pallas kernels, shards(): pl.pallas_call(functools.partial(first_tick_kernel, peers), out_shape=(sh...  14 us
    pallas_call x1, Pallas kernels, shards(): pl.pallas_call(functools.partial(spread_kernel, peers), out_shape=(shape(...  11.5 us
    all_to_all x2, starting transfers between devices, exchange(): lax.all_to_all(sent, 'patch', split_axis=0, concat_axis=0, tiled=True)  7.9 us
    ppermute x2, starting transfers between devices, shifted(): return lax.ppermute(x, axis, pairs)  6.56 us
    ppermute x2, waiting for transfers between devices, shifted(): return lax.ppermute(x, axis, pairs)  3.47 us
    pallas_call x1, Pallas kernels, shards(): pl.pallas_call(functools.partial(prep_kernel, peers), out_shape=(shape(bl...  1.58 us
  transfers between devices with their start and end apart: 4, of which 1 were waited for; matrix products, arithmetic and copies ran while one was open for 0% of the time, Pallas kernels for 15%

profile of v1, /device:TPU:1, one launch (start us, length us, event | category | flops | bytes accessed | tf_op | source)
XLA Modules:
  0.0 76.4 jit_solution(13076374580470873015)
XLA Ops:
  0.0 1.0 %copy-done = bf16[24,6144]{1,0:T(8,128)(2,1)S(1)} copy-done((bf16[24,6144]{1,0:T(8,128)(2,1)S(1)}, bf16[24,6144]{1,0:T(8,128)(2,1)}, u32[]{:S(2)}) %copy-start) | copy-done | bytes 294936
  1.0 0.7 copy-done.1
  1.8 0.7 copy-done.2
  2.4 0.7 copy-done.4
  3.1 0.7 copy-done.6
  3.8 1.6 %shard_map.92 = (f32[64,24,128]{2,1,0:T(8,128)S(1)}, bf16[64,24,128]{2,1,0:T(8,128)(2,1)S(1)}, f32[4,16,128]{2,1,0:T(8,128)S(1)}, bf16[32,24,128]{2,1,0:T(8,128)(2,1)}) custom-call(s32[4,8]{1,0:T(4,128)S(1)} %bitcast.22, s32[4]{0:T(128)S(1)} %bitcast.24, s32[64]{0:T(128)S(1)} %copy-done.6, s32[48,128]{1,0:T(8,128)S(1)} %bitcast.21, bf16[24,6144]{1,0:T(8,128)(2,1)S(1)} %copy-done), custom_call_target="tpu_custom_call" | custom-call | flops 1000000 | bytes 1000000 | tf_op jit(solution)/shard_map/pallas_call | solution.py:264
  5.3 4.3 %all-to-all-start = ((bf16[4,8,24,128]{3,2,1,0:T(8,128)(2,1)}), bf16[4,8,24,128]{3,2,1,0:T(8,128)(2,1)S(1)}, u32[]{:S(2)}, u32[]{:S(2)}) async-start(bf16[4,8,24,128]{3,2,1,0:T(8,128)(2,1)} %bitcast.11), calls=%async_computation | async-start | bytes 393216 | tf_op jit(solution)/shard_map/all_to_all | solution.py:289
  9.6 2.3 %copy-done.8 = bf16[64,4,9216]{2,1,0:T(4,128)(2,1)S(1)} copy-done((bf16[64,4,9216]{2,1,0:T(4,128)(2,1)S(1)}, bf16[64,4,9216]{2,1,0:T(4,128)(2,1)}, u32[]{:S(2)}) %copy-start.8) | copy-done | bytes 4718616
  11.9 1.1 %copy-done.9 = bf16[1,1,4,8,9216]{4,3,2,1,0:T(8,128)(2,1)S(1)} copy-done((bf16[1,1,4,8,9216]{4,3,2,1,0:T(8,128)(2,1)S(1)}, bf16[1,1,4,8,9216]{4,3,2,1,0:T(8,128)(2,1)}, u32[]{:S(2)}) %copy-start.9) | copy-done | bytes 589848
  13.0 11.5 %shard_map.91 = (bf16[64,512,128]{2,1,0:T(8,128)(2,1)S(1)}, bf16[32,128,128]{2,1,0:T(8,128)(2,1)S(1)}) custom-call(bf16[64,288,128]{2,1,0:T(8,128)(2,1)S(1)} %bitcast.26, bf16[4,576,128]{2,1,0:T(8,128)(2,1)S(1)} %bitcast.27), custom_call_target="tpu_custom_call" | custom-call | flops 4000000000 | bytes 16000000 | tf_op jit(solution)/shard_map/pallas_call | solution.py:278
  24.5 0.0 copy-start.12
  24.5 3.2 %copy-done.12 = bf16[64,512,128]{2,1,0:T(8,128)(2,1)} copy-done((bf16[64,512,128]{2,1,0:T(8,128)(2,1)}, bf16[64,512,128]{2,1,0:T(8,128)(2,1)S(1)}, u32[]{:S(2)}) %copy-start.12) | copy-done | bytes 8388632
  27.8 0.0 all-to-all-done
  27.8 0.0 copy-done.5
  27.8 3.4 %copy-done.13 = bf16[64,512,128]{2,1,0:T(8,128)(2,1)S(1)} copy-done((bf16[64,512,128]{2,1,0:T(8,128)(2,1)S(1)}, bf16[64,512,128]{2,1,0:T(8,128)(2,1)}, u32[]{:S(2)}) %copy-start.13) | copy-done | bytes 8388632
  31.2 14.0 %shard_map.93 = (bf16[64,24,128]{2,1,0:T(8,128)(2,1)S(1)}, bf16[32,24,128]{2,1,0:T(8,128)(2,1)}, bf16[8,24,128]{2,1,0:T(8,128)(2,1)S(1)}, bf16[8,24,128]{2,1,0:T(8,128)(2,1)S(1)}) custom-call(s32[4,64]{1,0:T(4,128)S(1)} %bitcast.28, s32[64]{0:T(128)S(1)} %copy-done.7, s32[4,8]{1,0:T(4,128)S(1)} %bitcast.30, s32[4,8]{1,0:T(4,128)S(1)} %bitcast.23, ...), custom_call_target="tpu_custom_call" | custom-call | flops 10000000000 | bytes 16000000 | tf_op jit(solution)/shard_map/pallas_call | solution.py:293
  45.2 3.6 %all-to-all-start.1 = ((bf16[4,8,24,128]{3,2,1,0:T(8,128)(2,1)}), bf16[4,8,24,128]{3,2,1,0:T(8,128)(2,1)S(1)}, u32[]{:S(2)}, u32[]{:S(2)}) async-start(bf16[4,8,24,128]{3,2,1,0:T(8,128)(2,1)} %bitcast.13), calls=%async_computation.1 | async-start | bytes 393216 | tf_op jit(solution)/shard_map/all_to_all | solution.py:289
  48.9 4.6 %collective-permute-start = (bf16[8,24,128]{2,1,0:T(8,128)(2,1)S(1)}, bf16[8,24,128]{2,1,0:T(8,128)(2,1)S(1)}, u32[]{:S(2)}, u32[]{:S(2)}) collective-permute-start(bf16[8,24,128]{2,1,0:T(8,128)(2,1)S(1)} %get-tuple-element.23), channel_id=1, source_target_pairs={{0,4},{4,8},{8,12},{12,16},{16,20},{20,24},{24,28},{1,5},{5,9},{9,... | collective-permute-start | bytes 147464 | tf_op jit(solution)/shard_map/ppermute | solution.py:241
  53.5 1.9 %collective-permute-start.1 = (bf16[8,24,128]{2,1,0:T(8,128)(2,1)S(1)}, bf16[8,24,128]{2,1,0:T(8,128)(2,1)S(1)}, u32[]{:S(2)}, u32[]{:S(2)}) collective-permute-start(bf16[8,24,128]{2,1,0:T(8,128)(2,1)S(1)} %get-tuple-element.24), channel_id=1, source_target_pairs={{4,0},{8,4},{12,8},{16,12},{20,16},{24,20},{28,24},{5,1},{9,5},{13... | collective-permute-start | bytes 147464 | tf_op jit(solution)/shard_map/ppermute | solution.py:241
  55.4 0.0 collective-permute-done.from_left_ref
  55.5 3.5 %collective-permute-done.1.from_right_ref = bf16[8,24,128]{2,1,0:T(8,128)(2,1)S(1)} collective-permute-done((bf16[8,24,128]{2,1,0:T(8,128)(2,1)S(1)}, bf16[8,24,128]{2,1,0:T(8,128)(2,1)S(1)}, u32[]{:S(2)}, u32[]{:S(2)}) %collective-permute-start.1) | collective-permute-done | bytes 49184 | tf_op jit(solution)/shard_map/ppermute | solution.py:241
  58.9 0.0 all-to-all-done.1
  58.9 3.4 %copy-done.14 = bf16[64,512,128]{2,1,0:T(8,128)(2,1)S(1)} copy-done((bf16[64,512,128]{2,1,0:T(8,128)(2,1)S(1)}, bf16[64,512,128]{2,1,0:T(8,128)(2,1)}, u32[]{:S(2)}) %copy-start.14) | copy-done | bytes 8388632
  62.3 14.1 %shard_map.94 = f32[24,6144]{1,0:T(8,128)} custom-call(s32[4,64]{1,0:T(4,128)S(1)} %bitcast.29, s32[64]{0:T(128)S(1)} %copy-done.7, s32[4,8]{1,0:T(4,128)S(1)} %bitcast.31, bf16[64,512,128]{2,1,0:T(8,128)(2,1)S(1)} %copy-done.14, bf16[32,128,128]{2,1,0:T(8,128)(2,1)S(1)} %get-tuple-element.16.face_ref, bf16[32,24,128]{2,1,0:T(8,128)(2,1)S(1)} %bitcast.19, ...), custom_call_target="tpu_custom_call" | custom-call | flops 10000000000 | bytes 16000000 | tf_op jit(solution)/shard_map/pallas_call | solution.py:311
  (18 shorter events, 0.0 us)
Async XLA Ops:
  0.0 27.8 %copy-start.7 = (s32[64]{0:T(128)S(1)}, s32[64]{0:T(128)}, u32[]{:S(2)}) copy-start(s32[64]{0:T(128)} %hole_ref.5) | copy-start | bytes 772
  0.0 27.8 %copy-start.5 = (s32[1,1,4]{2,1,0:T(1,128)S(1)}, s32[1,1,4]{2,1,0:T(1,128)}, u32[]{:S(2)}) copy-start(s32[1,1,4]{2,1,0:T(1,128)} %param.15) | copy-start | bytes 52
  0.0 27.8 %copy-start.3 = (s32[1,1,4,8]{3,2,1,0:T(4,128)S(1)}, s32[1,1,4,8]{3,2,1,0:T(4,128)}, u32[]{:S(2)}) copy-start(s32[1,1,4,8]{3,2,1,0:T(4,128)} %param.14) | copy-start | bytes 388
  0.0 27.8 %copy-start.10 = (s32[64,4]{0,1:T(4,128)S(1)}, s32[64,4]{0,1:T(4,128)}, u32[]{:S(2)}) copy-start(s32[64,4]{0,1:T(4,128)} %param.11) | copy-start | bytes 3076
  0.0 1.0 %copy-start = (bf16[24,6144]{1,0:T(8,128)(2,1)S(1)}, bf16[24,6144]{1,0:T(8,128)(2,1)}, u32[]{:S(2)}) copy-start(bf16[24,6144]{1,0:T(8,128)(2,1)} %rhs_ref.1) | copy-start | bytes 884740
  1.0 0.7 copy-start.1
  1.8 0.7 copy-start.2
  2.4 0.7 copy-start.4
  3.1 0.7 copy-start.6
  3.8 24.0 %copy-start.11 = (s32[1,1,4,8]{3,2,1,0:T(4,128)S(1)}, s32[1,1,4,8]{3,2,1,0:T(4,128)}, u32[]{:S(2)}) copy-start(s32[1,1,4,8]{3,2,1,0:T(4,128)} %param.16) | copy-start | bytes 388
  5.3 22.4 %all-to-all-start = ((bf16[4,8,24,128]{3,2,1,0:T(8,128)(2,1)}), bf16[4,8,24,128]{3,2,1,0:T(8,128)(2,1)S(1)}, u32[]{:S(2)}, u32[]{:S(2)}) async-start(bf16[4,8,24,128]{3,2,1,0:T(8,128)(2,1)} %bitcast.11), calls=%async_computation | async-start | bytes 393216 | tf_op jit(solution)/shard_map/all_to_all | solution.py:289
  9.6 2.3 %copy-start.8 = (bf16[64,4,9216]{2,1,0:T(4,128)(2,1)S(1)}, bf16[64,4,9216]{2,1,0:T(4,128)(2,1)}, u32[]{:S(2)}) copy-start(bf16[64,4,9216]{2,1,0:T(4,128)(2,1)} %param.10) | copy-start | bytes 14155780
  11.9 1.1 %copy-start.9 = (bf16[1,1,4,8,9216]{4,3,2,1,0:T(8,128)(2,1)S(1)}, bf16[1,1,4,8,9216]{4,3,2,1,0:T(8,128)(2,1)}, u32[]{:S(2)}) copy-start(bf16[1,1,4,8,9216]{4,3,2,1,0:T(8,128)(2,1)} %param.17) | copy-start | bytes 1769476
  24.5 3.3 %copy-start.12 = (bf16[64,512,128]{2,1,0:T(8,128)(2,1)}, bf16[64,512,128]{2,1,0:T(8,128)(2,1)S(1)}, u32[]{:S(2)}) copy-start(bf16[64,512,128]{2,1,0:T(8,128)(2,1)S(1)} %get-tuple-element.15.matrix_ref) | copy-start | bytes 25165828
  27.8 3.4 %copy-start.13 = (bf16[64,512,128]{2,1,0:T(8,128)(2,1)S(1)}, bf16[64,512,128]{2,1,0:T(8,128)(2,1)}, u32[]{:S(2)}) copy-start(bf16[64,512,128]{2,1,0:T(8,128)(2,1)} %copy-done.12) | copy-start | bytes 25165828
  45.2 13.7 %all-to-all-start.1 = ((bf16[4,8,24,128]{3,2,1,0:T(8,128)(2,1)}), bf16[4,8,24,128]{3,2,1,0:T(8,128)(2,1)S(1)}, u32[]{:S(2)}, u32[]{:S(2)}) async-start(bf16[4,8,24,128]{3,2,1,0:T(8,128)(2,1)} %bitcast.13), calls=%async_computation.1 | async-start | bytes 393216 | tf_op jit(solution)/shard_map/all_to_all | solution.py:289
  48.9 6.6 %collective-permute-start = (bf16[8,24,128]{2,1,0:T(8,128)(2,1)S(1)}, bf16[8,24,128]{2,1,0:T(8,128)(2,1)S(1)}, u32[]{:S(2)}, u32[]{:S(2)}) collective-permute-start(bf16[8,24,128]{2,1,0:T(8,128)(2,1)S(1)} %get-tuple-element.23), channel_id=1, source_target_pairs={{0,4},{4,8},{8,12},{12,16},{16,20},{20,24},{24,28},{1,5},{5,9},{9,... | collective-permute-start | bytes 147464 | tf_op jit(solution)/shard_map/ppermute | solution.py:241
  53.5 5.4 %collective-permute-start.1 = (bf16[8,24,128]{2,1,0:T(8,128)(2,1)S(1)}, bf16[8,24,128]{2,1,0:T(8,128)(2,1)S(1)}, u32[]{:S(2)}, u32[]{:S(2)}) collective-permute-start(bf16[8,24,128]{2,1,0:T(8,128)(2,1)S(1)} %get-tuple-element.24), channel_id=1, source_target_pairs={{4,0},{8,4},{12,8},{16,12},{20,16},{24,20},{28,24},{5,1},{9,5},{13... | collective-permute-start | bytes 147464 | tf_op jit(solution)/shard_map/ppermute | solution.py:241
  58.9 3.4 %copy-start.14 = (bf16[64,512,128]{2,1,0:T(8,128)(2,1)S(1)}, bf16[64,512,128]{2,1,0:T(8,128)(2,1)}, u32[]{:S(2)}) copy-start(bf16[64,512,128]{2,1,0:T(8,128)(2,1)} %copy-done.12) | copy-start | bytes 25165828

commit v2 on v1

v2 whole, which is shorter than its diff:
```python
import functools

import jax
import jax.numpy as jnp
from jax import lax
from jax.experimental import pallas as pl
from jax.experimental.pallas import tpu as pltpu
from jax.sharding import PartitionSpec as P

BS = 96
COLS = 24
NB = 64
K = 4
F = 8
NI = 8
ITERS = 8
TICKS = 2
COUPLING = 0.85

LANES = 128
PAD = 128
QUAD = 4
TILES = 3
VMEM_LIMIT = 30 * 2**20
GROUP = 8

VMEM = pl.BlockSpec(memory_space=pltpu.VMEM)
SMEM = pl.BlockSpec(memory_space=pltpu.SMEM)
HBM = pl.BlockSpec(memory_space=pltpu.HBM)


def params():
    return pltpu.CompilerParams(vmem_limit_bytes=VMEM_LIMIT)


def cost(flops, size):
    return pl.CostEstimate(flops=flops, bytes_accessed=size, transcendentals=0)


def iota(shape, axis):
    return lax.broadcasted_iota(jnp.int32, shape, axis)


def split_quad(tiles):
    first, second, third = tiles
    lane = iota(first.shape, 1)
    parts = (
        first,
        jnp.where(lane < 64, second, first),
        jnp.where(lane < 64, third, second),
        third,
    )
    keep = lane < BS
    return [
        jnp.where(keep, pltpu.roll(part, 32 * j, 1) if j else part, 0.0)
        for j, part in enumerate(parts)
    ]


def join_quad(blocks):
    lane = iota(blocks[0].shape, 1)
    parts = [
        pltpu.roll(block, LANES - 32 * j, 1) if j else block for j, block in enumerate(blocks)
    ]
    return [
        jnp.where(lane < 96, parts[0], parts[1]),
        jnp.where(lane < 64, parts[1], parts[2]),
        jnp.where(lane < 32, parts[2], parts[3]),
    ]


def write_sent(peers, send_ref, count_ref, sign_ref, state_ref, sent_refs):
    me = lax.axis_index("patch")
    for i in range(peers):
        q = lax.rem(me + i, peers)
        for f in range(F):
            block = send_ref[q, f]
            scale = jnp.where(f < count_ref[q], 1.0, 0.0).astype(jnp.float32)
            sign = sign_ref[lax.rem(block, QUAD), pl.ds(lax.div(block, QUAD), 1), :] * scale
            picked = state_ref[block].astype(jnp.float32) * sign
            sent_refs[i][f] = picked.astype(jnp.bfloat16)


def copies(sources, targets, sems):
    started = [
        pltpu.make_async_copy(source, target, sems.at[i])
        for i, (source, target) in enumerate(zip(sources, targets))
    ]
    for one in started:
        one.start()
    return started


def prep_kernel(peers, *refs):
    sources = refs[:5]
    state_ref, sign_ref = refs[5:7]
    sent_refs = refs[7 : 7 + peers]
    held, sems = refs[7 + peers : -1], refs[-1]
    send_ref, count_ref, hole_ref, flip_ref, rhs_ref = held
    for one in copies(sources, held, sems):
        one.wait()
    quads = NB // QUAD
    flips = [
        1.0 - 2.0 * flip_ref[pl.ds(u, quads, stride=TILES), :].astype(jnp.float32)
        for u in range(TILES)
    ]
    for j, sign in enumerate(split_quad(flips)):
        sign_ref[j] = sign
    for q in range(quads):
        at = q * TILES * LANES
        tiles = [
            rhs_ref[:, at + u * LANES : at + (u + 1) * LANES].astype(jnp.float32)
            for u in range(TILES)
        ]
        for j, block in enumerate(split_quad(tiles)):
            n = q * QUAD + j
            keep = hole_ref[n].astype(jnp.float32)
            state_ref[n] = (keep * block).astype(jnp.bfloat16)
    write_sent(peers, send_ref, count_ref, sign_ref, state_ref, sent_refs)


def picker(group):
    depth = 8 * TILES * group
    row = iota((32 * group, 2 * depth), 0)
    at = iota((32 * group, 2 * depth), 1)
    member, e = row // 32, row % 32
    r, j = e // QUAD, e % QUAD
    low = jnp.where(j == 0, 0, jnp.where(j == 1, 1, 2))
    high = jnp.where(j < 2, 0, j - 1)
    want_low = (r * TILES + low) * group + member
    want_high = (r * TILES + high) * group + member + depth
    return ((at == want_low) | (at == want_high)).astype(jnp.float32).astype(jnp.bfloat16)


def stack(select, rows, group):
    depth = 8 * TILES * group
    wide = jnp.concatenate([rows[g * depth : (g + 1) * depth] for g in range(3)], axis=1)
    high = iota(wide.shape, 1) % LANES >= 64
    zero = jnp.zeros_like(wide)
    both = jnp.concatenate([jnp.where(high, zero, wide), jnp.where(high, wide, zero)], axis=0)
    return jnp.dot(select, both, preferred_element_type=jnp.float32).astype(jnp.bfloat16)


def unstack(picked, member):
    mine = picked[32 * member : 32 * (member + 1)]
    return jnp.concatenate([mine[:, g * LANES : (g + 1) * LANES] for g in range(3)], axis=0)


def turn(square):
    pad = jnp.zeros((PAD - BS, LANES), jnp.bfloat16)
    turned = jnp.concatenate([square, pad], axis=0).T
    bands = [turned[32 * a : 32 * (a + 1)] for a in range(4)]
    lane = iota((32, LANES), 1)
    for bit in (1, 2):
        odd = lane & bit == bit
        bands = [jnp.where(odd, bands[(a - bit) % 4], bands[a]) for a in range(4)]
    return jnp.concatenate(bands, axis=0)


def spread_kernel(
    peers, curl_hbm, dtn_hbm, matrix_ref, face_ref, curl_ref, dtn_ref, even_ref, odd_ref, sems
):
    groups = NB // GROUP
    started = copies(
        [curl_hbm.at[pl.ds(i * GROUP, GROUP)] for i in range(groups)] + [dtn_hbm],
        [curl_ref.at[pl.ds(i * GROUP, GROUP)] for i in range(groups)] + [dtn_ref],
        sems,
    )
    select = picker(K)

    def stacked(i):
        return [stack(select, curl_ref[i * GROUP + step], K) for step in range(GROUP)]

    def store(results, held_ref):
        for step, picked in enumerate(results):
            for k in range(K):
                held_ref[step * K + k] = unstack(picked, k)

    def finish(i, held_ref):
        for step in range(GROUP):
            for k in range(K):
                matrix_ref[i * GROUP + step, k * PAD : (k + 1) * PAD] = turn(held_ref[step * K + k])

    held = (even_ref, odd_ref)
    started[0].wait()
    store(stacked(0), even_ref)
    for i in range(groups):
        if i + 1 < groups:
            started[i + 1].wait()
            results = stacked(i + 1)
        finish(i, held[i % 2])
        if i + 1 < groups:
            store(results, held[(i + 1) % 2])
    started[groups].wait()
    select_faces = picker(F)

    def face_step(q, carry):
        picked = stack(select_faces, dtn_ref[q], F)
        for f in range(F):
            face_ref[q * F + f] = turn(unstack(picked, f))
        return carry

    lax.fori_loop(0, peers, face_step, 0)


def add_faces(peers, target_ref, hole_ref, received_refs, face_ref, forcing_ref):
    me = lax.axis_index("patch")
    products = []
    for i in range(peers):
        q = lax.rem(me + peers - i, peers)
        for f in range(F):
            product = jnp.dot(
                received_refs[i][f], face_ref[q * F + f], preferred_element_type=jnp.float32
            )
            products.append((q, f, product.astype(jnp.bfloat16).astype(jnp.float32)))
    for q, f, product in products:
        n = target_ref[q, f]
        forcing_ref[n] = forcing_ref[n] + hole_ref[n].astype(jnp.float32) * product


def sweep(cols_ref, hole_ref, matrix_ref, forcing_ref, old_ref, new_ref):
    images = []
    for n in range(NB):
        nearby = jnp.concatenate([old_ref[cols_ref[k, n]] for k in range(K)], axis=1)
        images.append(jnp.dot(nearby, matrix_ref[n], preferred_element_type=jnp.float32))
    for n in range(NB):
        scale = COUPLING * hole_ref[n].astype(jnp.float32)
        new_ref[n] = (forcing_ref[n] - scale * images[n]).astype(new_ref.dtype)


def first_tick_kernel(peers, *refs):
    cols_ref, hole_ref, target_ref, send_ref, count_ref = refs[:5]
    sign_ref, matrix_ref, face_ref, begin_ref, start_ref = refs[5:10]
    received_refs = refs[10 : 10 + peers]
    state_ref, left_ref, right_ref = refs[10 + peers : 13 + peers]
    sent_refs = refs[13 + peers : 13 + 2 * peers]
    forcing_ref, other_ref = refs[13 + 2 * peers :]
    forcing_ref[...] = begin_ref[...].astype(jnp.float32)
    add_faces(peers, target_ref, hole_ref, received_refs, face_ref, forcing_ref)
    state_ref[...] = start_ref[...]

    def two(i, carry):
        sweep(cols_ref, hole_ref, matrix_ref, forcing_ref, state_ref, other_ref)
        sweep(cols_ref, hole_ref, matrix_ref, forcing_ref, other_ref, state_ref)
        return carry

    lax.fori_loop(0, ITERS // 2, two, 0)
    left_ref[...] = state_ref[:NI]
    right_ref[...] = state_ref[NB - NI :]
    write_sent(peers, send_ref, count_ref, sign_ref, state_ref, sent_refs)


def last_tick_kernel(peers, *refs):
    cols_ref, hole_ref, target_ref, matrix_ref, face_ref, begin_ref, start_ref = refs[:7]
    from_left_ref, from_right_ref = refs[7:9]
    received_refs = refs[9 : 9 + peers]
    out_ref, forcing_ref, state_ref, other_ref, final_ref = refs[9 + peers :]
    forcing_ref[...] = begin_ref[...].astype(jnp.float32)
    for n in range(NI):
        for block, arrived in ((n, from_left_ref[n]), (NB - NI + n, from_right_ref[n])):
            keep = hole_ref[block].astype(jnp.float32)
            forcing_ref[block] = forcing_ref[block] + keep * arrived.astype(jnp.float32)
    add_faces(peers, target_ref, hole_ref, received_refs, face_ref, forcing_ref)
    state_ref[...] = start_ref[...]

    def two(i, carry):
        sweep(cols_ref, hole_ref, matrix_ref, forcing_ref, state_ref, other_ref)
        sweep(cols_ref, hole_ref, matrix_ref, forcing_ref, other_ref, state_ref)
        return carry

    lax.fori_loop(0, ITERS // 2 - 1, two, 0)
    sweep(cols_ref, hole_ref, matrix_ref, forcing_ref, state_ref, other_ref)
    sweep(cols_ref, hole_ref, matrix_ref, forcing_ref, other_ref, final_ref)
    for q in range(NB // QUAD):
        tiles = join_quad([final_ref[q * QUAD + j] for j in range(QUAD)])
        for u, tile in enumerate(tiles):
            at = (q * TILES + u) * LANES
            out_ref[:, at : at + LANES] = tile


def shifted(x, axis, by):
    size = lax.axis_size(axis)
    pairs = [(i, i + by) for i in range(size) if 0 <= i + by < size]
    return lax.ppermute(x, axis, pairs)


def shape(dims, dtype):
    return jax.ShapeDtypeStruct(dims, dtype)


def shards(
    rhs, curl_blocks, block_cols, hole_mask, edge_flip, send_list, send_count, recv_list, dtn_blocks
):
    peers = send_list.shape[2]
    f32, bf16 = jnp.float32, jnp.bfloat16
    tiles = BS * BS // LANES
    cols = block_cols.T
    sends, counts, targets = send_list[0, 0], send_count[0, 0], recv_list[0, 0]
    flips = edge_flip.reshape(NB * BS // LANES, LANES)
    curl_rows = curl_blocks.reshape(NB, K, tiles, LANES).transpose(0, 2, 1, 3)
    curl_rows = curl_rows.reshape(NB, tiles * K, LANES)
    dtn_rows = dtn_blocks[0, 0].reshape(peers, F, tiles, LANES).transpose(0, 2, 1, 3)
    dtn_rows = dtn_rows.reshape(peers, tiles * F, LANES)

    block_shape = (NB, COLS, PAD)
    face = shape((F, COLS, PAD), bf16)
    ends = shape((NI, COLS, PAD), bf16)
    state, sign, *sent = pl.pallas_call(
        functools.partial(prep_kernel, peers),
        out_shape=(shape(block_shape, bf16), shape((QUAD, NB // QUAD, LANES), f32)) + (face,) * peers,
        in_specs=[HBM] * 5,
        out_specs=[VMEM] * (2 + peers),
        scratch_shapes=[
            pltpu.SMEM(sends.shape, jnp.int32),
            pltpu.SMEM(counts.shape, jnp.int32),
            pltpu.SMEM(hole_mask.shape, jnp.int32),
            pltpu.VMEM(flips.shape, jnp.int32),
            pltpu.VMEM(rhs.shape, bf16),
            pltpu.SemaphoreType.DMA((5,)),
        ],
        compiler_params=params(),
        cost_estimate=cost(10**6, 10**6),
    )(sends, counts, hole_mask, flips, rhs)

    matrices, faces = pl.pallas_call(
        functools.partial(spread_kernel, peers),
        out_shape=(shape((NB, K * PAD, PAD), bf16), shape((peers * F, PAD, PAD), bf16)),
        in_specs=[HBM] * 2,
        out_specs=[VMEM] * 2,
        scratch_shapes=[
            pltpu.VMEM(curl_rows.shape, bf16),
            pltpu.VMEM(dtn_rows.shape, bf16),
            pltpu.VMEM((GROUP * K, BS, LANES), bf16),
            pltpu.VMEM((GROUP * K, BS, LANES), bf16),
            pltpu.SemaphoreType.DMA((NB // GROUP + 1,)),
        ],
        compiler_params=params(),
        cost_estimate=cost(4 * 10**9, 16 * 10**6),
    )(curl_rows, dtn_rows)

    def exchange(sent):
        pairs = [[(p, (p + i) % peers) for p in range(peers)] for i in range(peers)]
        return [sent[0]] + [lax.ppermute(sent[i], "patch", pairs[i]) for i in range(1, peers)]

    received = exchange(sent)
    begin = state
    state, to_left, to_right, *sent = pl.pallas_call(
        functools.partial(first_tick_kernel, peers),
        out_shape=(shape(block_shape, bf16), ends, ends) + (face,) * peers,
        in_specs=[SMEM] * 5 + [VMEM] * (5 + peers),
        out_specs=[VMEM] * (3 + peers),
        scratch_shapes=[pltpu.VMEM(block_shape, f32), pltpu.VMEM(block_shape, bf16)],
        compiler_params=params(),
        cost_estimate=cost(10**10, 16 * 10**6),
    )(cols, hole_mask, targets, sends, counts, sign, matrices, faces, begin, begin, *received)

    received = exchange(sent)
    from_left = shifted(to_right, "sec", 1)
    from_right = shifted(to_left, "sec", -1)
    return pl.pallas_call(
        functools.partial(last_tick_kernel, peers),
        out_shape=shape((COLS, NB * BS), f32),
        in_specs=[SMEM] * 3 + [VMEM] * (6 + peers),
        out_specs=VMEM,
        scratch_shapes=[
            pltpu.VMEM(block_shape, f32),
            pltpu.VMEM(block_shape, bf16),
            pltpu.VMEM(block_shape, bf16),
            pltpu.VMEM(block_shape, f32),
        ],
        compiler_params=params(),
        cost_estimate=cost(10**10, 16 * 10**6),
    )(cols, hole_mask, targets, matrices, faces, begin, state, from_left, from_right, *received)


def solution(mesh):
    in_specs = (
        P(None, ("sec", "patch")),
        P(("sec", "patch"), None, None),
        P(("sec", "patch"), None),
        P(("sec", "patch")),
        P(("sec", "patch")),
        P("sec", "patch", None, None),
        P("sec", "patch", None),
        P("sec", "patch", None, None),
        P("sec", "patch", None, None, None),
    )
    out_specs = P(None, ("sec", "patch"))
    return jax.shard_map(shards, mesh=mesh, in_specs=in_specs, out_specs=out_specs, check_vma=False)
```

time: 77 us -> 57.5 us (0.75)
  the two profiles are of different devices: /device:TPU:1 before, /device:TPU:26 now
where the time goes in v2:
time: 57.5 us; the launch traced here: 57.1 us
  Pallas kernels  32.7 us (57%)
  starting transfers between devices  12.1 us (21%)
  local copies, waits for them, and re-layouts  7.14 us (12%)
  waiting for transfers between devices  4.99 us (9%)
    pallas_call x1, Pallas kernels, shards(): pl.pallas_call(functools.partial(last_tick_kernel, peers), out_shape=shap...  12.9 us
    pallas_call x1, Pallas kernels, shards(): pl.pallas_call(functools.partial(first_tick_kernel, peers), out_shape=(sh...  12.2 us
    unnamed x24, local copies, waits for them, and re-layouts  7.14 us
    pallas_call x1, Pallas kernels, shards(): pl.pallas_call(functools.partial(spread_kernel, peers), out_shape=(shape(...  6.74 us
    ppermute x6, starting transfers between devices, exchange(): lax.ppermute(sent[i], 'patch', pairs[i])  6.56 us
    ppermute x2, starting transfers between devices, shifted(): return lax.ppermute(x, axis, pairs)  5.56 us
    ppermute x6, waiting for transfers between devices, exchange(): lax.ppermute(sent[i], 'patch', pairs[i])  4.98 us
  transfers between devices with their start and end apart: 8, of which 3 were waited for; matrix products, arithmetic and copies ran while one was open for 0% of the time, Pallas kernels for 12%

profile of v2, /device:TPU:26, one launch (start us, length us, event | category | flops | bytes accessed | tf_op | source)
XLA Modules:
  0.0 57.1 jit_solution(8279550839721036326)
XLA Ops:
  0.0 1.0 %copy-done = bf16[24,6144]{1,0:T(8,128)(2,1)S(1)} copy-done((bf16[24,6144]{1,0:T(8,128)(2,1)S(1)}, bf16[24,6144]{1,0:T(8,128)(2,1)}, u32[]{:S(2)}) %copy-start) | copy-done | bytes 294936
  1.0 0.7 %copy-done.1 = s32[6144]{0:T(1024)S(1)} copy-done((s32[6144]{0:T(1024)S(1)}, s32[6144]{0:T(1024)}, u32[]{:S(2)}) %copy-start.1) | copy-done | bytes 24600
  1.8 0.7 %copy-done.2 = s32[1,1,4,8]{3,2,1,0:T(4,128)S(1)} copy-done((s32[1,1,4,8]{3,2,1,0:T(4,128)S(1)}, s32[1,1,4,8]{3,2,1,0:T(4,128)}, u32[]{:S(2)}) %copy-start.2) | copy-done | bytes 152
  2.4 0.7 %copy-done.4 = s32[1,1,4]{2,1,0:T(1,128)S(1)} copy-done((s32[1,1,4]{2,1,0:T(1,128)S(1)}, s32[1,1,4]{2,1,0:T(1,128)}, u32[]{:S(2)}) %copy-start.4) | copy-done | bytes 40
  3.1 0.7 %copy-done.6 = s32[64]{0:T(128)S(1)} copy-done((s32[64]{0:T(128)S(1)}, s32[64]{0:T(128)}, u32[]{:S(2)}) %copy-start.6) | copy-done | bytes 280
  3.8 0.9 %shard_map.92 = (bf16[64,24,128]{2,1,0:T(8,128)(2,1)S(1)}, f32[4,16,128]{2,1,0:T(8,128)S(1)}, bf16[8,24,128]{2,1,0:T(8,128)(2,1)S(1)}, bf16[8,24,128]{2,1,0:T(8,...) custom-call(s32[4,8]{1,0:T(4,128)S(1)} %bitcast.16, s32[4]{0:T(128)S(1)} %bitcast.18, ...), custom_call_target="tpu_custom_call" | custom-call | flops 1000000 | bytes 1000000 | tf_op jit(solution)/shard_map/pallas_call | solution.py:308
  4.7 1.5 %collective-permute-start = (bf16[8,24,128]{2,1,0:T(8,128)(2,1)S(1)}, bf16[8,24,128]{2,1,0:T(8,128)(2,1)S(1)}, u32[]{:S(2)}, u32[]{:S(2)}) collective-permute-start(bf16[8,24,128]{2,1,0:T(8,128)(2,1)S(1)} %get-tuple-element.25), channel_id=1, source_target_pairs={{0,1},{1,2},{2,3},{3,0},{4,5},{5,6},{6,7},{7,4},{8,9},{9,10},{10,1... | collective-permute-start | bytes 147464 | tf_op jit(solution)/shard_map/ppermute | solution.py:343
  6.2 0.5 collective-permute-start.1
  6.8 1.5 %collective-permute-start.2 = (bf16[8,24,128]{2,1,0:T(8,128)(2,1)S(1)}, bf16[8,24,128]{2,1,0:T(8,128)(2,1)S(1)}, u32[]{:S(2)}, u32[]{:S(2)}) collective-permute-start(bf16[8,24,128]{2,1,0:T(8,128)(2,1)S(1)} %get-tuple-element.27), channel_id=1, source_target_pairs={{0,3},{1,0},{2,1},{3,2},{4,7},{5,4},{6,5},{7,6},{8,11},{9,8},{10,9... | collective-permute-start | bytes 147464 | tf_op jit(solution)/shard_map/ppermute | solution.py:343
  8.3 2.3 %copy-done.8 = bf16[64,4,9216]{2,1,0:T(4,128)(2,1)S(1)} copy-done((bf16[64,4,9216]{2,1,0:T(4,128)(2,1)S(1)}, bf16[64,4,9216]{2,1,0:T(4,128)(2,1)}, u32[]{:S(2)}) %copy-start.8) | copy-done | bytes 4718616
  10.6 1.1 %copy-done.9 = bf16[1,1,4,8,9216]{4,3,2,1,0:T(8,128)(2,1)S(1)} copy-done((bf16[1,1,4,8,9216]{4,3,2,1,0:T(8,128)(2,1)S(1)}, bf16[1,1,4,8,9216]{4,3,2,1,0:T(8,128)(2,1)}, u32[]{:S(2)}) %copy-start.9) | copy-done | bytes 589848
  11.7 6.7 %shard_map.91 = (bf16[64,512,128]{2,1,0:T(8,128)(2,1)S(1)}, bf16[32,128,128]{2,1,0:T(8,128)(2,1)S(1)}) custom-call(bf16[64,288,128]{2,1,0:T(8,128)(2,1)S(1)} %bitcast.20, bf16[4,576,128]{2,1,0:T(8,128)(2,1)S(1)} %bitcast.21), custom_call_target="tpu_custom_call" | custom-call | flops 4000000000 | bytes 16000000 | tf_op jit(solution)/shard_map/pallas_call | solution.py:325
  18.5 0.0 collective-permute-done.1.refs_12_
  18.5 0.0 collective-permute-done.2.refs_13_
  18.5 12.2 %shard_map.93 = (bf16[64,24,128]{2,1,0:T(8,128)(2,1)S(1)}, bf16[8,24,128]{2,1,0:T(8,128)(2,1)S(1)}, bf16[8,24,128]{2,1,0:T(8,128)(2,1)S(1)}, bf16[8,24,128]{2,1,...) custom-call(s32[4,64]{1,0:T(4,128)S(1)} %bitcast.22, ...), custom_call_target="tpu_custom_call" | custom-call | flops 10000000000 | bytes 16000000 | tf_op jit(solution)/shard_map/pallas_call | solution.py:347
  30.7 1.9 %collective-permute-start.3 = (bf16[8,24,128]{2,1,0:T(8,128)(2,1)S(1)}, bf16[8,24,128]{2,1,0:T(8,128)(2,1)S(1)}, u32[]{:S(2)}, u32[]{:S(2)}) collective-permute-start(bf16[8,24,128]{2,1,0:T(8,128)(2,1)S(1)} %get-tuple-element.29), channel_id=1, source_target_pairs={{0,4},{4,8},{8,12},{12,16},{16,20},{20,24},{24,28},{1,5},{5,9},{9,... | collective-permute-start | bytes 147464 | tf_op jit(solution)/shard_map/ppermute | solution.py:284
  32.7 3.6 %collective-permute-start.4 = (bf16[8,24,128]{2,1,0:T(8,128)(2,1)S(1)}, bf16[8,24,128]{2,1,0:T(8,128)(2,1)S(1)}, u32[]{:S(2)}, u32[]{:S(2)}) collective-permute-start(bf16[8,24,128]{2,1,0:T(8,128)(2,1)S(1)} %get-tuple-element.30), channel_id=1, source_target_pairs={{4,0},{8,4},{12,8},{16,12},{20,16},{24,20},{28,24},{5,1},{9,5},{13... | collective-permute-start | bytes 147464 | tf_op jit(solution)/shard_map/ppermute | solution.py:284
  36.3 1.4 %collective-permute-start.5 = (bf16[8,24,128]{2,1,0:T(8,128)(2,1)S(1)}, bf16[8,24,128]{2,1,0:T(8,128)(2,1)S(1)}, u32[]{:S(2)}, u32[]{:S(2)}) collective-permute-start(bf16[8,24,128]{2,1,0:T(8,128)(2,1)S(1)} %get-tuple-element.32), channel_id=1, source_target_pairs={{0,1},{1,2},{2,3},{3,0},{4,5},{5,6},{6,7},{7,4},{8,9},{9,10},{10,1... | collective-permute-start | bytes 147464 | tf_op jit(solution)/shard_map/ppermute | solution.py:343
  37.8 1.5 %collective-permute-start.6 = (bf16[8,24,128]{2,1,0:T(8,128)(2,1)S(1)}, bf16[8,24,128]{2,1,0:T(8,128)(2,1)S(1)}, u32[]{:S(2)}, u32[]{:S(2)}) collective-permute-start(bf16[8,24,128]{2,1,0:T(8,128)(2,1)S(1)} %get-tuple-element.33), channel_id=1, source_target_pairs={{0,2},{1,3},{2,0},{3,1},{4,6},{5,7},{6,4},{7,5},{8,10},{9,11},{10,... | collective-permute-start | bytes 147464 | tf_op jit(solution)/shard_map/ppermute | solution.py:343
  39.3 0.0 collective-permute-start.7
  39.3 1.6 %collective-permute-done.5.refs_10_ = bf16[8,24,128]{2,1,0:T(8,128)(2,1)S(1)} collective-permute-done((bf16[8,24,128]{2,1,0:T(8,128)(2,1)S(1)}, bf16[8,24,128]{2,1,0:T(8,128)(2,1)S(1)}, u32[]{:S(2)}, u32[]{:S(2)}) %collective-permute-start.5) | collective-permute-done | bytes 49184 | tf_op jit(solution)/shard_map/ppermute | solution.py:343
  40.9 1.2 %collective-permute-done.6.refs_11_ = bf16[8,24,128]{2,1,0:T(8,128)(2,1)S(1)} collective-permute-done((bf16[8,24,128]{2,1,0:T(8,128)(2,1)S(1)}, bf16[8,24,128]{2,1,0:T(8,128)(2,1)S(1)}, u32[]{:S(2)}, u32[]{:S(2)}) %collective-permute-start.6) | collective-permute-done | bytes 49184 | tf_op jit(solution)/shard_map/ppermute | solution.py:343
  42.0 2.2 %collective-permute-done.7.refs_12_ = bf16[8,24,128]{2,1,0:T(8,128)(2,1)S(1)} collective-permute-done((bf16[8,24,128]{2,1,0:T(8,128)(2,1)S(1)}, bf16[8,24,128]{2,1,0:T(8,128)(2,1)S(1)}, u32[]{:S(2)}, u32[]{:S(2)}) %collective-permute-start.7) | collective-permute-done | bytes 49184 | tf_op jit(solution)/shard_map/ppermute | solution.py:343
  44.3 12.9 %shard_map.94 = f32[24,6144]{1,0:T(8,128)} custom-call(s32[4,64]{1,0:T(4,128)S(1)} %bitcast.23, s32[64]{0:T(128)S(1)} %copy-done.7, s32[4,8]{1,0:T(4,128)S(1)} %bitcast.25, bf16[64,512,128]{2,1,0:T(8,128)(2,1)S(1)} %get-tuple-element.20.refs_6_.refs_3_, bf16[32,128,128]{2,1,0:T(8,128)(2,1)S(1)} %get-tuple-element.21.refs_7_.refs_4_, ...), custom_call_target="tpu_custom_call" | custom-call | flops 10000000000 | bytes 16000000 | tf_op jit(solution)/shard_map/pallas_call | solution.py:360
  (20 shorter events, 0.0 us)
Async XLA Ops:
  0.0 18.5 %copy-start.7 = (s32[64]{0:T(128)S(1)}, s32[64]{0:T(128)}, u32[]{:S(2)}) copy-start(s32[64]{0:T(128)} %refs_1_.3) | copy-start | bytes 772
  0.0 18.5 %copy-start.5 = (s32[1,1,4]{2,1,0:T(1,128)S(1)}, s32[1,1,4]{2,1,0:T(1,128)}, u32[]{:S(2)}) copy-start(s32[1,1,4]{2,1,0:T(1,128)} %param.15) | copy-start | bytes 52
  0.0 18.5 %copy-start.3 = (s32[1,1,4,8]{3,2,1,0:T(4,128)S(1)}, s32[1,1,4,8]{3,2,1,0:T(4,128)}, u32[]{:S(2)}) copy-start(s32[1,1,4,8]{3,2,1,0:T(4,128)} %param.14) | copy-start | bytes 388
  0.0 18.5 %copy-start.10 = (s32[64,4]{0,1:T(4,128)S(1)}, s32[64,4]{0,1:T(4,128)}, u32[]{:S(2)}) copy-start(s32[64,4]{0,1:T(4,128)} %param.11) | copy-start | bytes 3076
  0.0 1.0 %copy-start = (bf16[24,6144]{1,0:T(8,128)(2,1)S(1)}, bf16[24,6144]{1,0:T(8,128)(2,1)}, u32[]{:S(2)}) copy-start(bf16[24,6144]{1,0:T(8,128)(2,1)} %refs_4_.1) | copy-start | bytes 884740
  1.0 0.7 %copy-start.1 = (s32[6144]{0:T(1024)S(1)}, s32[6144]{0:T(1024)}, u32[]{:S(2)}) copy-start(s32[6144]{0:T(1024)} %param.13) | copy-start | bytes 73732
  1.8 0.7 %copy-start.2 = (s32[1,1,4,8]{3,2,1,0:T(4,128)S(1)}, s32[1,1,4,8]{3,2,1,0:T(4,128)}, u32[]{:S(2)}) copy-start(s32[1,1,4,8]{3,2,1,0:T(4,128)} %param.14) | copy-start | bytes 388
  2.4 0.7 %copy-start.4 = (s32[1,1,4]{2,1,0:T(1,128)S(1)}, s32[1,1,4]{2,1,0:T(1,128)}, u32[]{:S(2)}) copy-start(s32[1,1,4]{2,1,0:T(1,128)} %param.15) | copy-start | bytes 52
  3.1 0.7 %copy-start.6 = (s32[64]{0:T(128)S(1)}, s32[64]{0:T(128)}, u32[]{:S(2)}) copy-start(s32[64]{0:T(128)} %refs_1_.3) | copy-start | bytes 772
  3.8 14.8 %copy-start.11 = (s32[1,1,4,8]{3,2,1,0:T(4,128)S(1)}, s32[1,1,4,8]{3,2,1,0:T(4,128)}, u32[]{:S(2)}) copy-start(s32[1,1,4,8]{3,2,1,0:T(4,128)} %param.16) | copy-start | bytes 388
  4.7 13.8 %collective-permute-start = (bf16[8,24,128]{2,1,0:T(8,128)(2,1)S(1)}, bf16[8,24,128]{2,1,0:T(8,128)(2,1)S(1)}, u32[]{:S(2)}, u32[]{:S(2)}) collective-permute-start(bf16[8,24,128]{2,1,0:T(8,128)(2,1)S(1)} %get-tuple-element.25), channel_id=1, source_target_pairs={{0,1},{1,2},{2,3},{3,0},{4,5},{5,6},{6,7},{7,4},{8,9},{9,10},{10,1... | collective-permute-start | bytes 147464 | tf_op jit(solution)/shard_map/ppermute | solution.py:343
  6.2 12.2 %collective-permute-start.1 = (bf16[8,24,128]{2,1,0:T(8,128)(2,1)S(1)}, bf16[8,24,128]{2,1,0:T(8,128)(2,1)S(1)}, u32[]{:S(2)}, u32[]{:S(2)}) collective-permute-start(bf16[8,24,128]{2,1,0:T(8,128)(2,1)S(1)} %get-tuple-element.26), channel_id=1, source_target_pairs={{0,2},{1,3},{2,0},{3,1},{4,6},{5,7},{6,4},{7,5},{8,10},{9,11},{10,... | collective-permute-start | bytes 147464 | tf_op jit(solution)/shard_map/ppermute | solution.py:343
  6.8 11.7 %collective-permute-start.2 = (bf16[8,24,128]{2,1,0:T(8,128)(2,1)S(1)}, bf16[8,24,128]{2,1,0:T(8,128)(2,1)S(1)}, u32[]{:S(2)}, u32[]{:S(2)}) collective-permute-start(bf16[8,24,128]{2,1,0:T(8,128)(2,1)S(1)} %get-tuple-element.27), channel_id=1, source_target_pairs={{0,3},{1,0},{2,1},{3,2},{4,7},{5,4},{6,5},{7,6},{8,11},{9,8},{10,9... | collective-permute-start | bytes 147464 | tf_op jit(solution)/shard_map/ppermute | solution.py:343
  8.3 2.3 %copy-start.8 = (bf16[64,4,9216]{2,1,0:T(4,128)(2,1)S(1)}, bf16[64,4,9216]{2,1,0:T(4,128)(2,1)}, u32[]{:S(2)}) copy-start(bf16[64,4,9216]{2,1,0:T(4,128)(2,1)} %param.10) | copy-start | bytes 14155780
  10.6 1.1 %copy-start.9 = (bf16[1,1,4,8,9216]{4,3,2,1,0:T(8,128)(2,1)S(1)}, bf16[1,1,4,8,9216]{4,3,2,1,0:T(8,128)(2,1)}, u32[]{:S(2)}) copy-start(bf16[1,1,4,8,9216]{4,3,2,1,0:T(8,128)(2,1)} %param.17) | copy-start | bytes 1769476
  30.7 8.5 %collective-permute-start.3 = (bf16[8,24,128]{2,1,0:T(8,128)(2,1)S(1)}, bf16[8,24,128]{2,1,0:T(8,128)(2,1)S(1)}, u32[]{:S(2)}, u32[]{:S(2)}) collective-permute-start(bf16[8,24,128]{2,1,0:T(8,128)(2,1)S(1)} %get-tuple-element.29), channel_id=1, source_target_pairs={{0,4},{4,8},{8,12},{12,16},{16,20},{20,24},{24,28},{1,5},{5,9},{9,... | collective-permute-start | bytes 147464 | tf_op jit(solution)/shard_map/ppermute | solution.py:284
  32.7 6.6 %collective-permute-start.4 = (bf16[8,24,128]{2,1,0:T(8,128)(2,1)S(1)}, bf16[8,24,128]{2,1,0:T(8,128)(2,1)S(1)}, u32[]{:S(2)}, u32[]{:S(2)}) collective-permute-start(bf16[8,24,128]{2,1,0:T(8,128)(2,1)S(1)} %get-tuple-element.30), channel_id=1, source_target_pairs={{4,0},{8,4},{12,8},{16,12},{20,16},{24,20},{28,24},{5,1},{9,5},{13... | collective-permute-start | bytes 147464 | tf_op jit(solution)/shard_map/ppermute | solution.py:284
  36.3 4.6 %collective-permute-start.5 = (bf16[8,24,128]{2,1,0:T(8,128)(2,1)S(1)}, bf16[8,24,128]{2,1,0:T(8,128)(2,1)S(1)}, u32[]{:S(2)}, u32[]{:S(2)}) collective-permute-start(bf16[8,24,128]{2,1,0:T(8,128)(2,1)S(1)} %get-tuple-element.32), channel_id=1, source_target_pairs={{0,1},{1,2},{2,3},{3,0},{4,5},{5,6},{6,7},{7,4},{8,9},{9,10},{10,1... | collective-permute-start | bytes 147464 | tf_op jit(solution)/shard_map/ppermute | solution.py:343
  37.8 4.3 %collective-permute-start.6 = (bf16[8,24,128]{2,1,0:T(8,128)(2,1)S(1)}, bf16[8,24,128]{2,1,0:T(8,128)(2,1)S(1)}, u32[]{:S(2)}, u32[]{:S(2)}) collective-permute-start(bf16[8,24,128]{2,1,0:T(8,128)(2,1)S(1)} %get-tuple-element.33), channel_id=1, source_target_pairs={{0,2},{1,3},{2,0},{3,1},{4,6},{5,7},{6,4},{7,5},{8,10},{9,11},{10,... | collective-permute-start | bytes 147464 | tf_op jit(solution)/shard_map/ppermute | solution.py:343
  39.3 5.0 %collective-permute-start.7 = (bf16[8,24,128]{2,1,0:T(8,128)(2,1)S(1)}, bf16[8,24,128]{2,1,0:T(8,128)(2,1)S(1)}, u32[]{:S(2)}, u32[]{:S(2)}) collective-permute-start(bf16[8,24,128]{2,1,0:T(8,128)(2,1)S(1)} %get-tuple-element.34), channel_id=1, source_target_pairs={{0,3},{1,0},{2,1},{3,2},{4,7},{5,4},{6,5},{7,6},{8,11},{9,8},{10,9... | collective-permute-start | bytes 147464 | tf_op jit(solution)/shard_map/ppermute | solution.py:343

commit v3 on v2

--- a/solution.py
+++ b/solution.py
@@ -23,6 +23,7 @@
 TILES = 3
 VMEM_LIMIT = 30 * 2**20
 GROUP = 8
+CHUNK = 32
 
 VMEM = pl.BlockSpec(memory_space=pltpu.VMEM)
 SMEM = pl.BlockSpec(memory_space=pltpu.SMEM)
@@ -72,7 +73,7 @@
 def write_sent(peers, send_ref, count_ref, sign_ref, state_ref, sent_refs):
     me = lax.axis_index("patch")
     for i in range(peers):
-        q = lax.rem(me + i, peers)
+        q = me ^ i
         for f in range(F):
             block = send_ref[q, f]
             scale = jnp.where(f < count_ref[q], 1.0, 0.0).astype(jnp.float32)
@@ -154,7 +155,7 @@
     for bit in (1, 2):
         odd = lane & bit == bit
         bands = [jnp.where(odd, bands[(a - bit) % 4], bands[a]) for a in range(4)]
-    return jnp.concatenate(bands, axis=0)
+    return jnp.concatenate(bands[: BS // 32], axis=0)
 
 
 def spread_kernel(
@@ -166,73 +167,91 @@
         [curl_ref.at[pl.ds(i * GROUP, GROUP)] for i in range(groups)] + [dtn_ref],
         sems,
     )
-    select = picker(K)
-
-    def stacked(i):
-        return [stack(select, curl_ref[i * GROUP + step], K) for step in range(GROUP)]
+    select, select_faces = picker(K), picker(F)
+    tasks = [
+        ([started[i]], [(select, curl_ref, i * GROUP + step, K) for step in range(GROUP)])
+        for i in range(groups)
+    ]
+    quarter = GROUP * K // F
+    for first in range(0, peers, quarter):
+        waits = [started[groups]] if first == 0 else []
+        members = range(first, min(first + quarter, peers))
+        tasks.append((waits, [(select_faces, dtn_ref, q, F) for q in members]))
+
+    def gather(task):
+        waits, items = task
+        for one in waits:
+            one.wait()
+        return [(rows, n, size, stack(pick, rows[n], size)) for pick, rows, n, size in items]
 
     def store(results, held_ref):
-        for step, picked in enumerate(results):
-            for k in range(K):
-                held_ref[step * K + k] = unstack(picked, k)
-
-    def finish(i, held_ref):
-        for step in range(GROUP):
-            for k in range(K):
-                matrix_ref[i * GROUP + step, k * PAD : (k + 1) * PAD] = turn(held_ref[step * K + k])
+        for at, (_, _, size, picked) in enumerate(results):
+            for member in range(size):
+                held_ref[at * size + member] = unstack(picked, member)
+
+    def finish(results, held_ref):
+        for at, (rows, n, size, _) in enumerate(results):
+            for member in range(size):
+                half, side = member // 2, slice(member % 2 * PAD, (member % 2 + 1) * PAD)
+                block = turn(held_ref[at * size + member])
+                if rows is curl_ref:
+                    matrix_ref[n, half, :, side] = block
+                else:
+                    face_ref[n, half, :, side] = block
 
     held = (even_ref, odd_ref)
-    started[0].wait()
-    store(stacked(0), even_ref)
-    for i in range(groups):
-        if i + 1 < groups:
-            started[i + 1].wait()
-            results = stacked(i + 1)
-        finish(i, held[i % 2])
-        if i + 1 < groups:
-            store(results, held[(i + 1) % 2])
-    started[groups].wait()
-    select_faces = picker(F)
-
-    def face_step(q, carry):
-        picked = stack(select_faces, dtn_ref[q], F)
-        for f in range(F):
-            face_ref[q * F + f] = turn(unstack(picked, f))
-        return carry
-
-    lax.fori_loop(0, peers, face_step, 0)
+    results = gather(tasks[0])
+    store(results, held[0])
+    for i in range(len(tasks)):
+        upcoming = gather(tasks[i + 1]) if i + 1 < len(tasks) else []
+        finish(results, held[i % 2])
+        store(upcoming, held[(i + 1) % 2])
+        results = upcoming
+
+
+def paired(left, right, matrices):
+    both = jnp.concatenate([left, right], axis=0)[:, :BS]
+    wide = jnp.dot(both, matrices, preferred_element_type=jnp.float32)
+    return wide[:COLS, :PAD], wide[COLS:, PAD:]
 
 
 def add_faces(peers, target_ref, hole_ref, received_refs, face_ref, forcing_ref):
     me = lax.axis_index("patch")
     products = []
     for i in range(peers):
-        q = lax.rem(me + peers - i, peers)
-        for f in range(F):
-            product = jnp.dot(
-                received_refs[i][f], face_ref[q * F + f], preferred_element_type=jnp.float32
-            )
-            products.append((q, f, product.astype(jnp.bfloat16).astype(jnp.float32)))
+        q = me ^ i
+        for f in range(0, F, 2):
+            pair = paired(received_refs[i][f], received_refs[i][f + 1], face_ref[q, f // 2])
+            for step, product in enumerate(pair):
+                products.append((q, f + step, product.astype(jnp.bfloat16).astype(jnp.float32)))
     for q, f, product in products:
         n = target_ref[q, f]
         forcing_ref[n] = forcing_ref[n] + hole_ref[n].astype(jnp.float32) * product
 
 
+def image_of(cols_ref, matrix_ref, old_ref, n):
+    total = None
+    for half in range(K // 2):
+        nearby = [old_ref[cols_ref[2 * half + side, n]] for side in range(2)]
+        left, right = paired(nearby[0], nearby[1], matrix_ref[n, half])
+        total = left + right if total is None else total + (left + right)
+    return total
+
+
 def sweep(cols_ref, hole_ref, matrix_ref, forcing_ref, old_ref, new_ref):
-    images = []
-    for n in range(NB):
-        nearby = jnp.concatenate([old_ref[cols_ref[k, n]] for k in range(K)], axis=1)
-        images.append(jnp.dot(nearby, matrix_ref[n], preferred_element_type=jnp.float32))
-    for n in range(NB):
-        scale = COUPLING * hole_ref[n].astype(jnp.float32)
-        new_ref[n] = (forcing_ref[n] - scale * images[n]).astype(new_ref.dtype)
+    for first in range(0, NB, CHUNK):
+        chunk = range(first, first + CHUNK)
+        images = [image_of(cols_ref, matrix_ref, old_ref, n) for n in chunk]
+        for n, image in zip(chunk, images):
+            scale = COUPLING * hole_ref[n].astype(jnp.float32)
+            new_ref[n] = (forcing_ref[n] - scale * image).astype(new_ref.dtype)
 
 
 def first_tick_kernel(peers, *refs):
     cols_ref, hole_ref, target_ref, send_ref, count_ref = refs[:5]
     sign_ref, matrix_ref, face_ref, begin_ref, start_ref = refs[5:10]
     received_refs = refs[10 : 10 + peers]
-    state_ref, left_ref, right_ref = refs[10 + peers : 13 + peers]
+    state_ref, swap_in_ref, swap_out_ref = refs[10 + peers : 13 + peers]
     sent_refs = refs[13 + peers : 13 + 2 * peers]
     forcing_ref, other_ref = refs[13 + 2 * peers :]
     forcing_ref[...] = begin_ref[...].astype(jnp.float32)
@@ -245,23 +264,36 @@
         return carry
 
     lax.fori_loop(0, ITERS // 2, two, 0)
-    left_ref[...] = state_ref[:NI]
-    right_ref[...] = state_ref[NB - NI :]
+    low, high = state_ref[:NI], state_ref[NB - NI :]
+    even = lax.rem(lax.axis_index("sec"), 2) == 0
+    swap_in_ref[...] = jnp.where(even, high, low)
+    swap_out_ref[...] = jnp.where(even, low, high)
     write_sent(peers, send_ref, count_ref, sign_ref, state_ref, sent_refs)
 
 
+def first_image_kernel(cols_ref, matrix_ref, state_ref, image_ref):
+    for n in range(NB):
+        image_ref[n] = image_of(cols_ref, matrix_ref, state_ref, n)
+
+
 def last_tick_kernel(peers, *refs):
-    cols_ref, hole_ref, target_ref, matrix_ref, face_ref, begin_ref, start_ref = refs[:7]
-    from_left_ref, from_right_ref = refs[7:9]
+    cols_ref, hole_ref, target_ref, matrix_ref, face_ref, begin_ref, image_ref = refs[:7]
+    swap_in_ref, swap_out_ref = refs[7:9]
     received_refs = refs[9 : 9 + peers]
     out_ref, forcing_ref, state_ref, other_ref, final_ref = refs[9 + peers :]
     forcing_ref[...] = begin_ref[...].astype(jnp.float32)
+    even = lax.rem(lax.axis_index("sec"), 2) == 0
     for n in range(NI):
-        for block, arrived in ((n, from_left_ref[n]), (NB - NI + n, from_right_ref[n])):
+        inner, outer = swap_in_ref[n], swap_out_ref[n]
+        from_left = jnp.where(even, outer, inner)
+        from_right = jnp.where(even, inner, outer)
+        for block, arrived in ((n, from_left), (NB - NI + n, from_right)):
             keep = hole_ref[block].astype(jnp.float32)
             forcing_ref[block] = forcing_ref[block] + keep * arrived.astype(jnp.float32)
     add_faces(peers, target_ref, hole_ref, received_refs, face_ref, forcing_ref)
-    state_ref[...] = start_ref[...]
+    for n in range(NB):
+        scale = COUPLING * hole_ref[n].astype(jnp.float32)
+        state_ref[n] = (forcing_ref[n] - scale * image_ref[n]).astype(jnp.bfloat16)
 
     def two(i, carry):
         sweep(cols_ref, hole_ref, matrix_ref, forcing_ref, state_ref, other_ref)
@@ -269,8 +301,7 @@
         return carry
 
     lax.fori_loop(0, ITERS // 2 - 1, two, 0)
-    sweep(cols_ref, hole_ref, matrix_ref, forcing_ref, state_ref, other_ref)
-    sweep(cols_ref, hole_ref, matrix_ref, forcing_ref, other_ref, final_ref)
+    sweep(cols_ref, hole_ref, matrix_ref, forcing_ref, state_ref, final_ref)
     for q in range(NB // QUAD):
         tiles = join_quad([final_ref[q * QUAD + j] for j in range(QUAD)])
         for u, tile in enumerate(tiles):
@@ -278,9 +309,11 @@
             out_ref[:, at : at + LANES] = tile
 
 
-def shifted(x, axis, by):
+def swapped(x, axis, first):
     size = lax.axis_size(axis)
-    pairs = [(i, i + by) for i in range(size) if 0 <= i + by < size]
+    pairs = []
+    for i in range(first, size - 1, 2):
+        pairs += [(i, i + 1), (i + 1, i)]
     return lax.ppermute(x, axis, pairs)
 
 
@@ -295,6 +328,7 @@
     f32, bf16 = jnp.float32, jnp.bfloat16
     tiles = BS * BS // LANES
     cols = block_cols.T
+    in_hbm = functools.partial(pltpu.with_memory_space_constraint, memory_space=pltpu.HBM)
     sends, counts, targets = send_list[0, 0], send_count[0, 0], recv_list[0, 0]
     flips = edge_flip.reshape(NB * BS // LANES, LANES)
     curl_rows = curl_blocks.reshape(NB, K, tiles, LANES).transpose(0, 2, 1, 3)
@@ -320,11 +354,11 @@
         ],
         compiler_params=params(),
         cost_estimate=cost(10**6, 10**6),
-    )(sends, counts, hole_mask, flips, rhs)
+    )(*map(in_hbm, (sends, counts, hole_mask, flips, rhs)))
 
     matrices, faces = pl.pallas_call(
         functools.partial(spread_kernel, peers),
-        out_shape=(shape((NB, K * PAD, PAD), bf16), shape((peers * F, PAD, PAD), bf16)),
+        out_shape=(shape((NB, K // 2, BS, 2 * PAD), bf16), shape((peers, F // 2, BS, 2 * PAD), bf16)),
         in_specs=[HBM] * 2,
         out_specs=[VMEM] * 2,
         scratch_shapes=[
@@ -336,15 +370,15 @@
         ],
         compiler_params=params(),
         cost_estimate=cost(4 * 10**9, 16 * 10**6),
-    )(curl_rows, dtn_rows)
+    )(in_hbm(curl_rows), in_hbm(dtn_rows))
 
     def exchange(sent):
-        pairs = [[(p, (p + i) % peers) for p in range(peers)] for i in range(peers)]
+        pairs = [[(p, p ^ i) for p in range(peers)] for i in range(peers)]
         return [sent[0]] + [lax.ppermute(sent[i], "patch", pairs[i]) for i in range(1, peers)]
 
     received = exchange(sent)
     begin = state
-    state, to_left, to_right, *sent = pl.pallas_call(
+    state, swap_in, swap_out, *sent = pl.pallas_call(
         functools.partial(first_tick_kernel, peers),
         out_shape=(shape(block_shape, bf16), ends, ends) + (face,) * peers,
         in_specs=[SMEM] * 5 + [VMEM] * (5 + peers),
@@ -355,8 +389,16 @@
     )(cols, hole_mask, targets, sends, counts, sign, matrices, faces, begin, begin, *received)
 
     received = exchange(sent)
-    from_left = shifted(to_right, "sec", 1)
-    from_right = shifted(to_left, "sec", -1)
+    swap_out = swapped(swap_out, "sec", 1)
+    swap_in = swapped(swap_in, "sec", 0)
+    image = pl.pallas_call(
+        first_image_kernel,
+        out_shape=shape(block_shape, f32),
+        in_specs=[SMEM] + [VMEM] * 2,
+        out_specs=VMEM,
+        compiler_params=params(),
+        cost_estimate=cost(10**9, 8 * 10**6),
+    )(cols, matrices, state)
     return pl.pallas_call(
         functools.partial(last_tick_kernel, peers),
         out_shape=shape((COLS, NB * BS), f32),
@@ -370,7 +412,7 @@
         ],
         compiler_params=params(),
         cost_estimate=cost(10**10, 16 * 10**6),
-    )(cols, hole_mask, targets, matrices, faces, begin, state, from_left, from_right, *received)
+    )(cols, hole_mask, targets, matrices, faces, begin, image, swap_in, swap_out, *received)
 
 
 def solution(mesh):

time: 57.5 us -> 40.8 us (0.71)
  the two profiles are of different devices: /device:TPU:26 before, /device:TPU:1 now
where the time goes in v3:
time: 40.8 us; the launch traced here: 40.6 us
  Pallas kernels  27.4 us (67%)
  starting transfers between devices  11.1 us (27%)
  waiting for transfers between devices  1.93 us (5%)
    pallas_call x1, Pallas kernels, shards(): pl.pallas_call(functools.partial(first_tick_kernel, peers), out_shape=(sh...  9.57 us
    pallas_call x1, Pallas kernels, shards(): pl.pallas_call(functools.partial(last_tick_kernel, peers), out_shape=shap...  9.21 us
    ppermute x6, starting transfers between devices, exchange(): lax.ppermute(sent[i], 'patch', pairs[i])  6.08 us
    pallas_call x1, Pallas kernels, shards(): pl.pallas_call(functools.partial(spread_kernel, peers), out_shape=(shape(...  5.68 us
    ppermute x2, starting transfers between devices, swapped(): return lax.ppermute(x, axis, pairs)  5.03 us
    ppermute x6, waiting for transfers between devices, exchange(): lax.ppermute(sent[i], 'patch', pairs[i])  1.92 us
    pallas_call x1, Pallas kernels, shards(): pl.pallas_call(first_image_kernel, out_shape=shape(block_shape, f32), in_...  1.59 us
    pallas_call x1, Pallas kernels, shards(): pl.pallas_call(functools.partial(prep_kernel, peers), out_shape=(shape(bl...  1.32 us
  transfers between devices with their start and end apart: 8, of which 1 were waited for; matrix products, arithmetic and copies ran while one was open for 0% of the time, Pallas kernels for 18%

profile of v3, /device:TPU:1, one launch (start us, length us, event | category | flops | bytes accessed | tf_op | source)
XLA Modules:
  0.0 40.6 jit_solution(10832745584954102213)
XLA Ops:
  0.0 1.3 %shard_map.92 = (bf16[64,24,128]{2,1,0:T(8,128)(2,1)S(1)}, f32[4,16,128]{2,1,0:T(8,128)S(1)}, bf16[8,24,128]{2,1,0:T(8,128)(2,1)S(1)}, bf16[8,24,128]{2,1,0:T(8,...) custom-call(s32[4,8]{1,0:T(4,128)} %bitcast.15, s32[4]{0:T(128)} %bitcast.20, s32[64]{0:T(128)} %refs_1_.3, ...), custom_call_target="tpu_custom_call" | custom-call | flops 1000000 | bytes 1000000 | tf_op jit(solution)/shard_map/pallas_call | solution.py:342
  1.3 2.1 %collective-permute-start = (bf16[8,24,128]{2,1,0:T(8,128)(2,1)S(1)}, bf16[8,24,128]{2,1,0:T(8,128)(2,1)S(1)}, u32[]{:S(2)}, u32[]{:S(2)}) collective-permute-start(bf16[8,24,128]{2,1,0:T(8,128)(2,1)S(1)} %get-tuple-element.25), channel_id=1, source_target_pairs={{0,1},{1,0},{2,3},{3,2},{4,5},{5,4},{6,7},{7,6},{8,9},{9,8},{10,11... | collective-permute-start | bytes 147464 | tf_op jit(solution)/shard_map/ppermute | solution.py:377
  3.4 1.2 %collective-permute-start.1 = (bf16[8,24,128]{2,1,0:T(8,128)(2,1)S(1)}, bf16[8,24,128]{2,1,0:T(8,128)(2,1)S(1)}, u32[]{:S(2)}, u32[]{:S(2)}) collective-permute-start(bf16[8,24,128]{2,1,0:T(8,128)(2,1)S(1)} %get-tuple-element.26), channel_id=1, source_target_pairs={{0,2},{1,3},{2,0},{3,1},{4,6},{5,7},{6,4},{7,5},{8,10},{9,11},{10,... | collective-permute-start | bytes 147464 | tf_op jit(solution)/shard_map/ppermute | solution.py:377
  4.7 0.0 collective-permute-start.2
  4.7 0.0 copy-start.4
  4.7 5.7 %shard_map.91 = (bf16[64,2,96,256]{3,2,1,0:T(8,128)(2,1)S(1)}, bf16[4,4,96,256]{3,2,1,0:T(8,128)(2,1)S(1)}) custom-call(bf16[64,288,128]{2,1,0:T(8,128)(2,1)} %bitcast.25, bf16[4,576,128]{2,1,0:T(8,128)(2,1)} %bitcast.26), custom_call_target="tpu_custom_call" | custom-call | flops 4000000000 | bytes 16000000 | tf_op jit(solution)/shard_map/pallas_call | solution.py:359
  10.4 0.0 collective-permute-done.refs_11_
  10.4 0.0 collective-permute-done.1.refs_12_
  10.4 0.0 collective-permute-done.2.refs_13_
  10.4 0.0 copy-done
  10.4 0.0 copy-done.1
  10.5 9.6 %shard_map.93 = (bf16[64,24,128]{2,1,0:T(8,128)(2,1)S(1)}, bf16[8,24,128]{2,1,0:T(8,128)(2,1)S(1)}, bf16[8,24,128]{2,1,0:T(8,128)(2,1)S(1)}, bf16[8,24,128]{2,1,...) custom-call(s32[4,64]{1,0:T(4,128)S(1)} %bitcast.17, ...), custom_call_target="tpu_custom_call" | custom-call | flops 10000000000 | bytes 16000000 | tf_op jit(solution)/shard_map/pallas_call | solution.py:381
  20.1 1.3 %collective-permute-start.3 = (bf16[8,24,128]{2,1,0:T(8,128)(2,1)S(1)}, bf16[8,24,128]{2,1,0:T(8,128)(2,1)S(1)}, u32[]{:S(2)}, u32[]{:S(2)}) collective-permute-start(bf16[8,24,128]{2,1,0:T(8,128)(2,1)S(1)} %get-tuple-element.29), channel_id=1, source_target_pairs={{0,4},{4,0},{8,12},{12,8},{16,20},{20,16},{24,28},{28,24},{1,5},{5... | collective-permute-start | bytes 147464 | tf_op jit(solution)/shard_map/ppermute | solution.py:317
  21.4 3.7 %collective-permute-start.4 = (bf16[8,24,128]{2,1,0:T(8,128)(2,1)S(1)}, bf16[8,24,128]{2,1,0:T(8,128)(2,1)S(1)}, u32[]{:S(2)}, u32[]{:S(2)}) collective-permute-start(bf16[8,24,128]{2,1,0:T(8,128)(2,1)S(1)} %get-tuple-element.30), channel_id=1, source_target_pairs={{4,8},{8,4},{12,16},{16,12},{20,24},{24,20},{5,9},{9,5},{13,17},{1... | collective-permute-start | bytes 147464 | tf_op jit(solution)/shard_map/ppermute | solution.py:317
  25.1 1.2 %collective-permute-start.5 = (bf16[8,24,128]{2,1,0:T(8,128)(2,1)S(1)}, bf16[8,24,128]{2,1,0:T(8,128)(2,1)S(1)}, u32[]{:S(2)}, u32[]{:S(2)}) collective-permute-start(bf16[8,24,128]{2,1,0:T(8,128)(2,1)S(1)} %get-tuple-element.32), channel_id=1, source_target_pairs={{0,1},{1,0},{2,3},{3,2},{4,5},{5,4},{6,7},{7,6},{8,9},{9,8},{10,11... | collective-permute-start | bytes 147464 | tf_op jit(solution)/shard_map/ppermute | solution.py:377
  26.3 1.2 %collective-permute-start.6 = (bf16[8,24,128]{2,1,0:T(8,128)(2,1)S(1)}, bf16[8,24,128]{2,1,0:T(8,128)(2,1)S(1)}, u32[]{:S(2)}, u32[]{:S(2)}) collective-permute-start(bf16[8,24,128]{2,1,0:T(8,128)(2,1)S(1)} %get-tuple-element.33), channel_id=1, source_target_pairs={{0,2},{1,3},{2,0},{3,1},{4,6},{5,7},{6,4},{7,5},{8,10},{9,11},{10,... | collective-permute-start | bytes 147464 | tf_op jit(solution)/shard_map/ppermute | solution.py:377
  27.5 0.3 collective-permute-start.7
  27.8 1.6 %shard_map.94.refs_6_ = f32[64,24,128]{2,1,0:T(8,128)S(1)} custom-call(s32[4,64]{1,0:T(4,128)S(1)} %bitcast.18, bf16[64,2,96,256]{3,2,1,0:T(8,128)(2,1)S(1)} %get-tuple-element.20.refs_6_.matrix_ref.refs_3_, bf16[64,24,128]{2,1,0:T(8,128)(2,1)S(1)} %get-tuple-element.28.state_ref), custom_call_target="tpu_custom_call" | custom-call | flops 1000000000 | bytes 8000000 | tf_op jit(solution)/shard_map/pallas_call | solution.py:394
  29.4 0.0 collective-permute-done.3.refs_7_
  29.4 0.0 collective-permute-done.4.refs_8_
  29.4 0.0 collective-permute-done.5.refs_10_
  29.4 0.0 collective-permute-done.6.refs_11_
  29.5 1.9 %collective-permute-done.7.refs_12_ = bf16[8,24,128]{2,1,0:T(8,128)(2,1)S(1)} collective-permute-done((bf16[8,24,128]{2,1,0:T(8,128)(2,1)S(1)}, bf16[8,24,128]{2,1,0:T(8,128)(2,1)S(1)}, u32[]{:S(2)}, u32[]{:S(2)}) %collective-permute-start.7) | collective-permute-done | bytes 49184 | tf_op jit(solution)/shard_map/ppermute | solution.py:377
  31.4 9.2 %shard_map.95 = f32[24,6144]{1,0:T(8,128)} custom-call(s32[4,64]{1,0:T(4,128)S(1)} %bitcast.19, s32[64]{0:T(128)S(1)} %copy-done.3, s32[4,8]{1,0:T(4,128)S(1)} %bitcast.23, bf16[64,2,96,256]{3,2,1,0:T(8,128)(2,1)S(1)} %get-tuple-element.20.refs_6_.matrix_ref.refs_3_, bf16[4,4,96,256]{3,2,1,0:T(8,128)(2,1)S(1)} %get-tuple-element.21.refs_7_.refs_4_, ...), custom_call_target="tpu_custom_call" | custom-call | flops 10000000000 | bytes 16000000 | tf_op jit(solution)/shard_map/pallas_call | solution.py:402
  (7 shorter events, 0.0 us)
Async XLA Ops:
  1.3 9.1 %collective-permute-start = (bf16[8,24,128]{2,1,0:T(8,128)(2,1)S(1)}, bf16[8,24,128]{2,1,0:T(8,128)(2,1)S(1)}, u32[]{:S(2)}, u32[]{:S(2)}) collective-permute-start(bf16[8,24,128]{2,1,0:T(8,128)(2,1)S(1)} %get-tuple-element.25), channel_id=1, source_target_pairs={{0,1},{1,0},{2,3},{3,2},{4,5},{5,4},{6,7},{7,6},{8,9},{9,8},{10,11... | collective-permute-start | bytes 147464 | tf_op jit(solution)/shard_map/ppermute | solution.py:377
  3.4 7.0 %collective-permute-start.1 = (bf16[8,24,128]{2,1,0:T(8,128)(2,1)S(1)}, bf16[8,24,128]{2,1,0:T(8,128)(2,1)S(1)}, u32[]{:S(2)}, u32[]{:S(2)}) collective-permute-start(bf16[8,24,128]{2,1,0:T(8,128)(2,1)S(1)} %get-tuple-element.26), channel_id=1, source_target_pairs={{0,2},{1,3},{2,0},{3,1},{4,6},{5,7},{6,4},{7,5},{8,10},{9,11},{10,... | collective-permute-start | bytes 147464 | tf_op jit(solution)/shard_map/ppermute | solution.py:377
  4.7 5.8 %collective-permute-start.2 = (bf16[8,24,128]{2,1,0:T(8,128)(2,1)S(1)}, bf16[8,24,128]{2,1,0:T(8,128)(2,1)S(1)}, u32[]{:S(2)}, u32[]{:S(2)}) collective-permute-start(bf16[8,24,128]{2,1,0:T(8,128)(2,1)S(1)} %get-tuple-element.27), channel_id=1, source_target_pairs={{0,3},{1,2},{2,1},{3,0},{4,7},{5,6},{6,5},{7,4},{8,11},{9,10},{10,... | collective-permute-start | bytes 147464 | tf_op jit(solution)/shard_map/ppermute | solution.py:377
  4.7 5.7 %copy-start = (s32[1,1,4,8]{3,2,1,0:T(4,128)S(1)}, s32[1,1,4,8]{3,2,1,0:T(4,128)}, u32[]{:S(2)}) copy-start(s32[1,1,4,8]{3,2,1,0:T(4,128)} %param.14) | copy-start | bytes 388
  4.7 5.8 %copy-start.1 = (s32[64,4]{0,1:T(4,128)S(1)}, s32[64,4]{0,1:T(4,128)}, u32[]{:S(2)}) copy-start(s32[64,4]{0,1:T(4,128)} %param.11) | copy-start | bytes 3076
  4.7 5.8 %copy-start.2 = (s32[1,1,4]{2,1,0:T(1,128)S(1)}, s32[1,1,4]{2,1,0:T(1,128)}, u32[]{:S(2)}) copy-start(s32[1,1,4]{2,1,0:T(1,128)} %param.15) | copy-start | bytes 52
  4.7 5.8 %copy-start.3 = (s32[64]{0:T(128)S(1)}, s32[64]{0:T(128)}, u32[]{:S(2)}) copy-start(s32[64]{0:T(128)} %refs_1_.3) | copy-start | bytes 772
  4.7 5.8 %copy-start.4 = (s32[1,1,4,8]{3,2,1,0:T(4,128)S(1)}, s32[1,1,4,8]{3,2,1,0:T(4,128)}, u32[]{:S(2)}) copy-start(s32[1,1,4,8]{3,2,1,0:T(4,128)} %param.16) | copy-start | bytes 388
  20.1 9.4 %collective-permute-start.3 = (bf16[8,24,128]{2,1,0:T(8,128)(2,1)S(1)}, bf16[8,24,128]{2,1,0:T(8,128)(2,1)S(1)}, u32[]{:S(2)}, u32[]{:S(2)}) collective-permute-start(bf16[8,24,128]{2,1,0:T(8,128)(2,1)S(1)} %get-tuple-element.29), channel_id=1, source_target_pairs={{0,4},{4,0},{8,12},{12,8},{16,20},{20,16},{24,28},{28,24},{1,5},{5... | collective-permute-start | bytes 147464 | tf_op jit(solution)/shard_map/ppermute | solution.py:317
  21.4 8.1 %collective-permute-start.4 = (bf16[8,24,128]{2,1,0:T(8,128)(2,1)S(1)}, bf16[8,24,128]{2,1,0:T(8,128)(2,1)S(1)}, u32[]{:S(2)}, u32[]{:S(2)}) collective-permute-start(bf16[8,24,128]{2,1,0:T(8,128)(2,1)S(1)} %get-tuple-element.30), channel_id=1, source_target_pairs={{4,8},{8,4},{12,16},{16,12},{20,24},{24,20},{5,9},{9,5},{13,17},{1... | collective-permute-start | bytes 147464 | tf_op jit(solution)/shard_map/ppermute | solution.py:317
  25.1 4.3 %collective-permute-start.5 = (bf16[8,24,128]{2,1,0:T(8,128)(2,1)S(1)}, bf16[8,24,128]{2,1,0:T(8,128)(2,1)S(1)}, u32[]{:S(2)}, u32[]{:S(2)}) collective-permute-start(bf16[8,24,128]{2,1,0:T(8,128)(2,1)S(1)} %get-tuple-element.32), channel_id=1, source_target_pairs={{0,1},{1,0},{2,3},{3,2},{4,5},{5,4},{6,7},{7,6},{8,9},{9,8},{10,11... | collective-permute-start | bytes 147464 | tf_op jit(solution)/shard_map/ppermute | solution.py:377
  26.3 3.1 %collective-permute-start.6 = (bf16[8,24,128]{2,1,0:T(8,128)(2,1)S(1)}, bf16[8,24,128]{2,1,0:T(8,128)(2,1)S(1)}, u32[]{:S(2)}, u32[]{:S(2)}) collective-permute-start(bf16[8,24,128]{2,1,0:T(8,128)(2,1)S(1)} %get-tuple-element.33), channel_id=1, source_target_pairs={{0,2},{1,3},{2,0},{3,1},{4,6},{5,7},{6,4},{7,5},{8,10},{9,11},{10,... | collective-permute-start | bytes 147464 | tf_op jit(solution)/shard_map/ppermute | solution.py:377
  27.5 3.8 %collective-permute-start.7 = (bf16[8,24,128]{2,1,0:T(8,128)(2,1)S(1)}, bf16[8,24,128]{2,1,0:T(8,128)(2,1)S(1)}, u32[]{:S(2)}, u32[]{:S(2)}) collective-permute-start(bf16[8,24,128]{2,1,0:T(8,128)(2,1)S(1)} %get-tuple-element.34), channel_id=1, source_target_pairs={{0,3},{1,2},{2,1},{3,0},{4,7},{5,6},{6,5},{7,4},{8,11},{9,10},{10,... | collective-permute-start | bytes 147464 | tf_op jit(solution)/shard_map/ppermute | solution.py:377

commit v4 on v3

--- a/solution.py
+++ b/solution.py
@@ -22,7 +22,8 @@
 QUAD = 4
 TILES = 3
 VMEM_LIMIT = 30 * 2**20
-GROUP = 8
+STAGES = (16, 16, 16, 16)
+PIECE = 8
 CHUNK = 32
 
 VMEM = pl.BlockSpec(memory_space=pltpu.VMEM)
@@ -161,22 +162,24 @@
 def spread_kernel(
     peers, curl_hbm, dtn_hbm, matrix_ref, face_ref, curl_ref, dtn_ref, even_ref, odd_ref, sems
 ):
-    groups = NB // GROUP
+    pieces = NB // PIECE
     started = copies(
-        [curl_hbm.at[pl.ds(i * GROUP, GROUP)] for i in range(groups)] + [dtn_hbm],
-        [curl_ref.at[pl.ds(i * GROUP, GROUP)] for i in range(groups)] + [dtn_ref],
+        [curl_hbm.at[pl.ds(i * PIECE, PIECE)] for i in range(pieces)] + [dtn_hbm],
+        [curl_ref.at[pl.ds(i * PIECE, PIECE)] for i in range(pieces)] + [dtn_ref],
         sems,
     )
     select, select_faces = picker(K), picker(F)
-    tasks = [
-        ([started[i]], [(select, curl_ref, i * GROUP + step, K) for step in range(GROUP)])
-        for i in range(groups)
-    ]
-    quarter = GROUP * K // F
+    tasks, done = [], 0
+    for size in STAGES:
+        waits = [started[i] for i in range(-(-done // PIECE), -(-(done + size) // PIECE))]
+        tasks.append((waits, [(select, curl_ref, done + step, K) for step in range(size)]))
+        done += size
+    quarter = max(STAGES) * K // F
     for first in range(0, peers, quarter):
-        waits = [started[groups]] if first == 0 else []
+        waits = [started[pieces]] if first == 0 else []
         members = range(first, min(first + quarter, peers))
-        tasks.append((waits, [(select_faces, dtn_ref, q, F) for q in members]))
+        faces = [(select_faces, dtn_ref, q, F) for q in members]
+        tasks.append((waits, faces))
 
     def gather(task):
         waits, items = task
@@ -364,9 +367,9 @@
         scratch_shapes=[
             pltpu.VMEM(curl_rows.shape, bf16),
             pltpu.VMEM(dtn_rows.shape, bf16),
-            pltpu.VMEM((GROUP * K, BS, LANES), bf16),
-            pltpu.VMEM((GROUP * K, BS, LANES), bf16),
-            pltpu.SemaphoreType.DMA((NB // GROUP + 1,)),
+            pltpu.VMEM((max(STAGES) * K, BS, LANES), bf16),
+            pltpu.VMEM((max(STAGES) * K, BS, LANES), bf16),
+            pltpu.SemaphoreType.DMA((NB // PIECE + 1,)),
         ],
         compiler_params=params(),
         cost_estimate=cost(4 * 10**9, 16 * 10**6),
@@ -374,7 +377,8 @@
 
     def exchange(sent):
         pairs = [[(p, p ^ i) for p in range(peers)] for i in range(peers)]
-        return [sent[0]] + [lax.ppermute(sent[i], "patch", pairs[i]) for i in range(1, peers)]
+        arrived = {i: lax.ppermute(sent[i], "patch", pairs[i]) for i in reversed(range(1, peers))}
+        return [sent[0]] + [arrived[i] for i in range(1, peers)]
 
     received = exchange(sent)
     begin = state
@@ -389,8 +393,8 @@
     )(cols, hole_mask, targets, sends, counts, sign, matrices, faces, begin, begin, *received)
 
     received = exchange(sent)
+    swap_in = swapped(swap_in, "sec", 0)
     swap_out = swapped(swap_out, "sec", 1)
-    swap_in = swapped(swap_in, "sec", 0)
     image = pl.pallas_call(
         first_image_kernel,
         out_shape=shape(block_shape, f32),

time: 40.8 us -> 40.3 us (0.988)
  transfers between devices with their start and end apart: 8 -> 8, of which waited for: 1 -> 1; matrix products, arithmetic and copies ran while one was open for 0% -> 0% of each run, Pallas kernels for 18% -> 17%
where the time goes in v4:
time: 40.3 us; the launch traced here: 40.1 us
  Pallas kernels  27 us (67%)
  starting transfers between devices  10.9 us (27%)
  waiting for transfers between devices  2.07 us (5%)
    pallas_call x1, Pallas kernels, shards(): pl.pallas_call(functools.partial(first_tick_kernel, peers), out_shape=(sh...  9.53 us
    pallas_call x1, Pallas kernels, shards(): pl.pallas_call(functools.partial(last_tick_kernel, peers), out_shape=shap...  9.22 us
    ppermute x6, starting transfers between devices, exchange(): lax.ppermute(sent[i], 'patch', pairs[i])  6.08 us
    pallas_call x1, Pallas kernels, shards(): pl.pallas_call(functools.partial(spread_kernel, peers), out_shape=(shape(...  5.34 us
    ppermute x2, starting transfers between devices, swapped(): return lax.ppermute(x, axis, pairs)  4.84 us
    ppermute x6, waiting for transfers between devices, exchange(): lax.ppermute(sent[i], 'patch', pairs[i])  2.06 us
    pallas_call x1, Pallas kernels, shards(): pl.pallas_call(first_image_kernel, out_shape=shape(block_shape, f32), in_...  1.58 us
    pallas_call x1, Pallas kernels, shards(): pl.pallas_call(functools.partial(prep_kernel, peers), out_shape=(shape(bl...  1.32 us
  transfers between devices with their start and end apart: 8, of which 1 were waited for; matrix products, arithmetic and copies ran while one was open for 0% of the time, Pallas kernels for 17%

profile of v4, /device:TPU:1, one launch (start us, length us, event | category | flops | bytes accessed | tf_op | source)
XLA Modules:
  0.0 40.1 jit_solution(1316423381637580320)
XLA Ops:
  0.0 1.3 %shard_map.92 = (bf16[64,24,128]{2,1,0:T(8,128)(2,1)S(1)}, f32[4,16,128]{2,1,0:T(8,128)S(1)}, bf16[8,24,128]{2,1,0:T(8,128)(2,1)S(1)}, bf16[8,24,128]{2,1,0:T(8,...) custom-call(s32[4,8]{1,0:T(4,128)} %bitcast.15, s32[4]{0:T(128)} %bitcast.20, s32[64]{0:T(128)} %refs_1_.3, ...), custom_call_target="tpu_custom_call" | custom-call | flops 1000000 | bytes 1000000 | tf_op jit(solution)/shard_map/pallas_call | solution.py:345
  1.3 2.1 %collective-permute-start = (bf16[8,24,128]{2,1,0:T(8,128)(2,1)S(1)}, bf16[8,24,128]{2,1,0:T(8,128)(2,1)S(1)}, u32[]{:S(2)}, u32[]{:S(2)}) collective-permute-start(bf16[8,24,128]{2,1,0:T(8,128)(2,1)S(1)} %get-tuple-element.25), channel_id=1, source_target_pairs={{0,1},{1,0},{2,3},{3,2},{4,5},{5,4},{6,7},{7,6},{8,9},{9,8},{10,11... | collective-permute-start | bytes 147464 | tf_op jit(solution)/shard_map/ppermute | solution.py:380
  3.4 1.2 %collective-permute-start.1 = (bf16[8,24,128]{2,1,0:T(8,128)(2,1)S(1)}, bf16[8,24,128]{2,1,0:T(8,128)(2,1)S(1)}, u32[]{:S(2)}, u32[]{:S(2)}) collective-permute-start(bf16[8,24,128]{2,1,0:T(8,128)(2,1)S(1)} %get-tuple-element.26), channel_id=1, source_target_pairs={{0,2},{1,3},{2,0},{3,1},{4,6},{5,7},{6,4},{7,5},{8,10},{9,11},{10,... | collective-permute-start | bytes 147464 | tf_op jit(solution)/shard_map/ppermute | solution.py:380
  4.7 0.0 collective-permute-start.2
  4.7 0.0 copy-start.4
  4.7 5.3 %shard_map.91 = (bf16[64,2,96,256]{3,2,1,0:T(8,128)(2,1)S(1)}, bf16[4,4,96,256]{3,2,1,0:T(8,128)(2,1)S(1)}) custom-call(bf16[64,288,128]{2,1,0:T(8,128)(2,1)} %bitcast.25, bf16[4,576,128]{2,1,0:T(8,128)(2,1)} %bitcast.26), custom_call_target="tpu_custom_call" | custom-call | flops 4000000000 | bytes 16000000 | tf_op jit(solution)/shard_map/pallas_call | solution.py:362
  10.1 0.0 collective-permute-done.refs_11_
  10.1 0.0 collective-permute-done.1.refs_12_
  10.1 0.0 collective-permute-done.2.refs_13_
  10.1 0.0 copy-done
  10.1 0.0 copy-done.1
  10.1 9.5 %shard_map.93 = (bf16[64,24,128]{2,1,0:T(8,128)(2,1)S(1)}, bf16[8,24,128]{2,1,0:T(8,128)(2,1)S(1)}, bf16[8,24,128]{2,1,0:T(8,128)(2,1)S(1)}, bf16[8,24,128]{2,1,...) custom-call(s32[4,64]{1,0:T(4,128)S(1)} %bitcast.17, ...), custom_call_target="tpu_custom_call" | custom-call | flops 10000000000 | bytes 16000000 | tf_op jit(solution)/shard_map/pallas_call | solution.py:385
  19.7 1.3 %collective-permute-start.3 = (bf16[8,24,128]{2,1,0:T(8,128)(2,1)S(1)}, bf16[8,24,128]{2,1,0:T(8,128)(2,1)S(1)}, u32[]{:S(2)}, u32[]{:S(2)}) collective-permute-start(bf16[8,24,128]{2,1,0:T(8,128)(2,1)S(1)} %get-tuple-element.29), channel_id=1, source_target_pairs={{0,4},{4,0},{8,12},{12,8},{16,20},{20,16},{24,28},{28,24},{1,5},{5... | collective-permute-start | bytes 147464 | tf_op jit(solution)/shard_map/ppermute | solution.py:320
  21.0 3.5 %collective-permute-start.4 = (bf16[8,24,128]{2,1,0:T(8,128)(2,1)S(1)}, bf16[8,24,128]{2,1,0:T(8,128)(2,1)S(1)}, u32[]{:S(2)}, u32[]{:S(2)}) collective-permute-start(bf16[8,24,128]{2,1,0:T(8,128)(2,1)S(1)} %get-tuple-element.30), channel_id=1, source_target_pairs={{4,8},{8,4},{12,16},{16,12},{20,24},{24,20},{5,9},{9,5},{13,17},{1... | collective-permute-start | bytes 147464 | tf_op jit(solution)/shard_map/ppermute | solution.py:320
  24.5 1.4 %collective-permute-start.5 = (bf16[8,24,128]{2,1,0:T(8,128)(2,1)S(1)}, bf16[8,24,128]{2,1,0:T(8,128)(2,1)S(1)}, u32[]{:S(2)}, u32[]{:S(2)}) collective-permute-start(bf16[8,24,128]{2,1,0:T(8,128)(2,1)S(1)} %get-tuple-element.32), channel_id=1, source_target_pairs={{0,1},{1,0},{2,3},{3,2},{4,5},{5,4},{6,7},{7,6},{8,9},{9,8},{10,11... | collective-permute-start | bytes 147464 | tf_op jit(solution)/shard_map/ppermute | solution.py:380
  25.9 1.2 %collective-permute-start.6 = (bf16[8,24,128]{2,1,0:T(8,128)(2,1)S(1)}, bf16[8,24,128]{2,1,0:T(8,128)(2,1)S(1)}, u32[]{:S(2)}, u32[]{:S(2)}) collective-permute-start(bf16[8,24,128]{2,1,0:T(8,128)(2,1)S(1)} %get-tuple-element.33), channel_id=1, source_target_pairs={{0,2},{1,3},{2,0},{3,1},{4,6},{5,7},{6,4},{7,5},{8,10},{9,11},{10,... | collective-permute-start | bytes 147464 | tf_op jit(solution)/shard_map/ppermute | solution.py:380
  27.1 0.2 collective-permute-start.7
  27.2 1.6 %shard_map.94.refs_6_ = f32[64,24,128]{2,1,0:T(8,128)S(1)} custom-call(s32[4,64]{1,0:T(4,128)S(1)} %bitcast.18, bf16[64,2,96,256]{3,2,1,0:T(8,128)(2,1)S(1)} %get-tuple-element.20.refs_6_.matrix_ref.refs_3_, bf16[64,24,128]{2,1,0:T(8,128)(2,1)S(1)} %get-tuple-element.28.state_ref), custom_call_target="tpu_custom_call" | custom-call | flops 1000000000 | bytes 8000000 | tf_op jit(solution)/shard_map/pallas_call | solution.py:398
  28.8 0.0 collective-permute-done.3.refs_7_
  28.8 0.0 collective-permute-done.4.refs_8_
  28.9 0.0 collective-permute-done.5.refs_10_
  28.9 0.0 collective-permute-done.6.refs_11_
  28.9 2.0 %collective-permute-done.7.refs_12_ = bf16[8,24,128]{2,1,0:T(8,128)(2,1)S(1)} collective-permute-done((bf16[8,24,128]{2,1,0:T(8,128)(2,1)S(1)}, bf16[8,24,128]{2,1,0:T(8,128)(2,1)S(1)}, u32[]{:S(2)}, u32[]{:S(2)}) %collective-permute-start.7) | collective-permute-done | bytes 49184 | tf_op jit(solution)/shard_map/ppermute | solution.py:380
  30.9 9.2 %shard_map.95 = f32[24,6144]{1,0:T(8,128)} custom-call(s32[4,64]{1,0:T(4,128)S(1)} %bitcast.19, s32[64]{0:T(128)S(1)} %copy-done.3, s32[4,8]{1,0:T(4,128)S(1)} %bitcast.23, bf16[64,2,96,256]{3,2,1,0:T(8,128)(2,1)S(1)} %get-tuple-element.20.refs_6_.matrix_ref.refs_3_, bf16[4,4,96,256]{3,2,1,0:T(8,128)(2,1)S(1)} %get-tuple-element.21.refs_7_.refs_4_, ...), custom_call_target="tpu_custom_call" | custom-call | flops 10000000000 | bytes 16000000 | tf_op jit(solution)/shard_map/pallas_call | solution.py:406
  (7 shorter events, 0.0 us)
Async XLA Ops:
  1.3 8.7 %collective-permute-start = (bf16[8,24,128]{2,1,0:T(8,128)(2,1)S(1)}, bf16[8,24,128]{2,1,0:T(8,128)(2,1)S(1)}, u32[]{:S(2)}, u32[]{:S(2)}) collective-permute-start(bf16[8,24,128]{2,1,0:T(8,128)(2,1)S(1)} %get-tuple-element.25), channel_id=1, source_target_pairs={{0,1},{1,0},{2,3},{3,2},{4,5},{5,4},{6,7},{7,6},{8,9},{9,8},{10,11... | collective-permute-start | bytes 147464 | tf_op jit(solution)/shard_map/ppermute | solution.py:380
  3.4 6.6 %collective-permute-start.1 = (bf16[8,24,128]{2,1,0:T(8,128)(2,1)S(1)}, bf16[8,24,128]{2,1,0:T(8,128)(2,1)S(1)}, u32[]{:S(2)}, u32[]{:S(2)}) collective-permute-start(bf16[8,24,128]{2,1,0:T(8,128)(2,1)S(1)} %get-tuple-element.26), channel_id=1, source_target_pairs={{0,2},{1,3},{2,0},{3,1},{4,6},{5,7},{6,4},{7,5},{8,10},{9,11},{10,... | collective-permute-start | bytes 147464 | tf_op jit(solution)/shard_map/ppermute | solution.py:380
  4.7 5.4 %collective-permute-start.2 = (bf16[8,24,128]{2,1,0:T(8,128)(2,1)S(1)}, bf16[8,24,128]{2,1,0:T(8,128)(2,1)S(1)}, u32[]{:S(2)}, u32[]{:S(2)}) collective-permute-start(bf16[8,24,128]{2,1,0:T(8,128)(2,1)S(1)} %get-tuple-element.27), channel_id=1, source_target_pairs={{0,3},{1,2},{2,1},{3,0},{4,7},{5,6},{6,5},{7,4},{8,11},{9,10},{10,... | collective-permute-start | bytes 147464 | tf_op jit(solution)/shard_map/ppermute | solution.py:380
  4.7 5.4 %copy-start = (s32[1,1,4,8]{3,2,1,0:T(4,128)S(1)}, s32[1,1,4,8]{3,2,1,0:T(4,128)}, u32[]{:S(2)}) copy-start(s32[1,1,4,8]{3,2,1,0:T(4,128)} %param.14) | copy-start | bytes 388
  4.7 5.4 %copy-start.1 = (s32[64,4]{0,1:T(4,128)S(1)}, s32[64,4]{0,1:T(4,128)}, u32[]{:S(2)}) copy-start(s32[64,4]{0,1:T(4,128)} %param.11) | copy-start | bytes 3076
  4.7 5.4 %copy-start.2 = (s32[1,1,4]{2,1,0:T(1,128)S(1)}, s32[1,1,4]{2,1,0:T(1,128)}, u32[]{:S(2)}) copy-start(s32[1,1,4]{2,1,0:T(1,128)} %param.15) | copy-start | bytes 52
  4.7 5.4 %copy-start.3 = (s32[64]{0:T(128)S(1)}, s32[64]{0:T(128)}, u32[]{:S(2)}) copy-start(s32[64]{0:T(128)} %refs_1_.3) | copy-start | bytes 772
  4.7 5.4 %copy-start.4 = (s32[1,1,4,8]{3,2,1,0:T(4,128)S(1)}, s32[1,1,4,8]{3,2,1,0:T(4,128)}, u32[]{:S(2)}) copy-start(s32[1,1,4,8]{3,2,1,0:T(4,128)} %param.16) | copy-start | bytes 388
  19.7 9.2 %collective-permute-start.3 = (bf16[8,24,128]{2,1,0:T(8,128)(2,1)S(1)}, bf16[8,24,128]{2,1,0:T(8,128)(2,1)S(1)}, u32[]{:S(2)}, u32[]{:S(2)}) collective-permute-start(bf16[8,24,128]{2,1,0:T(8,128)(2,1)S(1)} %get-tuple-element.29), channel_id=1, source_target_pairs={{0,4},{4,0},{8,12},{12,8},{16,20},{20,16},{24,28},{28,24},{1,5},{5... | collective-permute-start | bytes 147464 | tf_op jit(solution)/shard_map/ppermute | solution.py:320
  21.0 7.9 %collective-permute-start.4 = (bf16[8,24,128]{2,1,0:T(8,128)(2,1)S(1)}, bf16[8,24,128]{2,1,0:T(8,128)(2,1)S(1)}, u32[]{:S(2)}, u32[]{:S(2)}) collective-permute-start(bf16[8,24,128]{2,1,0:T(8,128)(2,1)S(1)} %get-tuple-element.30), channel_id=1, source_target_pairs={{4,8},{8,4},{12,16},{16,12},{20,24},{24,20},{5,9},{9,5},{13,17},{1... | collective-permute-start | bytes 147464 | tf_op jit(solution)/shard_map/ppermute | solution.py:320
  24.5 4.3 %collective-permute-start.5 = (bf16[8,24,128]{2,1,0:T(8,128)(2,1)S(1)}, bf16[8,24,128]{2,1,0:T(8,128)(2,1)S(1)}, u32[]{:S(2)}, u32[]{:S(2)}) collective-permute-start(bf16[8,24,128]{2,1,0:T(8,128)(2,1)S(1)} %get-tuple-element.32), channel_id=1, source_target_pairs={{0,1},{1,0},{2,3},{3,2},{4,5},{5,4},{6,7},{7,6},{8,9},{9,8},{10,11... | collective-permute-start | bytes 147464 | tf_op jit(solution)/shard_map/ppermute | solution.py:380
  25.9 3.0 %collective-permute-start.6 = (bf16[8,24,128]{2,1,0:T(8,128)(2,1)S(1)}, bf16[8,24,128]{2,1,0:T(8,128)(2,1)S(1)}, u32[]{:S(2)}, u32[]{:S(2)}) collective-permute-start(bf16[8,24,128]{2,1,0:T(8,128)(2,1)S(1)} %get-tuple-element.33), channel_id=1, source_target_pairs={{0,2},{1,3},{2,0},{3,1},{4,6},{5,7},{6,4},{7,5},{8,10},{9,11},{10,... | collective-permute-start | bytes 147464 | tf_op jit(solution)/shard_map/ppermute | solution.py:380
  27.1 3.8 %collective-permute-start.7 = (bf16[8,24,128]{2,1,0:T(8,128)(2,1)S(1)}, bf16[8,24,128]{2,1,0:T(8,128)(2,1)S(1)}, u32[]{:S(2)}, u32[]{:S(2)}) collective-permute-start(bf16[8,24,128]{2,1,0:T(8,128)(2,1)S(1)} %get-tuple-element.34), channel_id=1, source_target_pairs={{0,3},{1,2},{2,1},{3,0},{4,7},{5,6},{6,5},{7,4},{8,11},{9,10},{10,... | collective-permute-start | bytes 147464 | tf_op jit(solution)/shard_map/ppermute | solution.py:380

commit v5 on v4

--- a/solution.py
+++ b/solution.py
@@ -69,6 +69,10 @@
         jnp.where(lane < 64, parts[1], parts[2]),
         jnp.where(lane < 32, parts[2], parts[3]),
     ]
+
+
+def arrivals(peers):
+    return [peers - 1] + list(range(1, peers - 1)) + [0]
 
 
 def write_sent(peers, send_ref, count_ref, sign_ref, state_ref, sent_refs):
@@ -221,10 +225,10 @@
 def add_faces(peers, target_ref, hole_ref, received_refs, face_ref, forcing_ref):
     me = lax.axis_index("patch")
     products = []
-    for i in range(peers):
+    for i, received_ref in zip(arrivals(peers), received_refs):
         q = me ^ i
         for f in range(0, F, 2):
-            pair = paired(received_refs[i][f], received_refs[i][f + 1], face_ref[q, f // 2])
+            pair = paired(received_ref[f], received_ref[f + 1], face_ref[q, f // 2])
             for step, product in enumerate(pair):
                 products.append((q, f + step, product.astype(jnp.bfloat16).astype(jnp.float32)))
     for q, f, product in products:
@@ -281,8 +285,8 @@
 
 def last_tick_kernel(peers, *refs):
     cols_ref, hole_ref, target_ref, matrix_ref, face_ref, begin_ref, image_ref = refs[:7]
-    swap_in_ref, swap_out_ref = refs[7:9]
-    received_refs = refs[9 : 9 + peers]
+    received_refs = refs[7 : 7 + peers]
+    swap_in_ref, swap_out_ref = refs[7 + peers : 9 + peers]
     out_ref, forcing_ref, state_ref, other_ref, final_ref = refs[9 + peers :]
     forcing_ref[...] = begin_ref[...].astype(jnp.float32)
     even = lax.rem(lax.axis_index("sec"), 2) == 0
@@ -377,8 +381,7 @@
 
     def exchange(sent):
         pairs = [[(p, p ^ i) for p in range(peers)] for i in range(peers)]
-        arrived = {i: lax.ppermute(sent[i], "patch", pairs[i]) for i in reversed(range(1, peers))}
-        return [sent[0]] + [arrived[i] for i in range(1, peers)]
+        return [lax.ppermute(sent[i], "patch", pairs[i]) if i else sent[0] for i in arrivals(peers)]
 
     received = exchange(sent)
     begin = state
@@ -416,7 +419,7 @@
         ],
         compiler_params=params(),
         cost_estimate=cost(10**10, 16 * 10**6),
-    )(cols, hole_mask, targets, matrices, faces, begin, image, swap_in, swap_out, *received)
+    )(cols, hole_mask, targets, matrices, faces, begin, image, *received, swap_in, swap_out)
 
 
 def solution(mesh):

time: 40.3 us -> 39.4 us (0.978)
  waiting for transfers between devices: 2.07 us -> 0.35 us
  starting transfers between devices: 10.9 us -> 11.7 us
    ppermute x6, waiting for transfers between devices: 2.06 us -> 0.02 us  [exchange(): lax.ppermute(sent[i], 'patch', pairs[i])]
    ppermute x2, starting transfers between devices: 4.84 us -> 5.56 us  [swapped(): return lax.ppermute(x, axis, pairs)]
  transfers between devices with their start and end apart: 8 -> 8, of which waited for: 1 -> 1; matrix products, arithmetic and copies ran while one was open for 0% -> 0% of each run, Pallas kernels for 17% -> 18%
where the time goes in v5:
time: 39.4 us; the launch traced here: 39.2 us
  Pallas kernels  27 us (69%)
  starting transfers between devices  11.7 us (30%)
    pallas_call x1, Pallas kernels, shards(): pl.pallas_call(functools.partial(first_tick_kernel, peers), out_shape=(sh...  9.52 us
    pallas_call x1, Pallas kernels, shards(): pl.pallas_call(functools.partial(last_tick_kernel, peers), out_shape=shap...  9.21 us
    ppermute x6, starting transfers between devices, exchange(): lax.ppermute(sent[i], 'patch', pairs[i])  6.14 us
    ppermute x2, starting transfers between devices, swapped(): return lax.ppermute(x, axis, pairs)  5.56 us
    pallas_call x1, Pallas kernels, shards(): pl.pallas_call(functools.partial(spread_kernel, peers), out_shape=(shape(...  5.34 us
    pallas_call x1, Pallas kernels, shards(): pl.pallas_call(first_image_kernel, out_shape=shape(block_shape, f32), in_...  1.59 us
    pallas_call x1, Pallas kernels, shards(): pl.pallas_call(functools.partial(prep_kernel, peers), out_shape=(shape(bl...  1.32 us
  transfers between devices with their start and end apart: 8, of which 1 were waited for; matrix products, arithmetic and copies ran while one was open for 0% of the time, Pallas kernels for 18%

profile of v5, /device:TPU:1, one launch (start us, length us, event | category | flops | bytes accessed | tf_op | source)
XLA Modules:
  0.0 39.2 jit_solution(14882432196720469600)
XLA Ops:
  0.0 1.3 %shard_map.92 = (bf16[64,24,128]{2,1,0:T(8,128)(2,1)S(1)}, f32[4,16,128]{2,1,0:T(8,128)S(1)}, bf16[8,24,128]{2,1,0:T(8,128)(2,1)S(1)}, bf16[8,24,128]{2,1,0:T(8,...) custom-call(s32[4,8]{1,0:T(4,128)} %bitcast.15, s32[4]{0:T(128)} %bitcast.20, s32[64]{0:T(128)} %refs_1_.3, ...), custom_call_target="tpu_custom_call" | custom-call | flops 1000000 | bytes 1000000 | tf_op jit(solution)/shard_map/pallas_call | solution.py:349
  1.3 3.1 %collective-permute-start = (bf16[8,24,128]{2,1,0:T(8,128)(2,1)S(1)}, bf16[8,24,128]{2,1,0:T(8,128)(2,1)S(1)}, u32[]{:S(2)}, u32[]{:S(2)}) collective-permute-start(bf16[8,24,128]{2,1,0:T(8,128)(2,1)S(1)} %get-tuple-element.24), channel_id=1, source_target_pairs={{0,3},{1,2},{2,1},{3,0},{4,7},{5,6},{6,5},{7,4},{8,11},{9,10},{10,... | collective-permute-start | bytes 147464 | tf_op jit(solution)/shard_map/ppermute | solution.py:384
  4.4 0.3 collective-permute-start.1
  4.6 0.1 collective-permute-start.2
  4.8 0.0 copy-start.4
  4.8 5.3 %shard_map.91 = (bf16[64,2,96,256]{3,2,1,0:T(8,128)(2,1)S(1)}, bf16[4,4,96,256]{3,2,1,0:T(8,128)(2,1)S(1)}) custom-call(bf16[64,288,128]{2,1,0:T(8,128)(2,1)} %bitcast.25, bf16[4,576,128]{2,1,0:T(8,128)(2,1)} %bitcast.26), custom_call_target="tpu_custom_call" | custom-call | flops 4000000000 | bytes 16000000 | tf_op jit(solution)/shard_map/pallas_call | solution.py:366
  10.1 0.0 collective-permute-done.refs_10_
  10.1 0.0 collective-permute-done.1.refs_11_
  10.1 0.0 collective-permute-done.2.refs_12_
  10.2 0.0 copy-done
  10.2 0.0 copy-done.1
  10.2 9.5 %shard_map.93 = (bf16[64,24,128]{2,1,0:T(8,128)(2,1)S(1)}, bf16[8,24,128]{2,1,0:T(8,128)(2,1)S(1)}, bf16[8,24,128]{2,1,0:T(8,128)(2,1)S(1)}, bf16[8,24,128]{2,1,...) custom-call(s32[4,64]{1,0:T(4,128)S(1)} %bitcast.17, ...), custom_call_target="tpu_custom_call" | custom-call | flops 10000000000 | bytes 16000000 | tf_op jit(solution)/shard_map/pallas_call | solution.py:388
  19.7 2.3 %collective-permute-start.3 = (bf16[8,24,128]{2,1,0:T(8,128)(2,1)S(1)}, bf16[8,24,128]{2,1,0:T(8,128)(2,1)S(1)}, u32[]{:S(2)}, u32[]{:S(2)}) collective-permute-start(bf16[8,24,128]{2,1,0:T(8,128)(2,1)S(1)} %get-tuple-element.29), channel_id=1, source_target_pairs={{0,3},{1,2},{2,1},{3,0},{4,7},{5,6},{6,5},{7,4},{8,11},{9,10},{10,... | collective-permute-start | bytes 147464 | tf_op jit(solution)/shard_map/ppermute | solution.py:384
  22.1 0.4 collective-permute-start.4
  22.4 0.0 collective-permute-start.5
  22.5 2.1 %collective-permute-start.6 = (bf16[8,24,128]{2,1,0:T(8,128)(2,1)S(1)}, bf16[8,24,128]{2,1,0:T(8,128)(2,1)S(1)}, u32[]{:S(2)}, u32[]{:S(2)}) collective-permute-start(bf16[8,24,128]{2,1,0:T(8,128)(2,1)S(1)} %get-tuple-element.33), channel_id=1, source_target_pairs={{0,4},{4,0},{8,12},{12,8},{16,20},{20,16},{24,28},{28,24},{1,5},{5... | collective-permute-start | bytes 147464 | tf_op jit(solution)/shard_map/ppermute | solution.py:324
  24.6 3.4 %collective-permute-start.7 = (bf16[8,24,128]{2,1,0:T(8,128)(2,1)S(1)}, bf16[8,24,128]{2,1,0:T(8,128)(2,1)S(1)}, u32[]{:S(2)}, u32[]{:S(2)}) collective-permute-start(bf16[8,24,128]{2,1,0:T(8,128)(2,1)S(1)} %get-tuple-element.34), channel_id=1, source_target_pairs={{4,8},{8,4},{12,16},{16,12},{20,24},{24,20},{5,9},{9,5},{13,17},{1... | collective-permute-start | bytes 147464 | tf_op jit(solution)/shard_map/ppermute | solution.py:324
  28.0 1.6 %shard_map.94.refs_6_ = f32[64,24,128]{2,1,0:T(8,128)S(1)} custom-call(s32[4,64]{1,0:T(4,128)S(1)} %bitcast.18, bf16[64,2,96,256]{3,2,1,0:T(8,128)(2,1)S(1)} %get-tuple-element.20.refs_6_.matrix_ref.refs_3_, bf16[64,24,128]{2,1,0:T(8,128)(2,1)S(1)} %get-tuple-element.28.state_ref), custom_call_target="tpu_custom_call" | custom-call | flops 1000000000 | bytes 8000000 | tf_op jit(solution)/shard_map/pallas_call | solution.py:401
  29.6 0.0 collective-permute-done.3.refs_7_
  29.6 0.0 collective-permute-done.4.refs_8_
  29.6 0.0 collective-permute-done.5.refs_9_
  29.6 0.0 collective-permute-done.6.refs_11_
  29.7 0.3 collective-permute-done.7.refs_12_
  30.0 9.2 %shard_map.95 = f32[24,6144]{1,0:T(8,128)} custom-call(s32[4,64]{1,0:T(4,128)S(1)} %bitcast.19, s32[64]{0:T(128)S(1)} %copy-done.3, s32[4,8]{1,0:T(4,128)S(1)} %bitcast.23, bf16[64,2,96,256]{3,2,1,0:T(8,128)(2,1)S(1)} %get-tuple-element.20.refs_6_.matrix_ref.refs_3_, bf16[4,4,96,256]{3,2,1,0:T(8,128)(2,1)S(1)} %get-tuple-element.21.refs_7_.refs_4_, ...), custom_call_target="tpu_custom_call" | custom-call | flops 10000000000 | bytes 16000000 | tf_op jit(solution)/shard_map/pallas_call | solution.py:409
  (7 shorter events, 0.0 us)
Async XLA Ops:
  1.3 8.8 %collective-permute-start = (bf16[8,24,128]{2,1,0:T(8,128)(2,1)S(1)}, bf16[8,24,128]{2,1,0:T(8,128)(2,1)S(1)}, u32[]{:S(2)}, u32[]{:S(2)}) collective-permute-start(bf16[8,24,128]{2,1,0:T(8,128)(2,1)S(1)} %get-tuple-element.24), channel_id=1, source_target_pairs={{0,3},{1,2},{2,1},{3,0},{4,7},{5,6},{6,5},{7,4},{8,11},{9,10},{10,... | collective-permute-start | bytes 147464 | tf_op jit(solution)/shard_map/ppermute | solution.py:384
  4.4 5.8 %collective-permute-start.1 = (bf16[8,24,128]{2,1,0:T(8,128)(2,1)S(1)}, bf16[8,24,128]{2,1,0:T(8,128)(2,1)S(1)}, u32[]{:S(2)}, u32[]{:S(2)}) collective-permute-start(bf16[8,24,128]{2,1,0:T(8,128)(2,1)S(1)} %get-tuple-element.25), channel_id=1, source_target_pairs={{0,1},{1,0},{2,3},{3,2},{4,5},{5,4},{6,7},{7,6},{8,9},{9,8},{10,11... | collective-permute-start | bytes 147464 | tf_op jit(solution)/shard_map/ppermute | solution.py:384
  4.6 5.5 %collective-permute-start.2 = (bf16[8,24,128]{2,1,0:T(8,128)(2,1)S(1)}, bf16[8,24,128]{2,1,0:T(8,128)(2,1)S(1)}, u32[]{:S(2)}, u32[]{:S(2)}) collective-permute-start(bf16[8,24,128]{2,1,0:T(8,128)(2,1)S(1)} %get-tuple-element.26), channel_id=1, source_target_pairs={{0,2},{1,3},{2,0},{3,1},{4,6},{5,7},{6,4},{7,5},{8,10},{9,11},{10,... | collective-permute-start | bytes 147464 | tf_op jit(solution)/shard_map/ppermute | solution.py:384
  4.8 5.4 %copy-start = (s32[1,1,4,8]{3,2,1,0:T(4,128)S(1)}, s32[1,1,4,8]{3,2,1,0:T(4,128)}, u32[]{:S(2)}) copy-start(s32[1,1,4,8]{3,2,1,0:T(4,128)} %param.14) | copy-start | bytes 388
  4.8 5.4 %copy-start.1 = (s32[64,4]{0,1:T(4,128)S(1)}, s32[64,4]{0,1:T(4,128)}, u32[]{:S(2)}) copy-start(s32[64,4]{0,1:T(4,128)} %param.11) | copy-start | bytes 3076
  4.8 5.4 %copy-start.2 = (s32[1,1,4]{2,1,0:T(1,128)S(1)}, s32[1,1,4]{2,1,0:T(1,128)}, u32[]{:S(2)}) copy-start(s32[1,1,4]{2,1,0:T(1,128)} %param.15) | copy-start | bytes 52
  4.8 5.4 %copy-start.3 = (s32[64]{0:T(128)S(1)}, s32[64]{0:T(128)}, u32[]{:S(2)}) copy-start(s32[64]{0:T(128)} %refs_1_.3) | copy-start | bytes 772
  4.8 5.4 %copy-start.4 = (s32[1,1,4,8]{3,2,1,0:T(4,128)S(1)}, s32[1,1,4,8]{3,2,1,0:T(4,128)}, u32[]{:S(2)}) copy-start(s32[1,1,4,8]{3,2,1,0:T(4,128)} %param.16) | copy-start | bytes 388
  19.7 9.9 %collective-permute-start.3 = (bf16[8,24,128]{2,1,0:T(8,128)(2,1)S(1)}, bf16[8,24,128]{2,1,0:T(8,128)(2,1)S(1)}, u32[]{:S(2)}, u32[]{:S(2)}) collective-permute-start(bf16[8,24,128]{2,1,0:T(8,128)(2,1)S(1)} %get-tuple-element.29), channel_id=1, source_target_pairs={{0,3},{1,2},{2,1},{3,0},{4,7},{5,6},{6,5},{7,4},{8,11},{9,10},{10,... | collective-permute-start | bytes 147464 | tf_op jit(solution)/shard_map/ppermute | solution.py:384
  22.1 7.6 %collective-permute-start.4 = (bf16[8,24,128]{2,1,0:T(8,128)(2,1)S(1)}, bf16[8,24,128]{2,1,0:T(8,128)(2,1)S(1)}, u32[]{:S(2)}, u32[]{:S(2)}) collective-permute-start(bf16[8,24,128]{2,1,0:T(8,128)(2,1)S(1)} %get-tuple-element.30), channel_id=1, source_target_pairs={{0,1},{1,0},{2,3},{3,2},{4,5},{5,4},{6,7},{7,6},{8,9},{9,8},{10,11... | collective-permute-start | bytes 147464 | tf_op jit(solution)/shard_map/ppermute | solution.py:384
  22.4 7.2 %collective-permute-start.5 = (bf16[8,24,128]{2,1,0:T(8,128)(2,1)S(1)}, bf16[8,24,128]{2,1,0:T(8,128)(2,1)S(1)}, u32[]{:S(2)}, u32[]{:S(2)}) collective-permute-start(bf16[8,24,128]{2,1,0:T(8,128)(2,1)S(1)} %get-tuple-element.31), channel_id=1, source_target_pairs={{0,2},{1,3},{2,0},{3,1},{4,6},{5,7},{6,4},{7,5},{8,10},{9,11},{10,... | collective-permute-start | bytes 147464 | tf_op jit(solution)/shard_map/ppermute | solution.py:384
  22.5 7.2 %collective-permute-start.6 = (bf16[8,24,128]{2,1,0:T(8,128)(2,1)S(1)}, bf16[8,24,128]{2,1,0:T(8,128)(2,1)S(1)}, u32[]{:S(2)}, u32[]{:S(2)}) collective-permute-start(bf16[8,24,128]{2,1,0:T(8,128)(2,1)S(1)} %get-tuple-element.33), channel_id=1, source_target_pairs={{0,4},{4,0},{8,12},{12,8},{16,20},{20,16},{24,28},{28,24},{1,5},{5... | collective-permute-start | bytes 147464 | tf_op jit(solution)/shard_map/ppermute | solution.py:324
  24.6 5.4 %collective-permute-start.7 = (bf16[8,24,128]{2,1,0:T(8,128)(2,1)S(1)}, bf16[8,24,128]{2,1,0:T(8,128)(2,1)S(1)}, u32[]{:S(2)}, u32[]{:S(2)}) collective-permute-start(bf16[8,24,128]{2,1,0:T(8,128)(2,1)S(1)} %get-tuple-element.34), channel_id=1, source_target_pairs={{4,8},{8,4},{12,16},{16,12},{20,24},{24,20},{5,9},{9,5},{13,17},{1... | collective-permute-start | bytes 147464 | tf_op jit(solution)/shard_map/ppermute | solution.py:324

commit v6 on v5

v6 whole, which is shorter than its diff:
```python
import functools

import jax
import jax.numpy as jnp
from jax import lax
from jax.experimental import pallas as pl
from jax.experimental.pallas import tpu as pltpu
from jax.sharding import PartitionSpec as P

BS = 96
COLS = 24
NB = 64
K = 4
F = 8
NI = 8
ITERS = 8
TICKS = 2
COUPLING = 0.85

LANES = 128
PAD = 128
QUAD = 4
TILES = 3
VMEM_LIMIT = 30 * 2**20
STAGES = (16, 16, 16, 16)
PIECE = 8
CHUNK = 4

VMEM = pl.BlockSpec(memory_space=pltpu.VMEM)
SMEM = pl.BlockSpec(memory_space=pltpu.SMEM)
HBM = pl.BlockSpec(memory_space=pltpu.HBM)


def params():
    return pltpu.CompilerParams(vmem_limit_bytes=VMEM_LIMIT)


def cost(flops, size):
    return pl.CostEstimate(flops=flops, bytes_accessed=size, transcendentals=0)


def iota(shape, axis):
    return lax.broadcasted_iota(jnp.int32, shape, axis)


def segments(tiles):
    first, second, third = tiles
    lane = iota(first.shape, 1)
    low = lane < 64
    return first, jnp.where(low, second, first), jnp.where(low, third, second), third


def turned_by(x, lanes):
    return pltpu.roll(x, lanes % LANES, 1) if lanes % LANES else x


def split_quad(tiles):
    return [turned_by(part, 32 * j) for j, part in enumerate(segments(tiles))]


def shift_quad(tiles):
    return [turned_by(part, 32 * j + BS) for j, part in enumerate(segments(tiles))]


def join_quad(blocks):
    lane = iota(blocks[0].shape, 1)
    parts = [turned_by(block, LANES - 32 * j) for j, block in enumerate(blocks)]
    return [
        jnp.where(lane < 96, parts[0], parts[1]),
        jnp.where(lane < 64, parts[1], parts[2]),
        jnp.where(lane < 32, parts[2], parts[3]),
    ]


def store_quad(state_ref, q, tiles):
    near, far = split_quad(tiles), shift_quad(tiles)
    for j in range(QUAD):
        state_ref[0, q * QUAD + j] = near[j].astype(jnp.bfloat16)
        state_ref[1, q * QUAD + j] = far[j].astype(jnp.bfloat16)


def tall(row_tile):
    return jnp.concatenate([row_tile] * (COLS // 8), axis=0)


def arrivals(peers):
    return [peers - 1] + list(range(1, peers - 1)) + [0]


def write_sent(peers, send_ref, count_ref, sign_ref, state_ref, sent_refs):
    me = lax.axis_index("patch")
    for i in range(peers):
        q = me ^ i
        for f in range(F):
            block = send_ref[q, f]
            scale = jnp.where(f < count_ref[q], 1.0, 0.0).astype(jnp.float32)
            sign = sign_ref[lax.rem(block, QUAD), pl.ds(lax.div(block, QUAD), 1), :] * scale
            picked = state_ref[0, block].astype(jnp.float32) * sign
            sent_refs[i][f] = picked.astype(jnp.bfloat16)


def copies(sources, targets, sems):
    started = [
        pltpu.make_async_copy(source, target, sems.at[i])
        for i, (source, target) in enumerate(zip(sources, targets))
    ]
    for one in started:
        one.start()
    return started


def prep_kernel(peers, *refs):
    sources = refs[:5]
    state_ref, sign_ref, source_ref, scale_ref = refs[5:9]
    sent_refs = refs[9 : 9 + peers]
    held, sems = refs[9 + peers : -1], refs[-1]
    send_ref, count_ref, hole_ref, flip_ref, rhs_ref = held
    for one in copies(sources, held, sems):
        one.wait()
    quads = NB // QUAD
    flips = [
        1.0 - 2.0 * flip_ref[pl.ds(u, quads, stride=TILES), :].astype(jnp.float32)
        for u in range(TILES)
    ]
    for j, sign in enumerate(split_quad(flips)):
        sign_ref[j] = sign
    lane = iota((8, LANES), 1)
    for q in range(quads):
        keeps = [hole_ref[q * QUAD + j].astype(jnp.float32) for j in range(QUAD)]
        tiles = []
        for u in range(TILES):
            at = (q * TILES + u) * LANES
            keep = jnp.where(lane < BS - 32 * u, keeps[u], keeps[u + 1])
            scale_ref[q * TILES + u] = COUPLING * keep
            tile = tall(keep) * rhs_ref[:, at : at + LANES].astype(jnp.float32)
            source_ref[q * TILES + u] = tile.astype(jnp.bfloat16)
            tiles.append(tile)
        store_quad(state_ref, q, tiles)
    write_sent(peers, send_ref, count_ref, sign_ref, state_ref, sent_refs)


def picker(group):
    depth = 8 * TILES * group
    row = iota((32 * group, 2 * depth), 0)
    at = iota((32 * group, 2 * depth), 1)
    member, e = row // 32, row % 32
    r, j = e // QUAD, e % QUAD
    low = jnp.where(j == 0, 0, jnp.where(j == 1, 1, 2))
    high = jnp.where(j < 2, 0, j - 1)
    want_low = (r * TILES + low) * group + member
    want_high = (r * TILES + high) * group + member + depth
    return ((at == want_low) | (at == want_high)).astype(jnp.float32).astype(jnp.bfloat16)


def stack(select, rows, group):
    depth = 8 * TILES * group
    wide = jnp.concatenate([rows[g * depth : (g + 1) * depth] for g in range(3)], axis=1)
    high = iota(wide.shape, 1) % LANES >= 64
    zero = jnp.zeros_like(wide)
    both = jnp.concatenate([jnp.where(high, zero, wide), jnp.where(high, wide, zero)], axis=0)
    return jnp.dot(select, both, preferred_element_type=jnp.float32).astype(jnp.bfloat16)


def unstack(picked, member):
    mine = picked[32 * member : 32 * (member + 1)]
    return jnp.concatenate([mine[:, g * LANES : (g + 1) * LANES] for g in range(3)], axis=0)


def turn(square):
    turned = square.T
    bands = [turned[32 * a : 32 * (a + 1)] for a in range(4)]
    lane = iota((32, LANES), 1)
    for bit in (1, 2):
        odd = lane & bit == bit
        bands = [jnp.where(odd, bands[(a - bit) % 4], bands[a]) for a in range(4)]
    return jnp.concatenate(bands[: BS // 32], axis=0)


def spread_kernel(
    peers, curl_hbm, dtn_hbm, matrix_ref, face_ref, curl_ref, dtn_ref, even_ref, odd_ref, sems
):
    pieces = NB // PIECE
    started = copies(
        [curl_hbm.at[pl.ds(i * PIECE, PIECE)] for i in range(pieces)] + [dtn_hbm],
        [curl_ref.at[pl.ds(i * PIECE, PIECE)] for i in range(pieces)] + [dtn_ref],
        sems,
    )
    select, select_faces = picker(K), picker(F)
    tasks, done = [], 0
    for size in STAGES:
        waits = [started[i] for i in range(-(-done // PIECE), -(-(done + size) // PIECE))]
        tasks.append((waits, [(select, curl_ref, done + step, K) for step in range(size)]))
        done += size
    quarter = max(STAGES) * K // F
    for first in range(0, peers, quarter):
        waits = [started[pieces]] if first == 0 else []
        members = range(first, min(first + quarter, peers))
        faces = [(select_faces, dtn_ref, q, F) for q in members]
        tasks.append((waits, faces))

    def gather(task):
        waits, items = task
        for one in waits:
            one.wait()
        return [(rows, n, size, stack(pick, rows[n], size)) for pick, rows, n, size in items]

    def store(results, held_ref):
        for at, (rows, _, size, picked) in enumerate(results):
            for member in range(size):
                square = unstack(picked, member)
                if rows is curl_ref:
                    slot, place = at // QUAD * K + member, at % QUAD
                else:
                    slot, place = (at * size + member) // QUAD, member % QUAD
                held_ref[slot, place * BS : (place + 1) * BS] = square

    def finish(results, held_ref):
        for at, (rows, n, size, _) in enumerate(results):
            if rows is dtn_ref:
                for member in range(size):
                    half, side = member // 2, slice(member % 2 * PAD, (member % 2 + 1) * PAD)
                    slot, place = (at * size + member) // QUAD, member % QUAD
                    pad = jnp.zeros((PAD - BS, LANES), jnp.bfloat16)
                    square = held_ref[slot, place * BS : (place + 1) * BS]
                    face_ref[n, half, :, side] = turn(jnp.concatenate([square, pad], axis=0))
            elif at % QUAD == 0:
                q = n // QUAD
                for k in range(K):
                    depth = slice(k % 2 * BS, (k % 2 + 1) * BS)
                    for u in range(TILES):
                        left = (q % 2 * TILES + u) * LANES
                        square = held_ref[at // QUAD * K + k, u * LANES : (u + 1) * LANES]
                        matrix_ref[q // 2, k // 2, depth, left : left + LANES] = turn(square)

    held = (even_ref, odd_ref)
    results = gather(tasks[0])
    store(results, held[0])
    for i in range(len(tasks)):
        upcoming = gather(tasks[i + 1]) if i + 1 < len(tasks) else []
        finish(results, held[i % 2])
        store(upcoming, held[(i + 1) % 2])
        results = upcoming


def paired(left, right, matrices):
    both = jnp.concatenate([left, right], axis=0)[:, :BS]
    wide = jnp.dot(both, matrices, preferred_element_type=jnp.float32)
    return wide[:COLS, :PAD], wide[COLS:, PAD:]


def add_faces(peers, target_ref, received_refs, face_ref, extra_ref):
    me = lax.axis_index("patch")
    products = []
    for i, received_ref in zip(arrivals(peers), received_refs):
        q = me ^ i
        for f in range(0, F, 2):
            pair = paired(received_ref[f], received_ref[f + 1], face_ref[q, f // 2])
            for step, product in enumerate(pair):
                products.append((q, f + step, product.astype(jnp.bfloat16).astype(jnp.float32)))
    for q, f, product in products:
        n = target_ref[q, f]
        extra_ref[n] = extra_ref[n] + product


def set_forcing(source_ref, scale_ref, extra_ref, forcing_ref):
    for q in range(NB // QUAD):
        tiles = join_quad([extra_ref[q * QUAD + j] for j in range(QUAD)])
        for u, tile in enumerate(tiles):
            at = q * TILES + u
            kept = jnp.where(tall(scale_ref[at]) > 0, tile, 0.0)
            forcing_ref[at] = source_ref[at].astype(jnp.float32) + kept


def images_of(cols_ref, matrix_ref, old_ref, group):
    lane = iota((COLS, LANES), 1)

    def nearby(n, half):
        near = old_ref[0, cols_ref[2 * half, n]]
        far = old_ref[1, cols_ref[2 * half + 1, n]]
        return jnp.concatenate([jnp.where(lane < BS, near, far), far], axis=1)

    totals = [None] * (2 * TILES)
    for third, rows in enumerate(((0, 1, 2), (2, 3, 4, 5), (5, 6, 7))):
        columns = slice(third * 2 * LANES, (third + 1) * 2 * LANES)
        for half in range(K // 2):
            left = jnp.concatenate([nearby(group * 2 * QUAD + j, half) for j in rows], axis=0)
            wide = jnp.dot(
                left[:, : 2 * BS], matrix_ref[group, half, :, columns],
                preferred_element_type=jnp.float32,
            )
            for side in range(2):
                tile = third * 2 + side
                first = tile * LANES // BS
                cut = (first + 1) * BS - tile * LANES
                at = rows.index(first) * COLS
                part = wide[:, side * LANES : (side + 1) * LANES]
                picked = jnp.where(lane < cut, part[at : at + COLS], part[at + COLS : at + 2 * COLS])
                totals[tile] = picked if half == 0 else totals[tile] + picked
    return totals


def step_tile(forcing_ref, scale_ref, image, at):
    return forcing_ref[at] - tall(scale_ref[at]) * image


def sweep(cols_ref, scale_ref, matrix_ref, forcing_ref, old_ref, new_ref):
    groups = NB // (2 * QUAD)
    for first in range(0, groups, CHUNK):
        chunk = range(first, first + CHUNK)
        images = [images_of(cols_ref, matrix_ref, old_ref, group) for group in chunk]
        for group, parts in zip(chunk, images):
            tiles = [
                step_tile(forcing_ref, scale_ref, part, group * 2 * TILES + i)
                for i, part in enumerate(parts)
            ]
            for side in range(2):
                store_quad(new_ref, group * 2 + side, tiles[side * TILES : (side + 1) * TILES])


def first_tick_kernel(peers, *refs):
    cols_ref, target_ref, send_ref, count_ref = refs[:4]
    sign_ref, scale_ref, matrix_ref, face_ref, source_ref, start_ref = refs[4:10]
    received_refs = refs[10 : 10 + peers]
    state_ref, swap_in_ref, swap_out_ref = refs[10 + peers : 13 + peers]
    sent_refs = refs[13 + peers : 13 + 2 * peers]
    forcing_ref, extra_ref, other_ref = refs[13 + 2 * peers :]
    extra_ref[...] = jnp.zeros_like(extra_ref)
    add_faces(peers, target_ref, received_refs, face_ref, extra_ref)
    set_forcing(source_ref, scale_ref, extra_ref, forcing_ref)
    state_ref[...] = start_ref[...]

    def two(i, carry):
        sweep(cols_ref, scale_ref, matrix_ref, forcing_ref, state_ref, other_ref)
        sweep(cols_ref, scale_ref, matrix_ref, forcing_ref, other_ref, state_ref)
        return carry

    lax.fori_loop(0, ITERS // 2, two, 0)
    low, high = state_ref[0, :NI], state_ref[0, NB - NI :]
    even = lax.rem(lax.axis_index("sec"), 2) == 0
    swap_in_ref[...] = jnp.where(even, high, low)
    swap_out_ref[...] = jnp.where(even, low, high)
    write_sent(peers, send_ref, count_ref, sign_ref, state_ref, sent_refs)


def first_image_kernel(cols_ref, matrix_ref, state_ref, image_ref):
    for group in range(NB // (2 * QUAD)):
        for i, part in enumerate(images_of(cols_ref, matrix_ref, state_ref, group)):
            image_ref[group * 2 * TILES + i] = part


def last_tick_kernel(peers, *refs):
    cols_ref, target_ref, scale_ref, matrix_ref, face_ref, source_ref, image_ref = refs[:7]
    received_refs = refs[7 : 7 + peers]
    swap_in_ref, swap_out_ref = refs[7 + peers : 9 + peers]
    out_ref, forcing_ref, extra_ref, state_ref, other_ref = refs[9 + peers :]
    even = lax.rem(lax.axis_index("sec"), 2) == 0
    extra_ref[NI : NB - NI] = jnp.zeros((NB - 2 * NI, COLS, PAD), jnp.float32)
    inner = swap_in_ref[...].astype(jnp.float32)
    outer = swap_out_ref[...].astype(jnp.float32)
    extra_ref[:NI] = jnp.where(even, outer, inner)
    extra_ref[NB - NI :] = jnp.where(even, inner, outer)
    add_faces(peers, target_ref, received_refs, face_ref, extra_ref)
    set_forcing(source_ref, scale_ref, extra_ref, forcing_ref)
    for q in range(NB // QUAD):
        tiles = range(q * TILES, (q + 1) * TILES)
        store_quad(state_ref, q, [step_tile(forcing_ref, scale_ref, image_ref[i], i) for i in tiles])

    def two(i, carry):
        sweep(cols_ref, scale_ref, matrix_ref, forcing_ref, state_ref, other_ref)
        sweep(cols_ref, scale_ref, matrix_ref, forcing_ref, other_ref, state_ref)
        return carry

    lax.fori_loop(0, ITERS // 2 - 1, two, 0)
    for group in range(NB // (2 * QUAD)):
        for i, part in enumerate(images_of(cols_ref, matrix_ref, state_ref, group)):
            at = group * 2 * TILES + i
            out_ref[:, at * LANES : (at + 1) * LANES] = step_tile(forcing_ref, scale_ref, part, at)


def swapped(x, axis, first):
    size = lax.axis_size(axis)
    pairs = []
    for i in range(first, size - 1, 2):
        pairs += [(i, i + 1), (i + 1, i)]
    return lax.ppermute(x, axis, pairs)


def shape(dims, dtype):
    return jax.ShapeDtypeStruct(dims, dtype)


def shards(
    rhs, curl_blocks, block_cols, hole_mask, edge_flip, send_list, send_count, recv_list, dtn_blocks
):
    peers = send_list.shape[2]
    f32, bf16 = jnp.float32, jnp.bfloat16
    tiles = BS * BS // LANES
    cols = block_cols.T
    in_hbm = functools.partial(pltpu.with_memory_space_constraint, memory_space=pltpu.HBM)
    sends, counts, targets = send_list[0, 0], send_count[0, 0], recv_list[0, 0]
    flips = edge_flip.reshape(NB * BS // LANES, LANES)
    curl_rows = curl_blocks.reshape(NB, K, tiles, LANES).transpose(0, 2, 1, 3)
    curl_rows = curl_rows.reshape(NB, tiles * K, LANES)
    dtn_rows = dtn_blocks[0, 0].reshape(peers, F, tiles, LANES).transpose(0, 2, 1, 3)
    dtn_rows = dtn_rows.reshape(peers, tiles * F, LANES)

    count = NB * BS // LANES
    block_shape = (NB, COLS, PAD)
    tile_shape = (count, COLS, LANES)
    state_shape = (2, NB, COLS, PAD)
    face = shape((F, COLS, PAD), bf16)
    ends = shape((NI, COLS, PAD), bf16)
    state, sign, source, scale, *sent = pl.pallas_call(
        functools.partial(prep_kernel, peers),
        out_shape=(
            shape(state_shape, bf16),
            shape((QUAD, NB // QUAD, LANES), f32),
            shape(tile_shape, bf16),
            shape((count, 8, LANES), f32),
        )
        + (face,) * peers,
        in_specs=[HBM] * 5,
        out_specs=[VMEM] * (4 + peers),
        scratch_shapes=[
            pltpu.SMEM(sends.shape, jnp.int32),
            pltpu.SMEM(counts.shape, jnp.int32),
            pltpu.SMEM(hole_mask.shape, jnp.int32),
            pltpu.VMEM(flips.shape, jnp.int32),
            pltpu.VMEM(rhs.shape, bf16),
            pltpu.SemaphoreType.DMA((5,)),
        ],
        compiler_params=params(),
        cost_estimate=cost(10**6, 10**6),
    )(*map(in_hbm, (sends, counts, hole_mask, flips, rhs)))

    matrices, faces = pl.pallas_call(
        functools.partial(spread_kernel, peers),
        out_shape=(
            shape((NB // (2 * QUAD), K // 2, 2 * BS, 2 * TILES * LANES), bf16),
            shape((peers, F // 2, BS, 2 * PAD), bf16),
        ),
        in_specs=[HBM] * 2,
        out_specs=[VMEM] * 2,
        scratch_shapes=[
            pltpu.VMEM(curl_rows.shape, bf16),
            pltpu.VMEM(dtn_rows.shape, bf16),
            pltpu.VMEM((max(STAGES) * K // QUAD, QUAD * BS, LANES), bf16),
            pltpu.VMEM((max(STAGES) * K // QUAD, QUAD * BS, LANES), bf16),
            pltpu.SemaphoreType.DMA((NB // PIECE + 1,)),
        ],
        compiler_params=params(),
        cost_estimate=cost(4 * 10**9, 16 * 10**6),
    )(in_hbm(curl_rows), in_hbm(dtn_rows))

    def exchange(sent):
        pairs = [[(p, p ^ i) for p in range(peers)] for i in range(peers)]
        return [lax.ppermute(sent[i], "patch", pairs[i]) if i else sent[0] for i in arrivals(peers)]

    received = exchange(sent)
    state, swap_in, swap_out, *sent = pl.pallas_call(
        functools.partial(first_tick_kernel, peers),
        out_shape=(shape(state_shape, bf16), ends, ends) + (face,) * peers,
        in_specs=[SMEM] * 4 + [VMEM] * (6 + peers),
        out_specs=[VMEM] * (3 + peers),
        scratch_shapes=[
            pltpu.VMEM(tile_shape, f32),
            pltpu.VMEM(block_shape, f32),
            pltpu.VMEM(state_shape, bf16),
        ],
        compiler_params=params(),
        cost_estimate=cost(10**10, 16 * 10**6),
    )(cols, targets, sends, counts, sign, scale, matrices, faces, source, state, *received)

    received = exchange(sent)
    swap_in = swapped(swap_in, "sec", 0)
    swap_out = swapped(swap_out, "sec", 1)
    image = pl.pallas_call(
        first_image_kernel,
        out_shape=shape(tile_shape, f32),
        in_specs=[SMEM] + [VMEM] * 2,
        out_specs=VMEM,
        compiler_params=params(),
        cost_estimate=cost(10**9, 8 * 10**6),
    )(cols, matrices, state)
    return pl.pallas_call(
        functools.partial(last_tick_kernel, peers),
        out_shape=shape((COLS, NB * BS), f32),
        in_specs=[SMEM] * 2 + [VMEM] * (7 + peers),
        out_specs=VMEM,
        scratch_shapes=[
            pltpu.VMEM(tile_shape, f32),
            pltpu.VMEM(block_shape, f32),
            pltpu.VMEM(state_shape, bf16),
            pltpu.VMEM(state_shape, bf16),
        ],
        compiler_params=params(),
        cost_estimate=cost(10**10, 16 * 10**6),
    )(cols, targets, scale, matrices, faces, source, image, *received, swap_in, swap_out)


def solution(mesh):
    in_specs = (
        P(None, ("sec", "patch")),
        P(("sec", "patch"), None, None),
        P(("sec", "patch"), None),
        P(("sec", "patch")),
        P(("sec", "patch")),
        P("sec", "patch", None, None),
        P("sec", "patch", None),
        P("sec", "patch", None, None),
        P("sec", "patch", None, None, None),
    )
    out_specs = P(None, ("sec", "patch"))
    return jax.shard_map(shards, mesh=mesh, in_specs=in_specs, out_specs=out_specs, check_vma=False)
```

time: 39.4 us -> 38.5 us (0.977)
  Pallas kernels: 27 us -> 26.1 us
  transfers between devices with their start and end apart: 8 -> 8, of which waited for: 1 -> 1; matrix products, arithmetic and copies ran while one was open for 0% -> 0% of each run, Pallas kernels for 18% -> 17%
where the time goes in v6:
time: 38.5 us; the launch traced here: 38.4 us
  Pallas kernels  26.1 us (68%)
  starting transfers between devices  11.7 us (30%)
  waiting for transfers between devices  0.45 us (1%)
    pallas_call x1, Pallas kernels, shards(): pl.pallas_call(functools.partial(first_tick_kernel, peers), out_shape=(sh...  9.26 us
    pallas_call x1, Pallas kernels, shards(): pl.pallas_call(functools.partial(last_tick_kernel, peers), out_shape=shap...  9 us
    ppermute x6, starting transfers between devices, exchange(): lax.ppermute(sent[i], 'patch', pairs[i])  6.14 us
    ppermute x2, starting transfers between devices, swapped(): return lax.ppermute(x, axis, pairs)  5.54 us
    pallas_call x1, Pallas kernels, shards(): pl.pallas_call(functools.partial(spread_kernel, peers), out_shape=(shape(...  5.07 us
    pallas_call x1, Pallas kernels, shards(): pl.pallas_call(first_image_kernel, out_shape=shape(tile_shape, f32), in_s...  1.43 us
    pallas_call x1, Pallas kernels, shards(): pl.pallas_call(functools.partial(prep_kernel, peers), out_shape=(shape(st...  1.39 us
  transfers between devices with their start and end apart: 8, of which 1 were waited for; matrix products, arithmetic and copies ran while one was open for 0% of the time, Pallas kernels for 17%

profile of v6, /device:TPU:1, one launch (start us, length us, event | category | flops | bytes accessed | tf_op | source)
XLA Modules:
  0.0 38.4 jit_solution(3171889999321644569)
XLA Ops:
  0.0 1.4 %shard_map.91 = (bf16[2,64,24,128]{3,2,1,0:T(8,128)(2,1)S(1)}, f32[4,16,128]{2,1,0:T(8,128)S(1)}, bf16[48,24,128]{2,1,0:T(8,128)(2,1)S(1)}, f32[48,8,128]{2,1,0:...) custom-call(s32[4,8]{1,0:T(4,128)} %bitcast.15, ...), custom_call_target="tpu_custom_call" | custom-call | flops 1000000 | bytes 1000000 | tf_op jit(solution)/shard_map/pallas_call | solution.py:413
  1.4 3.1 %collective-permute-start = (bf16[8,24,128]{2,1,0:T(8,128)(2,1)S(1)}, bf16[8,24,128]{2,1,0:T(8,128)(2,1)S(1)}, u32[]{:S(2)}, u32[]{:S(2)}) collective-permute-start(bf16[8,24,128]{2,1,0:T(8,128)(2,1)S(1)} %get-tuple-element.28), channel_id=1, source_target_pairs={{0,3},{1,2},{2,1},{3,0},{4,7},{5,6},{6,5},{7,4},{8,11},{9,10},{10,... | collective-permute-start | bytes 147464 | tf_op jit(solution)/shard_map/ppermute | solution.py:457
  4.5 0.3 collective-permute-start.1
  4.7 0.1 collective-permute-start.2
  4.8 5.1 %shard_map.92 = (bf16[8,2,192,768]{3,2,1,0:T(8,128)(2,1)S(1)}, bf16[4,4,96,256]{3,2,1,0:T(8,128)(2,1)S(1)}) custom-call(bf16[64,288,128]{2,1,0:T(8,128)(2,1)} %bitcast.25, bf16[4,576,128]{2,1,0:T(8,128)(2,1)} %bitcast.26), custom_call_target="tpu_custom_call" | custom-call | flops 4000000000 | bytes 16000000 | tf_op jit(solution)/shard_map/pallas_call | solution.py:436
  9.9 0.0 collective-permute-done.refs_10_
  9.9 0.0 collective-permute-done.1.refs_11_
  9.9 0.0 collective-permute-done.2.refs_12_
  9.9 0.0 copy-done
  10.0 0.0 copy-done.1
  10.0 0.0 copy-done.2
  10.0 9.3 %shard_map.93 = (bf16[2,64,24,128]{3,2,1,0:T(8,128)(2,1)S(1)}, bf16[8,24,128]{2,1,0:T(8,128)(2,1)S(1)}, bf16[8,24,128]{2,1,0:T(8,128)(2,1)S(1)}, bf16[8,24,128]{...) custom-call(s32[4,64]{1,0:T(4,128)S(1)} %bitcast.17, ...), custom_call_target="tpu_custom_call" | custom-call | flops 10000000000 | bytes 16000000 | tf_op jit(solution)/shard_map/pallas_call | solution.py:460
  19.2 2.3 %collective-permute-start.3 = (bf16[8,24,128]{2,1,0:T(8,128)(2,1)S(1)}, bf16[8,24,128]{2,1,0:T(8,128)(2,1)S(1)}, u32[]{:S(2)}, u32[]{:S(2)}) collective-permute-start(bf16[8,24,128]{2,1,0:T(8,128)(2,1)S(1)} %get-tuple-element.33), channel_id=1, source_target_pairs={{0,3},{1,2},{2,1},{3,0},{4,7},{5,6},{6,5},{7,4},{8,11},{9,10},{10,... | collective-permute-start | bytes 147464 | tf_op jit(solution)/shard_map/ppermute | solution.py:457
  21.6 0.3 collective-permute-start.4
  21.9 0.1 collective-permute-start.5
  22.0 2.1 %collective-permute-start.6 = (bf16[8,24,128]{2,1,0:T(8,128)(2,1)S(1)}, bf16[8,24,128]{2,1,0:T(8,128)(2,1)S(1)}, u32[]{:S(2)}, u32[]{:S(2)}) collective-permute-start(bf16[8,24,128]{2,1,0:T(8,128)(2,1)S(1)} %get-tuple-element.37), channel_id=1, source_target_pairs={{0,4},{4,0},{8,12},{12,8},{16,20},{20,16},{24,28},{28,24},{1,5},{5... | collective-permute-start | bytes 147464 | tf_op jit(solution)/shard_map/ppermute | solution.py:385
  24.0 3.5 %collective-permute-start.7 = (bf16[8,24,128]{2,1,0:T(8,128)(2,1)S(1)}, bf16[8,24,128]{2,1,0:T(8,128)(2,1)S(1)}, u32[]{:S(2)}, u32[]{:S(2)}) collective-permute-start(bf16[8,24,128]{2,1,0:T(8,128)(2,1)S(1)} %get-tuple-element.38), channel_id=1, source_target_pairs={{4,8},{8,4},{12,16},{16,12},{20,24},{24,20},{5,9},{9,5},{13,17},{1... | collective-permute-start | bytes 147464 | tf_op jit(solution)/shard_map/ppermute | solution.py:385
  27.5 1.4 %shard_map.94.refs_6_ = f32[48,24,128]{2,1,0:T(8,128)S(1)} custom-call(s32[4,64]{1,0:T(4,128)S(1)} %bitcast.18, bf16[8,2,192,768]{3,2,1,0:T(8,128)(2,1)S(1)} %get-tuple-element.23.refs_6_.matrix_ref.refs_3_, bf16[2,64,24,128]{3,2,1,0:T(8,128)(2,1)S(1)} %get-tuple-element.32.state_ref), custom_call_target="tpu_custom_call" | custom-call | flops 1000000000 | bytes 8000000 | tf_op jit(solution)/shard_map/pallas_call | solution.py:477
  28.9 0.0 collective-permute-done.3.refs_7_
  29.0 0.0 collective-permute-done.4.refs_8_
  29.0 0.0 collective-permute-done.5.refs_9_
  29.0 0.0 collective-permute-done.6.refs_11_
  29.0 0.4 %collective-permute-done.7.refs_12_ = bf16[8,24,128]{2,1,0:T(8,128)(2,1)S(1)} collective-permute-done((bf16[8,24,128]{2,1,0:T(8,128)(2,1)S(1)}, bf16[8,24,128]{2,1,0:T(8,128)(2,1)S(1)}, u32[]{:S(2)}, u32[]{:S(2)}) %collective-permute-start.7) | collective-permute-done | bytes 49184 | tf_op jit(solution)/shard_map/ppermute | solution.py:385
  29.4 9.0 %shard_map.95 = f32[24,6144]{1,0:T(8,128)} custom-call(s32[4,64]{1,0:T(4,128)S(1)} %bitcast.19, s32[4,8]{1,0:T(4,128)S(1)} %bitcast.23, f32[48,8,128]{2,1,0:T(8,128)S(1)} %get-tuple-element.22.refs_5_.refs_2_, bf16[8,2,192,768]{3,2,1,0:T(8,128)(2,1)S(1)} %get-tuple-element.23.refs_6_.matrix_ref.refs_3_, ...), custom_call_target="tpu_custom_call" | custom-call | flops 10000000000 | bytes 16000000 | tf_op jit(solution)/shard_map/pallas_call | solution.py:485
  (5 shorter events, 0.0 us)
Async XLA Ops:
  1.4 8.5 %collective-permute-start = (bf16[8,24,128]{2,1,0:T(8,128)(2,1)S(1)}, bf16[8,24,128]{2,1,0:T(8,128)(2,1)S(1)}, u32[]{:S(2)}, u32[]{:S(2)}) collective-permute-start(bf16[8,24,128]{2,1,0:T(8,128)(2,1)S(1)} %get-tuple-element.28), channel_id=1, source_target_pairs={{0,3},{1,2},{2,1},{3,0},{4,7},{5,6},{6,5},{7,4},{8,11},{9,10},{10,... | collective-permute-start | bytes 147464 | tf_op jit(solution)/shard_map/ppermute | solution.py:457
  4.5 5.5 %collective-permute-start.1 = (bf16[8,24,128]{2,1,0:T(8,128)(2,1)S(1)}, bf16[8,24,128]{2,1,0:T(8,128)(2,1)S(1)}, u32[]{:S(2)}, u32[]{:S(2)}) collective-permute-start(bf16[8,24,128]{2,1,0:T(8,128)(2,1)S(1)} %get-tuple-element.29), channel_id=1, source_target_pairs={{0,1},{1,0},{2,3},{3,2},{4,5},{5,4},{6,7},{7,6},{8,9},{9,8},{10,11... | collective-permute-start | bytes 147464 | tf_op jit(solution)/shard_map/ppermute | solution.py:457
  4.7 5.2 %collective-permute-start.2 = (bf16[8,24,128]{2,1,0:T(8,128)(2,1)S(1)}, bf16[8,24,128]{2,1,0:T(8,128)(2,1)S(1)}, u32[]{:S(2)}, u32[]{:S(2)}) collective-permute-start(bf16[8,24,128]{2,1,0:T(8,128)(2,1)S(1)} %get-tuple-element.30), channel_id=1, source_target_pairs={{0,2},{1,3},{2,0},{3,1},{4,6},{5,7},{6,4},{7,5},{8,10},{9,11},{10,... | collective-permute-start | bytes 147464 | tf_op jit(solution)/shard_map/ppermute | solution.py:457
  4.8 5.1 %copy-start = (s32[1,1,4,8]{3,2,1,0:T(4,128)S(1)}, s32[1,1,4,8]{3,2,1,0:T(4,128)}, u32[]{:S(2)}) copy-start(s32[1,1,4,8]{3,2,1,0:T(4,128)} %param.14) | copy-start | bytes 388
  4.8 5.1 %copy-start.1 = (s32[64,4]{0,1:T(4,128)S(1)}, s32[64,4]{0,1:T(4,128)}, u32[]{:S(2)}) copy-start(s32[64,4]{0,1:T(4,128)} %param.11) | copy-start | bytes 3076
  4.8 5.1 %copy-start.2 = (s32[1,1,4]{2,1,0:T(1,128)S(1)}, s32[1,1,4]{2,1,0:T(1,128)}, u32[]{:S(2)}) copy-start(s32[1,1,4]{2,1,0:T(1,128)} %param.15) | copy-start | bytes 52
  4.8 5.1 %copy-start.3 = (s32[1,1,4,8]{3,2,1,0:T(4,128)S(1)}, s32[1,1,4,8]{3,2,1,0:T(4,128)}, u32[]{:S(2)}) copy-start(s32[1,1,4,8]{3,2,1,0:T(4,128)} %param.16) | copy-start | bytes 388
  19.2 9.7 %collective-permute-start.3 = (bf16[8,24,128]{2,1,0:T(8,128)(2,1)S(1)}, bf16[8,24,128]{2,1,0:T(8,128)(2,1)S(1)}, u32[]{:S(2)}, u32[]{:S(2)}) collective-permute-start(bf16[8,24,128]{2,1,0:T(8,128)(2,1)S(1)} %get-tuple-element.33), channel_id=1, source_target_pairs={{0,3},{1,2},{2,1},{3,0},{4,7},{5,6},{6,5},{7,4},{8,11},{9,10},{10,... | collective-permute-start | bytes 147464 | tf_op jit(solution)/shard_map/ppermute | solution.py:457
  21.6 7.4 %collective-permute-start.4 = (bf16[8,24,128]{2,1,0:T(8,128)(2,1)S(1)}, bf16[8,24,128]{2,1,0:T(8,128)(2,1)S(1)}, u32[]{:S(2)}, u32[]{:S(2)}) collective-permute-start(bf16[8,24,128]{2,1,0:T(8,128)(2,1)S(1)} %get-tuple-element.34), channel_id=1, source_target_pairs={{0,1},{1,0},{2,3},{3,2},{4,5},{5,4},{6,7},{7,6},{8,9},{9,8},{10,11... | collective-permute-start | bytes 147464 | tf_op jit(solution)/shard_map/ppermute | solution.py:457
  21.9 7.1 %collective-permute-start.5 = (bf16[8,24,128]{2,1,0:T(8,128)(2,1)S(1)}, bf16[8,24,128]{2,1,0:T(8,128)(2,1)S(1)}, u32[]{:S(2)}, u32[]{:S(2)}) collective-permute-start(bf16[8,24,128]{2,1,0:T(8,128)(2,1)S(1)} %get-tuple-element.35), channel_id=1, source_target_pairs={{0,2},{1,3},{2,0},{3,1},{4,6},{5,7},{6,4},{7,5},{8,10},{9,11},{10,... | collective-permute-start | bytes 147464 | tf_op jit(solution)/shard_map/ppermute | solution.py:457
  22.0 7.0 %collective-permute-start.6 = (bf16[8,24,128]{2,1,0:T(8,128)(2,1)S(1)}, bf16[8,24,128]{2,1,0:T(8,128)(2,1)S(1)}, u32[]{:S(2)}, u32[]{:S(2)}) collective-permute-start(bf16[8,24,128]{2,1,0:T(8,128)(2,1)S(1)} %get-tuple-element.37), channel_id=1, source_target_pairs={{0,4},{4,0},{8,12},{12,8},{16,20},{20,16},{24,28},{28,24},{1,5},{5... | collective-permute-start | bytes 147464 | tf_op jit(solution)/shard_map/ppermute | solution.py:385
  24.0 5.4 %collective-permute-start.7 = (bf16[8,24,128]{2,1,0:T(8,128)(2,1)S(1)}, bf16[8,24,128]{2,1,0:T(8,128)(2,1)S(1)}, u32[]{:S(2)}, u32[]{:S(2)}) collective-permute-start(bf16[8,24,128]{2,1,0:T(8,128)(2,1)S(1)} %get-tuple-element.38), channel_id=1, source_target_pairs={{4,8},{8,4},{12,16},{16,12},{20,24},{24,20},{5,9},{9,5},{13,17},{1... | collective-permute-start | bytes 147464 | tf_op jit(solution)/shard_map/ppermute | solution.py:385

commit v7 on v6

--- a/solution.py
+++ b/solution.py
@@ -110,12 +110,15 @@
 
 
 def prep_kernel(peers, *refs):
-    sources = refs[:5]
-    state_ref, sign_ref, source_ref, scale_ref = refs[5:9]
-    sent_refs = refs[9 : 9 + peers]
-    held, sems = refs[9 + peers : -1], refs[-1]
+    sources, curl_hbm = refs[:5], refs[5]
+    state_ref, sign_ref, source_ref, scale_ref, head_ref = refs[6:11]
+    sent_refs = refs[11 : 11 + peers]
+    held, sems = refs[11 + peers : -1], refs[-1]
     send_ref, count_ref, hole_ref, flip_ref, rhs_ref = held
-    for one in copies(sources, held, sems):
+    *needed, ahead = copies(
+        sources + (curl_hbm.at[pl.ds(0, STAGES[0])],), held + (head_ref,), sems
+    )
+    for one in needed:
         one.wait()
     quads = NB // QUAD
     flips = [
@@ -137,6 +140,7 @@
             tiles.append(tile)
         store_quad(state_ref, q, tiles)
     write_sent(peers, send_ref, count_ref, sign_ref, state_ref, sent_refs)
+    ahead.wait()
 
 
 def picker(group):
@@ -177,17 +181,19 @@
 
 
 def spread_kernel(
-    peers, curl_hbm, dtn_hbm, matrix_ref, face_ref, curl_ref, dtn_ref, even_ref, odd_ref, sems
+    peers, curl_hbm, dtn_hbm, head_ref, matrix_ref, face_ref, curl_ref, dtn_ref, even_ref, odd_ref,
+    sems,
 ):
-    pieces = NB // PIECE
+    ahead = STAGES[0]
+    pieces = (NB - ahead) // PIECE
     started = copies(
-        [curl_hbm.at[pl.ds(i * PIECE, PIECE)] for i in range(pieces)] + [dtn_hbm],
+        [curl_hbm.at[pl.ds(ahead + i * PIECE, PIECE)] for i in range(pieces)] + [dtn_hbm],
         [curl_ref.at[pl.ds(i * PIECE, PIECE)] for i in range(pieces)] + [dtn_ref],
         sems,
     )
     select, select_faces = picker(K), picker(F)
-    tasks, done = [], 0
-    for size in STAGES:
+    tasks, done = [([], [(select, head_ref, step, K) for step in range(ahead)])], 0
+    for size in STAGES[1:]:
         waits = [started[i] for i in range(-(-done // PIECE), -(-(done + size) // PIECE))]
         tasks.append((waits, [(select, curl_ref, done + step, K) for step in range(size)]))
         done += size
@@ -208,10 +214,10 @@
         for at, (rows, _, size, picked) in enumerate(results):
             for member in range(size):
                 square = unstack(picked, member)
-                if rows is curl_ref:
+                if rows is dtn_ref:
+                    slot, place = (at * size + member) // QUAD, member % QUAD
+                else:
                     slot, place = at // QUAD * K + member, at % QUAD
-                else:
-                    slot, place = (at * size + member) // QUAD, member % QUAD
                 held_ref[slot, place * BS : (place + 1) * BS] = square
 
     def finish(results, held_ref):
@@ -224,7 +230,7 @@
                     square = held_ref[slot, place * BS : (place + 1) * BS]
                     face_ref[n, half, :, side] = turn(jnp.concatenate([square, pad], axis=0))
             elif at % QUAD == 0:
-                q = n // QUAD
+                q = (n if rows is head_ref else ahead + n) // QUAD
                 for k in range(K):
                     depth = slice(k % 2 * BS, (k % 2 + 1) * BS)
                     for u in range(TILES):
@@ -259,12 +265,13 @@
                 products.append((q, f + step, product.astype(jnp.bfloat16).astype(jnp.float32)))
     for q, f, product in products:
         n = target_ref[q, f]
-        extra_ref[n] = extra_ref[n] + product
+        extra_ref[f % 2, n] = extra_ref[f % 2, n] + product
 
 
 def set_forcing(source_ref, scale_ref, extra_ref, forcing_ref):
     for q in range(NB // QUAD):
-        tiles = join_quad([extra_ref[q * QUAD + j] for j in range(QUAD)])
+        blocks = range(q * QUAD, (q + 1) * QUAD)
+        tiles = join_quad([extra_ref[0, n] + extra_ref[1, n] for n in blocks])
         for u, tile in enumerate(tiles):
             at = q * TILES + u
             kept = jnp.where(tall(scale_ref[at]) > 0, tile, 0.0)
@@ -317,9 +324,14 @@
                 store_quad(new_ref, group * 2 + side, tiles[side * TILES : (side + 1) * TILES])
 
 
+def end_blocks():
+    odd = lax.rem(lax.axis_index("sec"), 2)
+    return (1 - odd) * (NB - NI), odd * (NB - NI)
+
+
 def first_tick_kernel(peers, *refs):
     cols_ref, target_ref, send_ref, count_ref = refs[:4]
-    sign_ref, scale_ref, matrix_ref, face_ref, source_ref, start_ref = refs[4:10]
+    sign_ref, scale_ref, matrix_ref, face_ref, source_ref = refs[4:9]
     received_refs = refs[10 : 10 + peers]
     state_ref, swap_in_ref, swap_out_ref = refs[10 + peers : 13 + peers]
     sent_refs = refs[13 + peers : 13 + 2 * peers]
@@ -327,7 +339,6 @@
     extra_ref[...] = jnp.zeros_like(extra_ref)
     add_faces(peers, target_ref, received_refs, face_ref, extra_ref)
     set_forcing(source_ref, scale_ref, extra_ref, forcing_ref)
-    state_ref[...] = start_ref[...]
 
     def two(i, carry):
         sweep(cols_ref, scale_ref, matrix_ref, forcing_ref, state_ref, other_ref)
@@ -335,10 +346,9 @@
         return carry
 
     lax.fori_loop(0, ITERS // 2, two, 0)
-    low, high = state_ref[0, :NI], state_ref[0, NB - NI :]
-    even = lax.rem(lax.axis_index("sec"), 2) == 0
-    swap_in_ref[...] = jnp.where(even, high, low)
-    swap_out_ref[...] = jnp.where(even, low, high)
+    inner, outer = end_blocks()
+    swap_in_ref[...] = state_ref[0, pl.ds(inner, NI)]
+    swap_out_ref[...] = state_ref[0, pl.ds(outer, NI)]
     write_sent(peers, send_ref, count_ref, sign_ref, state_ref, sent_refs)
 
 
@@ -353,12 +363,10 @@
     received_refs = refs[7 : 7 + peers]
     swap_in_ref, swap_out_ref = refs[7 + peers : 9 + peers]
     out_ref, forcing_ref, extra_ref, state_ref, other_ref = refs[9 + peers :]
-    even = lax.rem(lax.axis_index("sec"), 2) == 0
-    extra_ref[NI : NB - NI] = jnp.zeros((NB - 2 * NI, COLS, PAD), jnp.float32)
-    inner = swap_in_ref[...].astype(jnp.float32)
-    outer = swap_out_ref[...].astype(jnp.float32)
-    extra_ref[:NI] = jnp.where(even, outer, inner)
-    extra_ref[NB - NI :] = jnp.where(even, inner, outer)
+    inner, outer = end_blocks()
+    extra_ref[...] = jnp.zeros_like(extra_ref)
+    extra_ref[0, pl.ds(inner, NI)] = swap_in_ref[...].astype(jnp.float32)
+    extra_ref[0, pl.ds(outer, NI)] = swap_out_ref[...].astype(jnp.float32)
     add_faces(peers, target_ref, received_refs, face_ref, extra_ref)
     set_forcing(source_ref, scale_ref, extra_ref, forcing_ref)
     for q in range(NB // QUAD):
@@ -410,28 +418,29 @@
     state_shape = (2, NB, COLS, PAD)
     face = shape((F, COLS, PAD), bf16)
     ends = shape((NI, COLS, PAD), bf16)
-    state, sign, source, scale, *sent = pl.pallas_call(
+    state, sign, source, scale, head, *sent = pl.pallas_call(
         functools.partial(prep_kernel, peers),
         out_shape=(
             shape(state_shape, bf16),
             shape((QUAD, NB // QUAD, LANES), f32),
             shape(tile_shape, bf16),
             shape((count, 8, LANES), f32),
+            shape((STAGES[0],) + curl_rows.shape[1:], bf16),
         )
         + (face,) * peers,
-        in_specs=[HBM] * 5,
-        out_specs=[VMEM] * (4 + peers),
+        in_specs=[HBM] * 6,
+        out_specs=[VMEM] * (5 + peers),
         scratch_shapes=[
             pltpu.SMEM(sends.shape, jnp.int32),
             pltpu.SMEM(counts.shape, jnp.int32),
             pltpu.SMEM(hole_mask.shape, jnp.int32),
             pltpu.VMEM(flips.shape, jnp.int32),
             pltpu.VMEM(rhs.shape, bf16),
-            pltpu.SemaphoreType.DMA((5,)),
+            pltpu.SemaphoreType.DMA((6,)),
         ],
         compiler_params=params(),
         cost_estimate=cost(10**6, 10**6),
-    )(*map(in_hbm, (sends, counts, hole_mask, flips, rhs)))
+    )(*map(in_hbm, (sends, counts, hole_mask, flips, rhs, curl_rows)))
 
     matrices, faces = pl.pallas_call(
         functools.partial(spread_kernel, peers),
@@ -439,18 +448,18 @@
             shape((NB // (2 * QUAD), K // 2, 2 * BS, 2 * TILES * LANES), bf16),
             shape((peers, F // 2, BS, 2 * PAD), bf16),
         ),
-        in_specs=[HBM] * 2,
+        in_specs=[HBM] * 2 + [VMEM],
         out_specs=[VMEM] * 2,
         scratch_shapes=[
-            pltpu.VMEM(curl_rows.shape, bf16),
+            pltpu.VMEM((NB - STAGES[0],) + curl_rows.shape[1:], bf16),
             pltpu.VMEM(dtn_rows.shape, bf16),
             pltpu.VMEM((max(STAGES) * K // QUAD, QUAD * BS, LANES), bf16),
             pltpu.VMEM((max(STAGES) * K // QUAD, QUAD * BS, LANES), bf16),
-            pltpu.SemaphoreType.DMA((NB // PIECE + 1,)),
+            pltpu.SemaphoreType.DMA(((NB - STAGES[0]) // PIECE + 1,)),
         ],
         compiler_params=params(),
         cost_estimate=cost(4 * 10**9, 16 * 10**6),
-    )(in_hbm(curl_rows), in_hbm(dtn_rows))
+    )(in_hbm(curl_rows), in_hbm(dtn_rows), head)
 
     def exchange(sent):
         pairs = [[(p, p ^ i) for p in range(peers)] for i in range(peers)]
@@ -464,9 +473,10 @@
         out_specs=[VMEM] * (3 + peers),
         scratch_shapes=[
             pltpu.VMEM(tile_shape, f32),
-            pltpu.VMEM(block_shape, f32),
+            pltpu.VMEM((2,) + block_shape, f32),
             pltpu.VMEM(state_shape, bf16),
         ],
+        input_output_aliases={9: 0},
         compiler_params=params(),
         cost_estimate=cost(10**10, 16 * 10**6),
     )(cols, targets, sends, counts, sign, scale, matrices, faces, source, state, *received)
@@ -489,7 +499,7 @@
         out_specs=VMEM,
         scratch_shapes=[
             pltpu.VMEM(tile_shape, f32),
-            pltpu.VMEM(block_shape, f32),
+            pltpu.VMEM((2,) + block_shape, f32),
             pltpu.VMEM(state_shape, bf16),
             pltpu.VMEM(state_shape, bf16),
         ],

time: 38.5 us -> 38.8 us (level)
  no operation moved by 1% of the time
where the time goes in v7:
time: 38.8 us; the launch traced here: 38.6 us
  Pallas kernels  26.2 us (68%)
  starting transfers between devices  11.8 us (30%)
  waiting for transfers between devices  0.46 us (1%)
    pallas_call x1, Pallas kernels, shards(): pl.pallas_call(functools.partial(first_tick_kernel, peers), out_shape=(sh...  9.27 us
    pallas_call x1, Pallas kernels, shards(): pl.pallas_call(functools.partial(last_tick_kernel, peers), out_shape=shap...  9.08 us
    ppermute x6, starting transfers between devices, exchange(): lax.ppermute(sent[i], 'patch', pairs[i])  6.14 us
    ppermute x2, starting transfers between devices, swapped(): return lax.ppermute(x, axis, pairs)  5.63 us
    pallas_call x1, Pallas kernels, shards(): pl.pallas_call(functools.partial(spread_kernel, peers), out_shape=(shape(...  5 us
    pallas_call x1, Pallas kernels, shards(): pl.pallas_call(functools.partial(prep_kernel, peers), out_shape=(shape(st...  1.44 us
    pallas_call x1, Pallas kernels, shards(): pl.pallas_call(first_image_kernel, out_shape=shape(tile_shape, f32), in_s...  1.44 us
  transfers between devices with their start and end apart: 8, of which 1 were waited for; matrix products, arithmetic and copies ran while one was open for 0% of the time, Pallas kernels for 17%

profile of v7, /device:TPU:1, one launch (start us, length us, event | category | flops | bytes accessed | tf_op | source)
XLA Modules:
  0.0 38.6 jit_solution(13606605075678308917)
XLA Ops:
  0.0 1.4 %shard_map.91 = (bf16[2,64,24,128]{3,2,1,0:T(8,128)(2,1)S(1)}, f32[4,16,128]{2,1,0:T(8,128)S(1)}, bf16[48,24,128]{2,1,0:T(8,128)(2,1)S(1)}, f32[48,8,128]{2,1,0:...) custom-call(s32[4,8]{1,0:T(4,128)} %bitcast.15, ...), custom_call_target="tpu_custom_call" | custom-call | flops 1000000 | bytes 1000000 | tf_op jit(solution)/shard_map/pallas_call | solution.py:421
  1.4 3.1 %collective-permute-start = (bf16[8,24,128]{2,1,0:T(8,128)(2,1)S(1)}, bf16[8,24,128]{2,1,0:T(8,128)(2,1)S(1)}, u32[]{:S(2)}, u32[]{:S(2)}) collective-permute-start(bf16[8,24,128]{2,1,0:T(8,128)(2,1)S(1)} %get-tuple-element.30), channel_id=1, source_target_pairs={{0,3},{1,2},{2,1},{3,0},{4,7},{5,6},{6,5},{7,4},{8,11},{9,10},{10,... | collective-permute-start | bytes 147464 | tf_op jit(solution)/shard_map/ppermute | solution.py:466
  4.5 0.3 collective-permute-start.1
  4.8 0.1 collective-permute-start.2
  4.9 5.0 %shard_map.92 = (bf16[8,2,192,768]{3,2,1,0:T(8,128)(2,1)S(1)}, bf16[4,4,96,256]{3,2,1,0:T(8,128)(2,1)S(1)}) custom-call(bf16[64,288,128]{2,1,0:T(8,128)(2,1)} %bitcast.25, bf16[4,576,128]{2,1,0:T(8,128)(2,1)} %bitcast.27, bf16[16,288,128]{2,1,0:T(8,128)(2,1)S(1)} %get-tuple-element.24.head_ref), custom_call_target="tpu_custom_call" | custom-call | flops 4000000000 | bytes 16000000 | tf_op jit(solution)/shard_map/pallas_call | solution.py:445
  9.9 0.0 collective-permute-done.refs_10_
  9.9 0.0 collective-permute-done.1.refs_11_
  9.9 0.0 collective-permute-done.2.refs_12_
  9.9 0.0 copy-done
  9.9 0.0 copy-done.1
  9.9 0.0 copy-done.2
  10.0 9.3 %shard_map.93 = (bf16[2,64,24,128]{3,2,1,0:T(8,128)(2,1)S(1)}, bf16[8,24,128]{2,1,0:T(8,128)(2,1)S(1)}, bf16[8,24,128]{2,1,0:T(8,128)(2,1)S(1)}, bf16[8,24,128]{...) custom-call(s32[4,64]{1,0:T(4,128)S(1)} %bitcast.17, ...), custom_call_target="tpu_custom_call", output_to_operand_aliasing={{0}: (9, {})} | custom-call | flops 10000000000 | bytes 16000000 | tf_op jit(solution)/shard_map/pallas_call | solution.py:469
  19.2 2.3 %collective-permute-start.3 = (bf16[8,24,128]{2,1,0:T(8,128)(2,1)S(1)}, bf16[8,24,128]{2,1,0:T(8,128)(2,1)S(1)}, u32[]{:S(2)}, u32[]{:S(2)}) collective-permute-start(bf16[8,24,128]{2,1,0:T(8,128)(2,1)S(1)} %get-tuple-element.35), channel_id=1, source_target_pairs={{0,3},{1,2},{2,1},{3,0},{4,7},{5,6},{6,5},{7,4},{8,11},{9,10},{10,... | collective-permute-start | bytes 147464 | tf_op jit(solution)/shard_map/ppermute | solution.py:466
  21.5 0.3 collective-permute-start.4
  21.8 0.2 collective-permute-start.5
  22.0 2.2 %collective-permute-start.6 = (bf16[8,24,128]{2,1,0:T(8,128)(2,1)S(1)}, bf16[8,24,128]{2,1,0:T(8,128)(2,1)S(1)}, u32[]{:S(2)}, u32[]{:S(2)}) collective-permute-start(bf16[8,24,128]{2,1,0:T(8,128)(2,1)S(1)} %get-tuple-element.39), channel_id=1, source_target_pairs={{0,4},{4,0},{8,12},{12,8},{16,20},{20,16},{24,28},{28,24},{1,5},{5... | collective-permute-start | bytes 147464 | tf_op jit(solution)/shard_map/ppermute | solution.py:393
  24.1 3.5 %collective-permute-start.7 = (bf16[8,24,128]{2,1,0:T(8,128)(2,1)S(1)}, bf16[8,24,128]{2,1,0:T(8,128)(2,1)S(1)}, u32[]{:S(2)}, u32[]{:S(2)}) collective-permute-start(bf16[8,24,128]{2,1,0:T(8,128)(2,1)S(1)} %get-tuple-element.40), channel_id=1, source_target_pairs={{4,8},{8,4},{12,16},{16,12},{20,24},{24,20},{5,9},{9,5},{13,17},{1... | collective-permute-start | bytes 147464 | tf_op jit(solution)/shard_map/ppermute | solution.py:393
  27.6 1.4 %shard_map.94.refs_6_ = f32[48,24,128]{2,1,0:T(8,128)S(1)} custom-call(s32[4,64]{1,0:T(4,128)S(1)} %bitcast.18, bf16[8,2,192,768]{3,2,1,0:T(8,128)(2,1)S(1)} %get-tuple-element.25.refs_6_.matrix_ref.refs_3_, bf16[2,64,24,128]{3,2,1,0:T(8,128)(2,1)S(1)} %get-tuple-element.34.state_ref), custom_call_target="tpu_custom_call" | custom-call | flops 1000000000 | bytes 8000000 | tf_op jit(solution)/shard_map/pallas_call | solution.py:487
  29.0 0.0 collective-permute-done.3.refs_7_
  29.1 0.0 collective-permute-done.4.refs_8_
  29.1 0.0 collective-permute-done.5.refs_9_
  29.1 0.0 collective-permute-done.6.refs_11_
  29.1 0.4 %collective-permute-done.7.refs_12_ = bf16[8,24,128]{2,1,0:T(8,128)(2,1)S(1)} collective-permute-done((bf16[8,24,128]{2,1,0:T(8,128)(2,1)S(1)}, bf16[8,24,128]{2,1,0:T(8,128)(2,1)S(1)}, u32[]{:S(2)}, u32[]{:S(2)}) %collective-permute-start.7) | collective-permute-done | bytes 49184 | tf_op jit(solution)/shard_map/ppermute | solution.py:393
  29.5 9.1 %shard_map.95 = f32[24,6144]{1,0:T(8,128)} custom-call(s32[4,64]{1,0:T(4,128)S(1)} %bitcast.19, s32[4,8]{1,0:T(4,128)S(1)} %bitcast.23, f32[48,8,128]{2,1,0:T(8,128)S(1)} %get-tuple-element.23.refs_5_.refs_2_, bf16[8,2,192,768]{3,2,1,0:T(8,128)(2,1)S(1)} %get-tuple-element.25.refs_6_.matrix_ref.refs_3_, ...), custom_call_target="tpu_custom_call" | custom-call | flops 10000000000 | bytes 16000000 | tf_op jit(solution)/shard_map/pallas_call | solution.py:495
  (5 shorter events, 0.0 us)
Async XLA Ops:
  1.4 8.4 %collective-permute-start = (bf16[8,24,128]{2,1,0:T(8,128)(2,1)S(1)}, bf16[8,24,128]{2,1,0:T(8,128)(2,1)S(1)}, u32[]{:S(2)}, u32[]{:S(2)}) collective-permute-start(bf16[8,24,128]{2,1,0:T(8,128)(2,1)S(1)} %get-tuple-element.30), channel_id=1, source_target_pairs={{0,3},{1,2},{2,1},{3,0},{4,7},{5,6},{6,5},{7,4},{8,11},{9,10},{10,... | collective-permute-start | bytes 147464 | tf_op jit(solution)/shard_map/ppermute | solution.py:466
  4.5 5.4 %collective-permute-start.1 = (bf16[8,24,128]{2,1,0:T(8,128)(2,1)S(1)}, bf16[8,24,128]{2,1,0:T(8,128)(2,1)S(1)}, u32[]{:S(2)}, u32[]{:S(2)}) collective-permute-start(bf16[8,24,128]{2,1,0:T(8,128)(2,1)S(1)} %get-tuple-element.31), channel_id=1, source_target_pairs={{0,1},{1,0},{2,3},{3,2},{4,5},{5,4},{6,7},{7,6},{8,9},{9,8},{10,11... | collective-permute-start | bytes 147464 | tf_op jit(solution)/shard_map/ppermute | solution.py:466
  4.8 5.2 %collective-permute-start.2 = (bf16[8,24,128]{2,1,0:T(8,128)(2,1)S(1)}, bf16[8,24,128]{2,1,0:T(8,128)(2,1)S(1)}, u32[]{:S(2)}, u32[]{:S(2)}) collective-permute-start(bf16[8,24,128]{2,1,0:T(8,128)(2,1)S(1)} %get-tuple-element.32), channel_id=1, source_target_pairs={{0,2},{1,3},{2,0},{3,1},{4,6},{5,7},{6,4},{7,5},{8,10},{9,11},{10,... | collective-permute-start | bytes 147464 | tf_op jit(solution)/shard_map/ppermute | solution.py:466
  4.9 5.1 %copy-start = (s32[1,1,4,8]{3,2,1,0:T(4,128)S(1)}, s32[1,1,4,8]{3,2,1,0:T(4,128)}, u32[]{:S(2)}) copy-start(s32[1,1,4,8]{3,2,1,0:T(4,128)} %param.14) | copy-start | bytes 388
  4.9 5.1 %copy-start.1 = (s32[64,4]{0,1:T(4,128)S(1)}, s32[64,4]{0,1:T(4,128)}, u32[]{:S(2)}) copy-start(s32[64,4]{0,1:T(4,128)} %param.11) | copy-start | bytes 3076
  4.9 5.1 %copy-start.2 = (s32[1,1,4]{2,1,0:T(1,128)S(1)}, s32[1,1,4]{2,1,0:T(1,128)}, u32[]{:S(2)}) copy-start(s32[1,1,4]{2,1,0:T(1,128)} %param.15) | copy-start | bytes 52
  4.9 5.1 %copy-start.3 = (s32[1,1,4,8]{3,2,1,0:T(4,128)S(1)}, s32[1,1,4,8]{3,2,1,0:T(4,128)}, u32[]{:S(2)}) copy-start(s32[1,1,4,8]{3,2,1,0:T(4,128)} %param.16) | copy-start | bytes 388
  19.2 9.8 %collective-permute-start.3 = (bf16[8,24,128]{2,1,0:T(8,128)(2,1)S(1)}, bf16[8,24,128]{2,1,0:T(8,128)(2,1)S(1)}, u32[]{:S(2)}, u32[]{:S(2)}) collective-permute-start(bf16[8,24,128]{2,1,0:T(8,128)(2,1)S(1)} %get-tuple-element.35), channel_id=1, source_target_pairs={{0,3},{1,2},{2,1},{3,0},{4,7},{5,6},{6,5},{7,4},{8,11},{9,10},{10,... | collective-permute-start | bytes 147464 | tf_op jit(solution)/shard_map/ppermute | solution.py:466
  21.5 7.5 %collective-permute-start.4 = (bf16[8,24,128]{2,1,0:T(8,128)(2,1)S(1)}, bf16[8,24,128]{2,1,0:T(8,128)(2,1)S(1)}, u32[]{:S(2)}, u32[]{:S(2)}) collective-permute-start(bf16[8,24,128]{2,1,0:T(8,128)(2,1)S(1)} %get-tuple-element.36), channel_id=1, source_target_pairs={{0,1},{1,0},{2,3},{3,2},{4,5},{5,4},{6,7},{7,6},{8,9},{9,8},{10,11... | collective-permute-start | bytes 147464 | tf_op jit(solution)/shard_map/ppermute | solution.py:466
  21.8 7.3 %collective-permute-start.5 = (bf16[8,24,128]{2,1,0:T(8,128)(2,1)S(1)}, bf16[8,24,128]{2,1,0:T(8,128)(2,1)S(1)}, u32[]{:S(2)}, u32[]{:S(2)}) collective-permute-start(bf16[8,24,128]{2,1,0:T(8,128)(2,1)S(1)} %get-tuple-element.37), channel_id=1, source_target_pairs={{0,2},{1,3},{2,0},{3,1},{4,6},{5,7},{6,4},{7,5},{8,10},{9,11},{10,... | collective-permute-start | bytes 147464 | tf_op jit(solution)/shard_map/ppermute | solution.py:466
  22.0 7.1 %collective-permute-start.6 = (bf16[8,24,128]{2,1,0:T(8,128)(2,1)S(1)}, bf16[8,24,128]{2,1,0:T(8,128)(2,1)S(1)}, u32[]{:S(2)}, u32[]{:S(2)}) collective-permute-start(bf16[8,24,128]{2,1,0:T(8,128)(2,1)S(1)} %get-tuple-element.39), channel_id=1, source_target_pairs={{0,4},{4,0},{8,12},{12,8},{16,20},{20,16},{24,28},{28,24},{1,5},{5... | collective-permute-start | bytes 147464 | tf_op jit(solution)/shard_map/ppermute | solution.py:393
  24.1 5.4 %collective-permute-start.7 = (bf16[8,24,128]{2,1,0:T(8,128)(2,1)S(1)}, bf16[8,24,128]{2,1,0:T(8,128)(2,1)S(1)}, u32[]{:S(2)}, u32[]{:S(2)}) collective-permute-start(bf16[8,24,128]{2,1,0:T(8,128)(2,1)S(1)} %get-tuple-element.40), channel_id=1, source_target_pairs={{4,8},{8,4},{12,16},{16,12},{20,24},{24,20},{5,9},{9,5},{13,17},{1... | collective-permute-start | bytes 147464 | tf_op jit(solution)/shard_map/ppermute | solution.py:393

commit v8 on v7

--- a/solution.py
+++ b/solution.py
@@ -24,6 +24,7 @@
 VMEM_LIMIT = 30 * 2**20
 STAGES = (16, 16, 16, 16)
 PIECE = 8
+OUT_PIECES = 4
 CHUNK = 4
 
 VMEM = pl.BlockSpec(memory_space=pltpu.VMEM)
@@ -156,13 +157,15 @@
     return ((at == want_low) | (at == want_high)).astype(jnp.float32).astype(jnp.bfloat16)
 
 
-def stack(select, rows, group):
+def stack(select, first, second, group):
     depth = 8 * TILES * group
-    wide = jnp.concatenate([rows[g * depth : (g + 1) * depth] for g in range(3)], axis=1)
+    parts = [rows[g * depth : (g + 1) * depth] for rows in (first, second) for g in range(3)]
+    wide = jnp.concatenate(parts, axis=1)
     high = iota(wide.shape, 1) % LANES >= 64
     zero = jnp.zeros_like(wide)
     both = jnp.concatenate([jnp.where(high, zero, wide), jnp.where(high, wide, zero)], axis=0)
-    return jnp.dot(select, both, preferred_element_type=jnp.float32).astype(jnp.bfloat16)
+    picked = jnp.dot(select, both, preferred_element_type=jnp.float32).astype(jnp.bfloat16)
+    return picked[:, : 3 * LANES], picked[:, 3 * LANES :]
 
 
 def unstack(picked, member):
@@ -208,7 +211,11 @@
         waits, items = task
         for one in waits:
             one.wait()
-        return [(rows, n, size, stack(pick, rows[n], size)) for pick, rows, n, size in items]
+        results = []
+        for (pick, rows, n, size), (*_, other, _) in zip(items[::2], items[1::2]):
+            pair = stack(pick, rows[n], rows[other], size)
+            results += [(rows, n, size, pair[0]), (rows, other, size, pair[1])]
+        return results
 
     def store(results, held_ref):
         for at, (rows, _, size, picked) in enumerate(results):
@@ -362,7 +369,7 @@
     cols_ref, target_ref, scale_ref, matrix_ref, face_ref, source_ref, image_ref = refs[:7]
     received_refs = refs[7 : 7 + peers]
     swap_in_ref, swap_out_ref = refs[7 + peers : 9 + peers]
-    out_ref, forcing_ref, extra_ref, state_ref, other_ref = refs[9 + peers :]
+    out_hbm, forcing_ref, extra_ref, state_ref, other_ref, out_ref, sems = refs[9 + peers :]
     inner, outer = end_blocks()
     extra_ref[...] = jnp.zeros_like(extra_ref)
     extra_ref[0, pl.ds(inner, NI)] = swap_in_ref[...].astype(jnp.float32)
@@ -379,10 +386,22 @@
         return carry
 
     lax.fori_loop(0, ITERS // 2 - 1, two, 0)
-    for group in range(NB // (2 * QUAD)):
+    groups = NB // (2 * QUAD)
+    width = 2 * groups // OUT_PIECES * TILES * LANES
+    leaving = []
+    for group in range(groups):
         for i, part in enumerate(images_of(cols_ref, matrix_ref, state_ref, group)):
             at = group * 2 * TILES + i
             out_ref[:, at * LANES : (at + 1) * LANES] = step_tile(forcing_ref, scale_ref, part, at)
+        if (group + 1) % (groups // OUT_PIECES) == 0:
+            piece = len(leaving)
+            columns = pl.ds(piece * width, width)
+            leaving.append(
+                pltpu.make_async_copy(out_ref.at[:, columns], out_hbm.at[:, columns], sems.at[piece])
+            )
+            leaving[-1].start()
+    for one in leaving:
+        one.wait()
 
 
 def swapped(x, axis, first):
@@ -496,12 +515,14 @@
         functools.partial(last_tick_kernel, peers),
         out_shape=shape((COLS, NB * BS), f32),
         in_specs=[SMEM] * 2 + [VMEM] * (7 + peers),
-        out_specs=VMEM,
+        out_specs=HBM,
         scratch_shapes=[
             pltpu.VMEM(tile_shape, f32),
             pltpu.VMEM((2,) + block_shape, f32),
             pltpu.VMEM(state_shape, bf16),
             pltpu.VMEM(state_shape, bf16),
+            pltpu.VMEM((COLS, NB * BS), f32),
+            pltpu.SemaphoreType.DMA((OUT_PIECES,)),
         ],
         compiler_params=params(),
         cost_estimate=cost(10**10, 16 * 10**6),

time: 38.8 us -> 38 us (0.979)
  Pallas kernels: 26.2 us -> 25.4 us
    pallas_call x1, Pallas kernels: 5 us -> 4.46 us  [shards(): pl.pallas_call(functools.partial(spread_kernel, peers), out_shape=(shape(...]
  transfers between devices with their start and end apart: 8 -> 8, of which waited for: 1 -> 1; matrix products, arithmetic and copies ran while one was open for 0% -> 0% of each run, Pallas kernels for 17% -> 16%
where the time goes in v8:
time: 38 us; the launch traced here: 37.8 us
  Pallas kernels  25.4 us (67%)
  starting transfers between devices  11.8 us (31%)
  waiting for transfers between devices  0.42 us (1%)
    pallas_call x1, Pallas kernels, shards(): pl.pallas_call(functools.partial(first_tick_kernel, peers), out_shape=(sh...  9.19 us
    pallas_call x1, Pallas kernels, shards(): pl.pallas_call(functools.partial(last_tick_kernel, peers), out_shape=shap...  8.9 us
    ppermute x6, starting transfers between devices, exchange(): lax.ppermute(sent[i], 'patch', pairs[i])  6.14 us
    ppermute x2, starting transfers between devices, swapped(): return lax.ppermute(x, axis, pairs)  5.65 us
    pallas_call x1, Pallas kernels, shards(): pl.pallas_call(functools.partial(spread_kernel, peers), out_shape=(shape(...  4.46 us
    pallas_call x1, Pallas kernels, shards(): pl.pallas_call(first_image_kernel, out_shape=shape(tile_shape, f32), in_s...  1.45 us
    pallas_call x1, Pallas kernels, shards(): pl.pallas_call(functools.partial(prep_kernel, peers), out_shape=(shape(st...  1.44 us
  transfers between devices with their start and end apart: 8, of which 1 were waited for; matrix products, arithmetic and copies ran while one was open for 0% of the time, Pallas kernels for 16%

profile of v8, /device:TPU:1, one launch (start us, length us, event | category | flops | bytes accessed | tf_op | source)
XLA Modules:
  0.0 37.8 jit_solution(15397818204837684520)
XLA Ops:
  0.0 1.4 %shard_map.91 = (bf16[2,64,24,128]{3,2,1,0:T(8,128)(2,1)S(1)}, f32[4,16,128]{2,1,0:T(8,128)S(1)}, bf16[48,24,128]{2,1,0:T(8,128)(2,1)S(1)}, f32[48,8,128]{2,1,0:...) custom-call(s32[4,8]{1,0:T(4,128)} %bitcast.15, ...), custom_call_target="tpu_custom_call" | custom-call | flops 1000000 | bytes 1000000 | tf_op jit(solution)/shard_map/pallas_call | solution.py:440
  1.4 3.1 %collective-permute-start = (bf16[8,24,128]{2,1,0:T(8,128)(2,1)S(1)}, bf16[8,24,128]{2,1,0:T(8,128)(2,1)S(1)}, u32[]{:S(2)}, u32[]{:S(2)}) collective-permute-start(bf16[8,24,128]{2,1,0:T(8,128)(2,1)S(1)} %get-tuple-element.30), channel_id=1, source_target_pairs={{0,3},{1,2},{2,1},{3,0},{4,7},{5,6},{6,5},{7,4},{8,11},{9,10},{10,... | collective-permute-start | bytes 147464 | tf_op jit(solution)/shard_map/ppermute | solution.py:485
  4.5 0.3 collective-permute-start.1
  4.8 0.1 collective-permute-start.2
  4.9 4.5 %shard_map.92 = (bf16[8,2,192,768]{3,2,1,0:T(8,128)(2,1)S(1)}, bf16[4,4,96,256]{3,2,1,0:T(8,128)(2,1)S(1)}) custom-call(bf16[64,288,128]{2,1,0:T(8,128)(2,1)} %bitcast.25, bf16[4,576,128]{2,1,0:T(8,128)(2,1)} %bitcast.27, bf16[16,288,128]{2,1,0:T(8,128)(2,1)S(1)} %get-tuple-element.24.head_ref), custom_call_target="tpu_custom_call" | custom-call | flops 4000000000 | bytes 16000000 | tf_op jit(solution)/shard_map/pallas_call | solution.py:464
  9.4 0.0 collective-permute-done.refs_10_
  9.4 0.0 collective-permute-done.1.refs_11_
  9.4 0.0 collective-permute-done.2.refs_12_
  9.4 0.0 copy-done
  9.4 0.0 copy-done.1
  9.4 0.0 copy-done.2
  9.4 9.2 %shard_map.93 = (bf16[2,64,24,128]{3,2,1,0:T(8,128)(2,1)S(1)}, bf16[8,24,128]{2,1,0:T(8,128)(2,1)S(1)}, bf16[8,24,128]{2,1,0:T(8,128)(2,1)S(1)}, bf16[8,24,128]{...) custom-call(s32[4,64]{1,0:T(4,128)S(1)} %bitcast.17, ...), custom_call_target="tpu_custom_call", output_to_operand_aliasing={{0}: (9, {})} | custom-call | flops 10000000000 | bytes 16000000 | tf_op jit(solution)/shard_map/pallas_call | solution.py:488
  18.6 2.4 %collective-permute-start.3 = (bf16[8,24,128]{2,1,0:T(8,128)(2,1)S(1)}, bf16[8,24,128]{2,1,0:T(8,128)(2,1)S(1)}, u32[]{:S(2)}, u32[]{:S(2)}) collective-permute-start(bf16[8,24,128]{2,1,0:T(8,128)(2,1)S(1)} %get-tuple-element.35), channel_id=1, source_target_pairs={{0,3},{1,2},{2,1},{3,0},{4,7},{5,6},{6,5},{7,4},{8,11},{9,10},{10,... | collective-permute-start | bytes 147464 | tf_op jit(solution)/shard_map/ppermute | solution.py:485
  21.0 0.3 collective-permute-start.4
  21.3 0.0 collective-permute-start.5
  21.3 2.2 %collective-permute-start.6 = (bf16[8,24,128]{2,1,0:T(8,128)(2,1)S(1)}, bf16[8,24,128]{2,1,0:T(8,128)(2,1)S(1)}, u32[]{:S(2)}, u32[]{:S(2)}) collective-permute-start(bf16[8,24,128]{2,1,0:T(8,128)(2,1)S(1)} %get-tuple-element.39), channel_id=1, source_target_pairs={{0,4},{4,0},{8,12},{12,8},{16,20},{20,16},{24,28},{28,24},{1,5},{5... | collective-permute-start | bytes 147464 | tf_op jit(solution)/shard_map/ppermute | solution.py:412
  23.5 3.5 %collective-permute-start.7 = (bf16[8,24,128]{2,1,0:T(8,128)(2,1)S(1)}, bf16[8,24,128]{2,1,0:T(8,128)(2,1)S(1)}, u32[]{:S(2)}, u32[]{:S(2)}) collective-permute-start(bf16[8,24,128]{2,1,0:T(8,128)(2,1)S(1)} %get-tuple-element.40), channel_id=1, source_target_pairs={{4,8},{8,4},{12,16},{16,12},{20,24},{24,20},{5,9},{9,5},{13,17},{1... | collective-permute-start | bytes 147464 | tf_op jit(solution)/shard_map/ppermute | solution.py:412
  27.0 1.5 %shard_map.94.refs_6_ = f32[48,24,128]{2,1,0:T(8,128)S(1)} custom-call(s32[4,64]{1,0:T(4,128)S(1)} %bitcast.18, bf16[8,2,192,768]{3,2,1,0:T(8,128)(2,1)S(1)} %get-tuple-element.25.refs_6_.matrix_ref.refs_3_, bf16[2,64,24,128]{3,2,1,0:T(8,128)(2,1)S(1)} %get-tuple-element.34.state_ref), custom_call_target="tpu_custom_call" | custom-call | flops 1000000000 | bytes 8000000 | tf_op jit(solution)/shard_map/pallas_call | solution.py:506
  28.5 0.0 collective-permute-done.3.refs_7_
  28.5 0.0 collective-permute-done.4.refs_8_
  28.5 0.0 collective-permute-done.5.refs_9_
  28.5 0.0 collective-permute-done.6.refs_11_
  28.5 0.4 %collective-permute-done.7.refs_12_ = bf16[8,24,128]{2,1,0:T(8,128)(2,1)S(1)} collective-permute-done((bf16[8,24,128]{2,1,0:T(8,128)(2,1)S(1)}, bf16[8,24,128]{2,1,0:T(8,128)(2,1)S(1)}, u32[]{:S(2)}, u32[]{:S(2)}) %collective-permute-start.7) | collective-permute-done | bytes 49184 | tf_op jit(solution)/shard_map/ppermute | solution.py:412
  28.9 8.9 %shard_map.95 = f32[24,6144]{1,0:T(8,128)} custom-call(s32[4,64]{1,0:T(4,128)S(1)} %bitcast.19, s32[4,8]{1,0:T(4,128)S(1)} %bitcast.23, f32[48,8,128]{2,1,0:T(8,128)S(1)} %get-tuple-element.23.refs_5_.refs_2_, bf16[8,2,192,768]{3,2,1,0:T(8,128)(2,1)S(1)} %get-tuple-element.25.refs_6_.matrix_ref.refs_3_, ...), custom_call_target="tpu_custom_call" | custom-call | flops 10000000000 | bytes 16000000 | tf_op jit(solution)/shard_map/pallas_call | solution.py:514
  (5 shorter events, 0.0 us)
Async XLA Ops:
  1.4 7.9 %collective-permute-start = (bf16[8,24,128]{2,1,0:T(8,128)(2,1)S(1)}, bf16[8,24,128]{2,1,0:T(8,128)(2,1)S(1)}, u32[]{:S(2)}, u32[]{:S(2)}) collective-permute-start(bf16[8,24,128]{2,1,0:T(8,128)(2,1)S(1)} %get-tuple-element.30), channel_id=1, source_target_pairs={{0,3},{1,2},{2,1},{3,0},{4,7},{5,6},{6,5},{7,4},{8,11},{9,10},{10,... | collective-permute-start | bytes 147464 | tf_op jit(solution)/shard_map/ppermute | solution.py:485
  4.5 4.9 %collective-permute-start.1 = (bf16[8,24,128]{2,1,0:T(8,128)(2,1)S(1)}, bf16[8,24,128]{2,1,0:T(8,128)(2,1)S(1)}, u32[]{:S(2)}, u32[]{:S(2)}) collective-permute-start(bf16[8,24,128]{2,1,0:T(8,128)(2,1)S(1)} %get-tuple-element.31), channel_id=1, source_target_pairs={{0,1},{1,0},{2,3},{3,2},{4,5},{5,4},{6,7},{7,6},{8,9},{9,8},{10,11... | collective-permute-start | bytes 147464 | tf_op jit(solution)/shard_map/ppermute | solution.py:485
  4.8 4.6 %collective-permute-start.2 = (bf16[8,24,128]{2,1,0:T(8,128)(2,1)S(1)}, bf16[8,24,128]{2,1,0:T(8,128)(2,1)S(1)}, u32[]{:S(2)}, u32[]{:S(2)}) collective-permute-start(bf16[8,24,128]{2,1,0:T(8,128)(2,1)S(1)} %get-tuple-element.32), channel_id=1, source_target_pairs={{0,2},{1,3},{2,0},{3,1},{4,6},{5,7},{6,4},{7,5},{8,10},{9,11},{10,... | collective-permute-start | bytes 147464 | tf_op jit(solution)/shard_map/ppermute | solution.py:485
  4.9 4.5 %copy-start = (s32[1,1,4,8]{3,2,1,0:T(4,128)S(1)}, s32[1,1,4,8]{3,2,1,0:T(4,128)}, u32[]{:S(2)}) copy-start(s32[1,1,4,8]{3,2,1,0:T(4,128)} %param.14) | copy-start | bytes 388
  4.9 4.5 %copy-start.1 = (s32[64,4]{0,1:T(4,128)S(1)}, s32[64,4]{0,1:T(4,128)}, u32[]{:S(2)}) copy-start(s32[64,4]{0,1:T(4,128)} %param.11) | copy-start | bytes 3076
  4.9 4.5 %copy-start.2 = (s32[1,1,4]{2,1,0:T(1,128)S(1)}, s32[1,1,4]{2,1,0:T(1,128)}, u32[]{:S(2)}) copy-start(s32[1,1,4]{2,1,0:T(1,128)} %param.15) | copy-start | bytes 52
  4.9 4.5 %copy-start.3 = (s32[1,1,4,8]{3,2,1,0:T(4,128)S(1)}, s32[1,1,4,8]{3,2,1,0:T(4,128)}, u32[]{:S(2)}) copy-start(s32[1,1,4,8]{3,2,1,0:T(4,128)} %param.16) | copy-start | bytes 388
  18.6 9.8 %collective-permute-start.3 = (bf16[8,24,128]{2,1,0:T(8,128)(2,1)S(1)}, bf16[8,24,128]{2,1,0:T(8,128)(2,1)S(1)}, u32[]{:S(2)}, u32[]{:S(2)}) collective-permute-start(bf16[8,24,128]{2,1,0:T(8,128)(2,1)S(1)} %get-tuple-element.35), channel_id=1, source_target_pairs={{0,3},{1,2},{2,1},{3,0},{4,7},{5,6},{6,5},{7,4},{8,11},{9,10},{10,... | collective-permute-start | bytes 147464 | tf_op jit(solution)/shard_map/ppermute | solution.py:485
  21.0 7.5 %collective-permute-start.4 = (bf16[8,24,128]{2,1,0:T(8,128)(2,1)S(1)}, bf16[8,24,128]{2,1,0:T(8,128)(2,1)S(1)}, u32[]{:S(2)}, u32[]{:S(2)}) collective-permute-start(bf16[8,24,128]{2,1,0:T(8,128)(2,1)S(1)} %get-tuple-element.36), channel_id=1, source_target_pairs={{0,1},{1,0},{2,3},{3,2},{4,5},{5,4},{6,7},{7,6},{8,9},{9,8},{10,11... | collective-permute-start | bytes 147464 | tf_op jit(solution)/shard_map/ppermute | solution.py:485
  21.3 7.2 %collective-permute-start.5 = (bf16[8,24,128]{2,1,0:T(8,128)(2,1)S(1)}, bf16[8,24,128]{2,1,0:T(8,128)(2,1)S(1)}, u32[]{:S(2)}, u32[]{:S(2)}) collective-permute-start(bf16[8,24,128]{2,1,0:T(8,128)(2,1)S(1)} %get-tuple-element.37), channel_id=1, source_target_pairs={{0,2},{1,3},{2,0},{3,1},{4,6},{5,7},{6,4},{7,5},{8,10},{9,11},{10,... | collective-permute-start | bytes 147464 | tf_op jit(solution)/shard_map/ppermute | solution.py:485
  21.3 7.2 %collective-permute-start.6 = (bf16[8,24,128]{2,1,0:T(8,128)(2,1)S(1)}, bf16[8,24,128]{2,1,0:T(8,128)(2,1)S(1)}, u32[]{:S(2)}, u32[]{:S(2)}) collective-permute-start(bf16[8,24,128]{2,1,0:T(8,128)(2,1)S(1)} %get-tuple-element.39), channel_id=1, source_target_pairs={{0,4},{4,0},{8,12},{12,8},{16,20},{20,16},{24,28},{28,24},{1,5},{5... | collective-permute-start | bytes 147464 | tf_op jit(solution)/shard_map/ppermute | solution.py:412
  23.5 5.4 %collective-permute-start.7 = (bf16[8,24,128]{2,1,0:T(8,128)(2,1)S(1)}, bf16[8,24,128]{2,1,0:T(8,128)(2,1)S(1)}, u32[]{:S(2)}, u32[]{:S(2)}) collective-permute-start(bf16[8,24,128]{2,1,0:T(8,128)(2,1)S(1)} %get-tuple-element.40), channel_id=1, source_target_pairs={{4,8},{8,4},{12,16},{16,12},{20,24},{24,20},{5,9},{9,5},{13,17},{1... | collective-permute-start | bytes 147464 | tf_op jit(solution)/shard_map/ppermute | solution.py:412

commit v9 on v8

--- a/solution.py
+++ b/solution.py
@@ -359,26 +359,44 @@
     write_sent(peers, send_ref, count_ref, sign_ref, state_ref, sent_refs)
 
 
-def first_image_kernel(cols_ref, matrix_ref, state_ref, image_ref):
-    for group in range(NB // (2 * QUAD)):
-        for i, part in enumerate(images_of(cols_ref, matrix_ref, state_ref, group)):
-            image_ref[group * 2 * TILES + i] = part
-
-
-def last_tick_kernel(peers, *refs):
-    cols_ref, target_ref, scale_ref, matrix_ref, face_ref, source_ref, image_ref = refs[:7]
-    received_refs = refs[7 : 7 + peers]
-    swap_in_ref, swap_out_ref = refs[7 + peers : 9 + peers]
-    out_hbm, forcing_ref, extra_ref, state_ref, other_ref, out_ref, sems = refs[9 + peers :]
-    inner, outer = end_blocks()
+def first_step_kernel(peers, *refs):
+    cols_ref, target_ref, scale_ref, matrix_ref, face_ref, source_ref, start_ref = refs[:7]
+    received_refs, swap_in_ref = refs[7 : 7 + peers], refs[7 + peers]
+    forcing_ref, state_ref, end_ref, extra_ref = refs[8 + peers :]
+    inner, _ = end_blocks()
     extra_ref[...] = jnp.zeros_like(extra_ref)
     extra_ref[0, pl.ds(inner, NI)] = swap_in_ref[...].astype(jnp.float32)
-    extra_ref[0, pl.ds(outer, NI)] = swap_out_ref[...].astype(jnp.float32)
     add_faces(peers, target_ref, received_refs, face_ref, extra_ref)
     set_forcing(source_ref, scale_ref, extra_ref, forcing_ref)
-    for q in range(NB // QUAD):
-        tiles = range(q * TILES, (q + 1) * TILES)
-        store_quad(state_ref, q, [step_tile(forcing_ref, scale_ref, image_ref[i], i) for i in tiles])
+    groups = NB // (2 * QUAD)
+    for group in range(groups):
+        parts = images_of(cols_ref, matrix_ref, start_ref, group)
+        tiles = [
+            step_tile(forcing_ref, scale_ref, part, group * 2 * TILES + i)
+            for i, part in enumerate(parts)
+        ]
+        for side in range(2):
+            store_quad(state_ref, group * 2 + side, tiles[side * TILES : (side + 1) * TILES])
+        if group in (0, groups - 1):
+            for i, tile in enumerate(tiles):
+                end_ref[group // (groups - 1), i] = tile
+
+
+def last_tick_kernel(*refs):
+    cols_ref, scale_ref, matrix_ref, end_ref, swap_out_ref = refs[:5]
+    out_hbm, forcing_ref, state_ref, other_ref, out_ref, sems = refs[7:]
+    odd = lax.rem(lax.axis_index("sec"), 2)
+    for side in range(2):
+        blocks = range(side * QUAD, (side + 1) * QUAD)
+        arrived = join_quad([swap_out_ref[n].astype(jnp.float32) for n in blocks])
+        stepped = []
+        for u, tile in enumerate(arrived):
+            i = side * TILES + u
+            at = odd * ((NB - NI) * BS // LANES) + i
+            kept = jnp.where(tall(scale_ref[at]) > 0, tile, 0.0)
+            forcing_ref[at] = forcing_ref[at] + kept
+            stepped.append(end_ref[odd, i] + kept)
+        store_quad(state_ref, odd * ((NB - NI) // QUAD) + side, stepped)
 
     def two(i, carry):
         sweep(cols_ref, scale_ref, matrix_ref, forcing_ref, state_ref, other_ref)
@@ -503,30 +521,34 @@
     received = exchange(sent)
     swap_in = swapped(swap_in, "sec", 0)
     swap_out = swapped(swap_out, "sec", 1)
-    image = pl.pallas_call(
-        first_image_kernel,
-        out_shape=shape(tile_shape, f32),
-        in_specs=[SMEM] + [VMEM] * 2,
-        out_specs=VMEM,
+    forcing, state, end = pl.pallas_call(
+        functools.partial(first_step_kernel, peers),
+        out_shape=(
+            shape(tile_shape, f32),
+            shape(state_shape, bf16),
+            shape((2, 2 * TILES, COLS, LANES), f32),
+        ),
+        in_specs=[SMEM] * 2 + [VMEM] * (6 + peers),
+        out_specs=[VMEM] * 3,
+        scratch_shapes=[pltpu.VMEM((2,) + block_shape, f32)],
         compiler_params=params(),
         cost_estimate=cost(10**9, 8 * 10**6),
-    )(cols, matrices, state)
-    return pl.pallas_call(
-        functools.partial(last_tick_kernel, peers),
-        out_shape=shape((COLS, NB * BS), f32),
-        in_specs=[SMEM] * 2 + [VMEM] * (7 + peers),
-        out_specs=HBM,
+    )(cols, targets, scale, matrices, faces, source, state, *received, swap_in)
+    out, _, _ = pl.pallas_call(
+        last_tick_kernel,
+        out_shape=(shape((COLS, NB * BS), f32), shape(tile_shape, f32), shape(state_shape, bf16)),
+        in_specs=[SMEM] + [VMEM] * 6,
+        out_specs=[HBM] + [VMEM] * 2,
         scratch_shapes=[
-            pltpu.VMEM(tile_shape, f32),
-            pltpu.VMEM((2,) + block_shape, f32),
-            pltpu.VMEM(state_shape, bf16),
             pltpu.VMEM(state_shape, bf16),
             pltpu.VMEM((COLS, NB * BS), f32),
             pltpu.SemaphoreType.DMA((OUT_PIECES,)),
         ],
+        input_output_aliases={5: 1, 6: 2},
         compiler_params=params(),
         cost_estimate=cost(10**10, 16 * 10**6),
-    )(cols, targets, scale, matrices, faces, source, image, *received, swap_in, swap_out)
+    )(cols, scale, matrices, end, swap_out, forcing, state)
+    return out
 
 
 def solution(mesh):

time: 38 us -> 38 us (level); the launches traced: 37.8 us -> 37.2 us
  waiting for transfers between devices: 0.42 us -> 0.02 us
    ppermute x2, waiting for transfers between devices: 0.4 us -> 0.01 us  [swapped(): return lax.ppermute(x, axis, pairs)]
  transfers between devices with their start and end apart: 8 -> 8, of which waited for: 1 -> 0; matrix products, arithmetic and copies ran while one was open for 0% -> 0% of each run, Pallas kernels for 16% -> 17%
where the time goes in v9:
time: 38 us; the launch traced here: 37.2 us
  Pallas kernels  25.5 us (67%)
  starting transfers between devices  11.6 us (31%)
    pallas_call x1, Pallas kernels, shards(): pl.pallas_call(functools.partial(first_tick_kernel, peers), out_shape=(sh...  9.35 us
    pallas_call x1, Pallas kernels, shards(): pl.pallas_call(last_tick_kernel, out_shape=(shape((COLS, NB * BS), f32),...  8.26 us
    ppermute x6, starting transfers between devices, exchange(): lax.ppermute(sent[i], 'patch', pairs[i])  6.14 us
    ppermute x2, starting transfers between devices, swapped(): return lax.ppermute(x, axis, pairs)  5.44 us
    pallas_call x1, Pallas kernels, shards(): pl.pallas_call(functools.partial(spread_kernel, peers), out_shape=(shape(...  4.46 us
    pallas_call x1, Pallas kernels, shards(): pl.pallas_call(functools.partial(first_step_kernel, peers), out_shape=(sh...  1.96 us
    pallas_call x1, Pallas kernels, shards(): pl.pallas_call(functools.partial(prep_kernel, peers), out_shape=(shape(st...  1.44 us
  transfers between devices with their start and end apart: 8, of which 0 were waited for; matrix products, arithmetic and copies ran while one was open for 0% of the time, Pallas kernels for 17%

profile of v9, /device:TPU:1, one launch (start us, length us, event | category | flops | bytes accessed | tf_op | source)
XLA Modules:
  0.0 37.2 jit_solution(6965371053680625593)
XLA Ops:
  0.0 1.4 %shard_map.91 = (bf16[2,64,24,128]{3,2,1,0:T(8,128)(2,1)S(1)}, f32[4,16,128]{2,1,0:T(8,128)S(1)}, bf16[48,24,128]{2,1,0:T(8,128)(2,1)S(1)}, f32[48,8,128]{2,1,0:...) custom-call(s32[4,8]{1,0:T(4,128)} %bitcast.15, ...), custom_call_target="tpu_custom_call" | custom-call | flops 1000000 | bytes 1000000 | tf_op jit(solution)/shard_map/pallas_call | solution.py:458
  1.4 3.1 %collective-permute-start = (bf16[8,24,128]{2,1,0:T(8,128)(2,1)S(1)}, bf16[8,24,128]{2,1,0:T(8,128)(2,1)S(1)}, u32[]{:S(2)}, u32[]{:S(2)}) collective-permute-start(bf16[8,24,128]{2,1,0:T(8,128)(2,1)S(1)} %get-tuple-element.34), channel_id=1, source_target_pairs={{0,3},{1,2},{2,1},{3,0},{4,7},{5,6},{6,5},{7,4},{8,11},{9,10},{10,... | collective-permute-start | bytes 147464 | tf_op jit(solution)/shard_map/ppermute | solution.py:503
  4.5 0.3 collective-permute-start.1
  4.8 0.1 collective-permute-start.2
  4.9 4.5 %shard_map.92 = (bf16[8,2,192,768]{3,2,1,0:T(8,128)(2,1)S(1)}, bf16[4,4,96,256]{3,2,1,0:T(8,128)(2,1)S(1)}) custom-call(bf16[64,288,128]{2,1,0:T(8,128)(2,1)} %bitcast.25, bf16[4,576,128]{2,1,0:T(8,128)(2,1)} %bitcast.27, bf16[16,288,128]{2,1,0:T(8,128)(2,1)S(1)} %get-tuple-element.28.head_ref), custom_call_target="tpu_custom_call" | custom-call | flops 4000000000 | bytes 16000000 | tf_op jit(solution)/shard_map/pallas_call | solution.py:482
  9.4 0.0 collective-permute-done.refs_10_
  9.4 0.0 collective-permute-done.1.refs_11_
  9.4 0.0 collective-permute-done.2.refs_12_
  9.4 0.0 copy-done
  9.4 0.0 copy-done.1
  9.4 0.0 copy-done.2
  9.4 9.3 %shard_map.93 = (bf16[2,64,24,128]{3,2,1,0:T(8,128)(2,1)S(1)}, bf16[8,24,128]{2,1,0:T(8,128)(2,1)S(1)}, bf16[8,24,128]{2,1,0:T(8,128)(2,1)S(1)}, bf16[8,24,128]{...) custom-call(s32[4,64]{1,0:T(4,128)S(1)} %bitcast.19, ...), custom_call_target="tpu_custom_call", output_to_operand_aliasing={{0}: (9, {})} | custom-call | flops 10000000000 | bytes 16000000 | tf_op jit(solution)/shard_map/pallas_call | solution.py:506
  18.8 2.4 %collective-permute-start.3 = (bf16[8,24,128]{2,1,0:T(8,128)(2,1)S(1)}, bf16[8,24,128]{2,1,0:T(8,128)(2,1)S(1)}, u32[]{:S(2)}, u32[]{:S(2)}) collective-permute-start(bf16[8,24,128]{2,1,0:T(8,128)(2,1)S(1)} %get-tuple-element.39), channel_id=1, source_target_pairs={{0,3},{1,2},{2,1},{3,0},{4,7},{5,6},{6,5},{7,4},{8,11},{9,10},{10,... | collective-permute-start | bytes 147464 | tf_op jit(solution)/shard_map/ppermute | solution.py:503
  21.1 0.2 collective-permute-start.4
  21.3 0.2 collective-permute-start.5
  21.5 2.0 %collective-permute-start.6 = (bf16[8,24,128]{2,1,0:T(8,128)(2,1)S(1)}, bf16[8,24,128]{2,1,0:T(8,128)(2,1)S(1)}, u32[]{:S(2)}, u32[]{:S(2)}) collective-permute-start(bf16[8,24,128]{2,1,0:T(8,128)(2,1)S(1)} %get-tuple-element.43), channel_id=1, source_target_pairs={{0,4},{4,0},{8,12},{12,8},{16,20},{20,16},{24,28},{28,24},{1,5},{5... | collective-permute-start | bytes 147464 | tf_op jit(solution)/shard_map/ppermute | solution.py:430
  23.5 3.4 %collective-permute-start.7 = (bf16[8,24,128]{2,1,0:T(8,128)(2,1)S(1)}, bf16[8,24,128]{2,1,0:T(8,128)(2,1)S(1)}, u32[]{:S(2)}, u32[]{:S(2)}) collective-permute-start(bf16[8,24,128]{2,1,0:T(8,128)(2,1)S(1)} %get-tuple-element.45), channel_id=1, source_target_pairs={{4,8},{8,4},{12,16},{16,12},{20,24},{24,20},{5,9},{9,5},{13,17},{1... | collective-permute-start | bytes 147464 | tf_op jit(solution)/shard_map/ppermute | solution.py:430
  26.9 0.0 collective-permute-done.3.refs_7_
  27.0 0.0 collective-permute-done.4.refs_8_
  27.0 0.0 collective-permute-done.5.refs_9_
  27.0 0.0 collective-permute-done.6.refs_11_
  27.0 2.0 %shard_map.94 = (f32[48,24,128]{2,1,0:T(8,128)S(1)}, bf16[2,64,24,128]{3,2,1,0:T(8,128)(2,1)S(1)}, f32[2,6,24,128]{3,2,1,0:T(8,128)S(1)}) custom-call(s32[4,64]{1,0:T(4,128)S(1)} %bitcast.20, s32[4,8]{1,0:T(4,128)S(1)} %bitcast.18, f32[48,8,128]{2,1,0:T(8,128)S(1)} %get-tuple-element.27.refs_5_.refs_2_.refs_1_, ...), custom_call_target="tpu_custom_call" | custom-call | flops 1000000000 | bytes 8000000 | tf_op jit(solution)/shard_map/pallas_call | solution.py:524
  28.9 0.0 collective-permute-done.7.refs_4_
  29.0 8.3 %shard_map.95 = (f32[24,6144]{1,0:T(8,128)}, f32[48,24,128]{2,1,0:T(8,128)S(1)}, bf16[2,64,24,128]{3,2,1,0:T(8,128)(2,1)S(1)}) custom-call(s32[4,64]{1,0:T(4,128)S(1)} %bitcast.21, f32[48,8,128]{2,1,0:T(8,128)S(1)} %get-tuple-element.27.refs_5_.refs_2_.refs_1_, ...), custom_call_target="tpu_custom_call", output_to_operand_aliasing={{1}: (5, {}), {2}: (6, {})} | custom-call | flops 10000000000 | bytes 16000000 | tf_op jit(solution)/shard_map/pallas_call | solution.py:537
  (5 shorter events, 0.0 us)
Async XLA Ops:
  1.4 7.9 %collective-permute-start = (bf16[8,24,128]{2,1,0:T(8,128)(2,1)S(1)}, bf16[8,24,128]{2,1,0:T(8,128)(2,1)S(1)}, u32[]{:S(2)}, u32[]{:S(2)}) collective-permute-start(bf16[8,24,128]{2,1,0:T(8,128)(2,1)S(1)} %get-tuple-element.34), channel_id=1, source_target_pairs={{0,3},{1,2},{2,1},{3,0},{4,7},{5,6},{6,5},{7,4},{8,11},{9,10},{10,... | collective-permute-start | bytes 147464 | tf_op jit(solution)/shard_map/ppermute | solution.py:503
  4.5 4.9 %collective-permute-start.1 = (bf16[8,24,128]{2,1,0:T(8,128)(2,1)S(1)}, bf16[8,24,128]{2,1,0:T(8,128)(2,1)S(1)}, u32[]{:S(2)}, u32[]{:S(2)}) collective-permute-start(bf16[8,24,128]{2,1,0:T(8,128)(2,1)S(1)} %get-tuple-element.35), channel_id=1, source_target_pairs={{0,1},{1,0},{2,3},{3,2},{4,5},{5,4},{6,7},{7,6},{8,9},{9,8},{10,11... | collective-permute-start | bytes 147464 | tf_op jit(solution)/shard_map/ppermute | solution.py:503
  4.8 4.6 %collective-permute-start.2 = (bf16[8,24,128]{2,1,0:T(8,128)(2,1)S(1)}, bf16[8,24,128]{2,1,0:T(8,128)(2,1)S(1)}, u32[]{:S(2)}, u32[]{:S(2)}) collective-permute-start(bf16[8,24,128]{2,1,0:T(8,128)(2,1)S(1)} %get-tuple-element.36), channel_id=1, source_target_pairs={{0,2},{1,3},{2,0},{3,1},{4,6},{5,7},{6,4},{7,5},{8,10},{9,11},{10,... | collective-permute-start | bytes 147464 | tf_op jit(solution)/shard_map/ppermute | solution.py:503
  4.9 4.5 %copy-start = (s32[1,1,4,8]{3,2,1,0:T(4,128)S(1)}, s32[1,1,4,8]{3,2,1,0:T(4,128)}, u32[]{:S(2)}) copy-start(s32[1,1,4,8]{3,2,1,0:T(4,128)} %param.14) | copy-start | bytes 388
  4.9 4.5 %copy-start.1 = (s32[1,1,4,8]{3,2,1,0:T(4,128)S(1)}, s32[1,1,4,8]{3,2,1,0:T(4,128)}, u32[]{:S(2)}) copy-start(s32[1,1,4,8]{3,2,1,0:T(4,128)} %param.16) | copy-start | bytes 388
  4.9 4.5 %copy-start.2 = (s32[64,4]{0,1:T(4,128)S(1)}, s32[64,4]{0,1:T(4,128)}, u32[]{:S(2)}) copy-start(s32[64,4]{0,1:T(4,128)} %param.11) | copy-start | bytes 3076
  4.9 4.5 %copy-start.3 = (s32[1,1,4]{2,1,0:T(1,128)S(1)}, s32[1,1,4]{2,1,0:T(1,128)}, u32[]{:S(2)}) copy-start(s32[1,1,4]{2,1,0:T(1,128)} %param.15) | copy-start | bytes 52
  18.8 8.2 %collective-permute-start.3 = (bf16[8,24,128]{2,1,0:T(8,128)(2,1)S(1)}, bf16[8,24,128]{2,1,0:T(8,128)(2,1)S(1)}, u32[]{:S(2)}, u32[]{:S(2)}) collective-permute-start(bf16[8,24,128]{2,1,0:T(8,128)(2,1)S(1)} %get-tuple-element.39), channel_id=1, source_target_pairs={{0,3},{1,2},{2,1},{3,0},{4,7},{5,6},{6,5},{7,4},{8,11},{9,10},{10,... | collective-permute-start | bytes 147464 | tf_op jit(solution)/shard_map/ppermute | solution.py:503
  21.1 5.8 %collective-permute-start.4 = (bf16[8,24,128]{2,1,0:T(8,128)(2,1)S(1)}, bf16[8,24,128]{2,1,0:T(8,128)(2,1)S(1)}, u32[]{:S(2)}, u32[]{:S(2)}) collective-permute-start(bf16[8,24,128]{2,1,0:T(8,128)(2,1)S(1)} %get-tuple-element.40), channel_id=1, source_target_pairs={{0,1},{1,0},{2,3},{3,2},{4,5},{5,4},{6,7},{7,6},{8,9},{9,8},{10,11... | collective-permute-start | bytes 147464 | tf_op jit(solution)/shard_map/ppermute | solution.py:503
  21.3 5.6 %collective-permute-start.5 = (bf16[8,24,128]{2,1,0:T(8,128)(2,1)S(1)}, bf16[8,24,128]{2,1,0:T(8,128)(2,1)S(1)}, u32[]{:S(2)}, u32[]{:S(2)}) collective-permute-start(bf16[8,24,128]{2,1,0:T(8,128)(2,1)S(1)} %get-tuple-element.41), channel_id=1, source_target_pairs={{0,2},{1,3},{2,0},{3,1},{4,6},{5,7},{6,4},{7,5},{8,10},{9,11},{10,... | collective-permute-start | bytes 147464 | tf_op jit(solution)/shard_map/ppermute | solution.py:503
  21.5 5.5 %collective-permute-start.6 = (bf16[8,24,128]{2,1,0:T(8,128)(2,1)S(1)}, bf16[8,24,128]{2,1,0:T(8,128)(2,1)S(1)}, u32[]{:S(2)}, u32[]{:S(2)}) collective-permute-start(bf16[8,24,128]{2,1,0:T(8,128)(2,1)S(1)} %get-tuple-element.43), channel_id=1, source_target_pairs={{0,4},{4,0},{8,12},{12,8},{16,20},{20,16},{24,28},{28,24},{1,5},{5... | collective-permute-start | bytes 147464 | tf_op jit(solution)/shard_map/ppermute | solution.py:430
  23.5 5.4 %collective-permute-start.7 = (bf16[8,24,128]{2,1,0:T(8,128)(2,1)S(1)}, bf16[8,24,128]{2,1,0:T(8,128)(2,1)S(1)}, u32[]{:S(2)}, u32[]{:S(2)}) collective-permute-start(bf16[8,24,128]{2,1,0:T(8,128)(2,1)S(1)} %get-tuple-element.45), channel_id=1, source_target_pairs={{4,8},{8,4},{12,16},{16,12},{20,24},{24,20},{5,9},{9,5},{13,17},{1... | collective-permute-start | bytes 147464 | tf_op jit(solution)/shard_map/ppermute | solution.py:430

commit v10 on v9

--- a/solution.py
+++ b/solution.py
@@ -359,10 +359,16 @@
     write_sent(peers, send_ref, count_ref, sign_ref, state_ref, sent_refs)
 
 
+def first_image_kernel(cols_ref, matrix_ref, state_ref, image_ref):
+    for group in range(NB // (2 * QUAD)):
+        for i, part in enumerate(images_of(cols_ref, matrix_ref, state_ref, group)):
+            image_ref[group * 2 * TILES + i] = part
+
+
 def first_step_kernel(peers, *refs):
-    cols_ref, target_ref, scale_ref, matrix_ref, face_ref, source_ref, start_ref = refs[:7]
-    received_refs, swap_in_ref = refs[7 : 7 + peers], refs[7 + peers]
-    forcing_ref, state_ref, end_ref, extra_ref = refs[8 + peers :]
+    target_ref, scale_ref, face_ref, source_ref, image_ref = refs[:5]
+    received_refs, swap_in_ref = refs[5 : 5 + peers], refs[5 + peers]
+    forcing_ref, state_ref, end_ref, extra_ref = refs[6 + peers :]
     inner, _ = end_blocks()
     extra_ref[...] = jnp.zeros_like(extra_ref)
     extra_ref[0, pl.ds(inner, NI)] = swap_in_ref[...].astype(jnp.float32)
@@ -370,10 +376,10 @@
     set_forcing(source_ref, scale_ref, extra_ref, forcing_ref)
     groups = NB // (2 * QUAD)
     for group in range(groups):
-        parts = images_of(cols_ref, matrix_ref, start_ref, group)
+        first = group * 2 * TILES
         tiles = [
-            step_tile(forcing_ref, scale_ref, part, group * 2 * TILES + i)
-            for i, part in enumerate(parts)
+            step_tile(forcing_ref, scale_ref, image_ref[at], at)
+            for at in range(first, first + 2 * TILES)
         ]
         for side in range(2):
             store_quad(state_ref, group * 2 + side, tiles[side * TILES : (side + 1) * TILES])
@@ -521,6 +527,14 @@
     received = exchange(sent)
     swap_in = swapped(swap_in, "sec", 0)
     swap_out = swapped(swap_out, "sec", 1)
+    image = pl.pallas_call(
+        first_image_kernel,
+        out_shape=shape(tile_shape, f32),
+        in_specs=[SMEM] + [VMEM] * 2,
+        out_specs=VMEM,
+        compiler_params=params(),
+        cost_estimate=cost(10**9, 8 * 10**6),
+    )(cols, matrices, state)
     forcing, state, end = pl.pallas_call(
         functools.partial(first_step_kernel, peers),
         out_shape=(
@@ -528,12 +542,12 @@
             shape(state_shape, bf16),
             shape((2, 2 * TILES, COLS, LANES), f32),
         ),
-        in_specs=[SMEM] * 2 + [VMEM] * (6 + peers),
+        in_specs=[SMEM] + [VMEM] * (5 + peers),
         out_specs=[VMEM] * 3,
         scratch_shapes=[pltpu.VMEM((2,) + block_shape, f32)],
         compiler_params=params(),
         cost_estimate=cost(10**9, 8 * 10**6),
-    )(cols, targets, scale, matrices, faces, source, state, *received, swap_in)
+    )(targets, scale, faces, source, image, *received, swap_in)
     out, _, _ = pl.pallas_call(
         last_tick_kernel,
         out_shape=(shape((COLS, NB * BS), f32), shape(tile_shape, f32), shape(state_shape, bf16)),

time: 38 us -> 38.3 us (level); the launches traced: 37.2 us -> 38.1 us
  Pallas kernels: 25.5 us -> 26.4 us
    pallas_call x0 -> x1, Pallas kernels: none -> 1.44 us  [shards(): pl.pallas_call(first_image_kernel, out_shape=shape(tile_shape, f32), in_s...]
    pallas_call x1, Pallas kernels: 1.96 us -> 1.42 us  [shards(): pl.pallas_call(functools.partial(first_step_kernel, peers), out_shape=(sh...]
  transfers between devices with their start and end apart: 8 -> 8, of which waited for: 0 -> 0; matrix products, arithmetic and copies ran while one was open for 0% -> 0% of each run, Pallas kernels for 17% -> 19%
where the time goes in v10:
time: 38.3 us; the launch traced here: 38.1 us
  Pallas kernels  26.4 us (69%)
  starting transfers between devices  11.6 us (30%)
    pallas_call x1, Pallas kernels, shards(): pl.pallas_call(functools.partial(first_tick_kernel, peers), out_shape=(sh...  9.27 us
    pallas_call x1, Pallas kernels, shards(): pl.pallas_call(last_tick_kernel, out_shape=(shape((COLS, NB * BS), f32),...  8.34 us
    ppermute x6, starting transfers between devices, exchange(): lax.ppermute(sent[i], 'patch', pairs[i])  6.15 us
    ppermute x2, starting transfers between devices, swapped(): return lax.ppermute(x, axis, pairs)  5.46 us
    pallas_call x1, Pallas kernels, shards(): pl.pallas_call(functools.partial(spread_kernel, peers), out_shape=(shape(...  4.46 us
    pallas_call x1, Pallas kernels, shards(): pl.pallas_call(first_image_kernel, out_shape=shape(tile_shape, f32), in_s...  1.44 us
    pallas_call x1, Pallas kernels, shards(): pl.pallas_call(functools.partial(prep_kernel, peers), out_shape=(shape(st...  1.44 us
    pallas_call x1, Pallas kernels, shards(): pl.pallas_call(functools.partial(first_step_kernel, peers), out_shape=(sh...  1.42 us
  transfers between devices with their start and end apart: 8, of which 0 were waited for; matrix products, arithmetic and copies ran while one was open for 0% of the time, Pallas kernels for 19%

profile of v10, /device:TPU:1, one launch (start us, length us, event | category | flops | bytes accessed | tf_op | source)
XLA Modules:
  0.0 38.1 jit_solution(2375523207532898821)
XLA Ops:
  0.0 1.4 %shard_map.91 = (bf16[2,64,24,128]{3,2,1,0:T(8,128)(2,1)S(1)}, f32[4,16,128]{2,1,0:T(8,128)S(1)}, bf16[48,24,128]{2,1,0:T(8,128)(2,1)S(1)}, f32[48,8,128]{2,1,0:...) custom-call(s32[4,8]{1,0:T(4,128)} %bitcast.15, ...), custom_call_target="tpu_custom_call" | custom-call | flops 1000000 | bytes 1000000 | tf_op jit(solution)/shard_map/pallas_call | solution.py:464
  1.4 3.1 %collective-permute-start = (bf16[8,24,128]{2,1,0:T(8,128)(2,1)S(1)}, bf16[8,24,128]{2,1,0:T(8,128)(2,1)S(1)}, u32[]{:S(2)}, u32[]{:S(2)}) collective-permute-start(bf16[8,24,128]{2,1,0:T(8,128)(2,1)S(1)} %get-tuple-element.34), channel_id=1, source_target_pairs={{0,3},{1,2},{2,1},{3,0},{4,7},{5,6},{6,5},{7,4},{8,11},{9,10},{10,... | collective-permute-start | bytes 147464 | tf_op jit(solution)/shard_map/ppermute | solution.py:509
  4.5 0.3 collective-permute-start.1
  4.8 0.1 collective-permute-start.2
  4.9 4.5 %shard_map.92 = (bf16[8,2,192,768]{3,2,1,0:T(8,128)(2,1)S(1)}, bf16[4,4,96,256]{3,2,1,0:T(8,128)(2,1)S(1)}) custom-call(bf16[64,288,128]{2,1,0:T(8,128)(2,1)} %bitcast.25, bf16[4,576,128]{2,1,0:T(8,128)(2,1)} %bitcast.27, bf16[16,288,128]{2,1,0:T(8,128)(2,1)S(1)} %get-tuple-element.28.head_ref), custom_call_target="tpu_custom_call" | custom-call | flops 4000000000 | bytes 16000000 | tf_op jit(solution)/shard_map/pallas_call | solution.py:488
  9.4 0.0 collective-permute-done.refs_10_
  9.4 0.0 collective-permute-done.1.refs_11_
  9.4 0.0 collective-permute-done.2.refs_12_
  9.4 0.0 copy-done
  9.4 0.0 copy-done.1
  9.4 9.3 %shard_map.93 = (bf16[2,64,24,128]{3,2,1,0:T(8,128)(2,1)S(1)}, bf16[8,24,128]{2,1,0:T(8,128)(2,1)S(1)}, bf16[8,24,128]{2,1,0:T(8,128)(2,1)S(1)}, bf16[8,24,128]{...) custom-call(s32[4,64]{1,0:T(4,128)S(1)} %bitcast.17, ...), custom_call_target="tpu_custom_call", output_to_operand_aliasing={{0}: (9, {})} | custom-call | flops 10000000000 | bytes 16000000 | tf_op jit(solution)/shard_map/pallas_call | solution.py:512
  18.7 2.4 %collective-permute-start.3 = (bf16[8,24,128]{2,1,0:T(8,128)(2,1)S(1)}, bf16[8,24,128]{2,1,0:T(8,128)(2,1)S(1)}, u32[]{:S(2)}, u32[]{:S(2)}) collective-permute-start(bf16[8,24,128]{2,1,0:T(8,128)(2,1)S(1)} %get-tuple-element.39), channel_id=1, source_target_pairs={{0,3},{1,2},{2,1},{3,0},{4,7},{5,6},{6,5},{7,4},{8,11},{9,10},{10,... | collective-permute-start | bytes 147464 | tf_op jit(solution)/shard_map/ppermute | solution.py:509
  21.1 0.2 collective-permute-start.4
  21.3 0.2 collective-permute-start.5
  21.4 2.0 %collective-permute-start.6 = (bf16[8,24,128]{2,1,0:T(8,128)(2,1)S(1)}, bf16[8,24,128]{2,1,0:T(8,128)(2,1)S(1)}, u32[]{:S(2)}, u32[]{:S(2)}) collective-permute-start(bf16[8,24,128]{2,1,0:T(8,128)(2,1)S(1)} %get-tuple-element.43), channel_id=1, source_target_pairs={{0,4},{4,0},{8,12},{12,8},{16,20},{20,16},{24,28},{28,24},{1,5},{5... | collective-permute-start | bytes 147464 | tf_op jit(solution)/shard_map/ppermute | solution.py:436
  23.4 3.4 %collective-permute-start.7 = (bf16[8,24,128]{2,1,0:T(8,128)(2,1)S(1)}, bf16[8,24,128]{2,1,0:T(8,128)(2,1)S(1)}, u32[]{:S(2)}, u32[]{:S(2)}) collective-permute-start(bf16[8,24,128]{2,1,0:T(8,128)(2,1)S(1)} %get-tuple-element.45), channel_id=1, source_target_pairs={{4,8},{8,4},{12,16},{16,12},{20,24},{24,20},{5,9},{9,5},{13,17},{1... | collective-permute-start | bytes 147464 | tf_op jit(solution)/shard_map/ppermute | solution.py:436
  26.9 1.4 %shard_map.94.refs_4_ = f32[48,24,128]{2,1,0:T(8,128)S(1)} custom-call(s32[4,64]{1,0:T(4,128)S(1)} %bitcast.18, bf16[8,2,192,768]{3,2,1,0:T(8,128)(2,1)S(1)} %get-tuple-element.29.refs_6_.matrix_ref.refs_2_, bf16[2,64,24,128]{3,2,1,0:T(8,128)(2,1)S(1)} %get-tuple-element.38.state_ref), custom_call_target="tpu_custom_call" | custom-call | flops 1000000000 | bytes 8000000 | tf_op jit(solution)/shard_map/pallas_call | solution.py:530
  28.3 0.0 collective-permute-done.3.refs_5_
  28.3 0.0 collective-permute-done.4.refs_6_
  28.4 0.0 collective-permute-done.5.refs_7_
  28.4 0.0 collective-permute-done.6.refs_9_
  28.4 1.4 %shard_map.95 = (f32[48,24,128]{2,1,0:T(8,128)S(1)}, bf16[2,64,24,128]{3,2,1,0:T(8,128)(2,1)S(1)}, f32[2,6,24,128]{3,2,1,0:T(8,128)S(1)}) custom-call(s32[4,8]{1,0:T(4,128)S(1)} %bitcast.23, f32[48,8,128]{2,1,0:T(8,128)S(1)} %get-tuple-element.27.refs_5_.refs_1_, bf16[4,4,96,256]{3,2,1,0:T(8,128)(2,1)S(1)} %get-tuple-element.30.refs_7_.refs_2_, ...), custom_call_target="tpu_custom_call" | custom-call | flops 1000000000 | bytes 8000000 | tf_op jit(solution)/shard_map/pallas_call | solution.py:538
  29.8 0.0 collective-permute-done.7.refs_4_
  29.8 8.3 %shard_map.96 = (f32[24,6144]{1,0:T(8,128)}, f32[48,24,128]{2,1,0:T(8,128)S(1)}, bf16[2,64,24,128]{3,2,1,0:T(8,128)(2,1)S(1)}) custom-call(s32[4,64]{1,0:T(4,128)S(1)} %bitcast.19, f32[48,8,128]{2,1,0:T(8,128)S(1)} %get-tuple-element.27.refs_5_.refs_1_, ...), custom_call_target="tpu_custom_call", output_to_operand_aliasing={{1}: (5, {}), {2}: (6, {})} | custom-call | flops 10000000000 | bytes 16000000 | tf_op jit(solution)/shard_map/pallas_call | solution.py:551
  (6 shorter events, 0.0 us)
Async XLA Ops:
  1.4 7.9 %collective-permute-start = (bf16[8,24,128]{2,1,0:T(8,128)(2,1)S(1)}, bf16[8,24,128]{2,1,0:T(8,128)(2,1)S(1)}, u32[]{:S(2)}, u32[]{:S(2)}) collective-permute-start(bf16[8,24,128]{2,1,0:T(8,128)(2,1)S(1)} %get-tuple-element.34), channel_id=1, source_target_pairs={{0,3},{1,2},{2,1},{3,0},{4,7},{5,6},{6,5},{7,4},{8,11},{9,10},{10,... | collective-permute-start | bytes 147464 | tf_op jit(solution)/shard_map/ppermute | solution.py:509
  4.5 4.9 %collective-permute-start.1 = (bf16[8,24,128]{2,1,0:T(8,128)(2,1)S(1)}, bf16[8,24,128]{2,1,0:T(8,128)(2,1)S(1)}, u32[]{:S(2)}, u32[]{:S(2)}) collective-permute-start(bf16[8,24,128]{2,1,0:T(8,128)(2,1)S(1)} %get-tuple-element.35), channel_id=1, source_target_pairs={{0,1},{1,0},{2,3},{3,2},{4,5},{5,4},{6,7},{7,6},{8,9},{9,8},{10,11... | collective-permute-start | bytes 147464 | tf_op jit(solution)/shard_map/ppermute | solution.py:509
  4.8 4.6 %collective-permute-start.2 = (bf16[8,24,128]{2,1,0:T(8,128)(2,1)S(1)}, bf16[8,24,128]{2,1,0:T(8,128)(2,1)S(1)}, u32[]{:S(2)}, u32[]{:S(2)}) collective-permute-start(bf16[8,24,128]{2,1,0:T(8,128)(2,1)S(1)} %get-tuple-element.36), channel_id=1, source_target_pairs={{0,2},{1,3},{2,0},{3,1},{4,6},{5,7},{6,4},{7,5},{8,10},{9,11},{10,... | collective-permute-start | bytes 147464 | tf_op jit(solution)/shard_map/ppermute | solution.py:509
  4.9 4.5 %copy-start = (s32[1,1,4,8]{3,2,1,0:T(4,128)S(1)}, s32[1,1,4,8]{3,2,1,0:T(4,128)}, u32[]{:S(2)}) copy-start(s32[1,1,4,8]{3,2,1,0:T(4,128)} %param.14) | copy-start | bytes 388
  4.9 4.5 %copy-start.1 = (s32[64,4]{0,1:T(4,128)S(1)}, s32[64,4]{0,1:T(4,128)}, u32[]{:S(2)}) copy-start(s32[64,4]{0,1:T(4,128)} %param.11) | copy-start | bytes 3076
  4.9 4.5 %copy-start.2 = (s32[1,1,4]{2,1,0:T(1,128)S(1)}, s32[1,1,4]{2,1,0:T(1,128)}, u32[]{:S(2)}) copy-start(s32[1,1,4]{2,1,0:T(1,128)} %param.15) | copy-start | bytes 52
  4.9 4.5 %copy-start.3 = (s32[1,1,4,8]{3,2,1,0:T(4,128)S(1)}, s32[1,1,4,8]{3,2,1,0:T(4,128)}, u32[]{:S(2)}) copy-start(s32[1,1,4,8]{3,2,1,0:T(4,128)} %param.16) | copy-start | bytes 388
  18.7 9.6 %collective-permute-start.3 = (bf16[8,24,128]{2,1,0:T(8,128)(2,1)S(1)}, bf16[8,24,128]{2,1,0:T(8,128)(2,1)S(1)}, u32[]{:S(2)}, u32[]{:S(2)}) collective-permute-start(bf16[8,24,128]{2,1,0:T(8,128)(2,1)S(1)} %get-tuple-element.39), channel_id=1, source_target_pairs={{0,3},{1,2},{2,1},{3,0},{4,7},{5,6},{6,5},{7,4},{8,11},{9,10},{10,... | collective-permute-start | bytes 147464 | tf_op jit(solution)/shard_map/ppermute | solution.py:509
  21.1 7.3 %collective-permute-start.4 = (bf16[8,24,128]{2,1,0:T(8,128)(2,1)S(1)}, bf16[8,24,128]{2,1,0:T(8,128)(2,1)S(1)}, u32[]{:S(2)}, u32[]{:S(2)}) collective-permute-start(bf16[8,24,128]{2,1,0:T(8,128)(2,1)S(1)} %get-tuple-element.40), channel_id=1, source_target_pairs={{0,1},{1,0},{2,3},{3,2},{4,5},{5,4},{6,7},{7,6},{8,9},{9,8},{10,11... | collective-permute-start | bytes 147464 | tf_op jit(solution)/shard_map/ppermute | solution.py:509
  21.3 7.1 %collective-permute-start.5 = (bf16[8,24,128]{2,1,0:T(8,128)(2,1)S(1)}, bf16[8,24,128]{2,1,0:T(8,128)(2,1)S(1)}, u32[]{:S(2)}, u32[]{:S(2)}) collective-permute-start(bf16[8,24,128]{2,1,0:T(8,128)(2,1)S(1)} %get-tuple-element.41), channel_id=1, source_target_pairs={{0,2},{1,3},{2,0},{3,1},{4,6},{5,7},{6,4},{7,5},{8,10},{9,11},{10,... | collective-permute-start | bytes 147464 | tf_op jit(solution)/shard_map/ppermute | solution.py:509
  21.4 6.9 %collective-permute-start.6 = (bf16[8,24,128]{2,1,0:T(8,128)(2,1)S(1)}, bf16[8,24,128]{2,1,0:T(8,128)(2,1)S(1)}, u32[]{:S(2)}, u32[]{:S(2)}) collective-permute-start(bf16[8,24,128]{2,1,0:T(8,128)(2,1)S(1)} %get-tuple-element.43), channel_id=1, source_target_pairs={{0,4},{4,0},{8,12},{12,8},{16,20},{20,16},{24,28},{28,24},{1,5},{5... | collective-permute-start | bytes 147464 | tf_op jit(solution)/shard_map/ppermute | solution.py:436
  23.4 6.4 %collective-permute-start.7 = (bf16[8,24,128]{2,1,0:T(8,128)(2,1)S(1)}, bf16[8,24,128]{2,1,0:T(8,128)(2,1)S(1)}, u32[]{:S(2)}, u32[]{:S(2)}) collective-permute-start(bf16[8,24,128]{2,1,0:T(8,128)(2,1)S(1)} %get-tuple-element.45), channel_id=1, source_target_pairs={{4,8},{8,4},{12,16},{16,12},{20,24},{24,20},{5,9},{9,5},{13,17},{1... | collective-permute-start | bytes 147464 | tf_op jit(solution)/shard_map/ppermute | solution.py:436
